TPU v7x, 512 devices: a whole 4x8x8 slice. The times are simulated.
512 devices in a mesh: row: 16 (over x, z_lo, core), col: 32 (over z_hi, y).
Axes of the slice: x: 4, y: 8, z: 8 (z_hi: 4, z_lo: 2; z = z_hi * 2 + z_lo), core: 2. Of those that a mesh axis runs over, the one named last changes fastest.
Arguments:
- vectors: float32 [28672, 128], P('row'), may hold values from -6 to 6
- tiles: float32 [16, 32, 10, 56, 56], P('row', 'col'), may hold values from -0.1875 to 0.1875
- tile_pos: int32 [16, 32, 2, 10], P('row', 'col'), may hold values from 0 to 31
- diag_blocks: float32 [512, 56, 56], P(('row', 'col')), as said below
Outputs:
- filtered: float32 [28672, 128], P('row')
Inputs may be any that keep to these rules, and one draw needn't show every extreme that they name: Where 10 + 1 <= 32, the stored blocks of the device at (r, c) lie in 10 different local block rows, none of them among c * 1 to c + 1 - 1. `diag_blocks`: every diagonal block is symmetric.
All inputs are finite; a program needn't handle non-finite values.
Results may differ from a plain program's by a relative error of at most 0.00011.
Values sent between devices are 32-bit elements; how exact they have to be, the bound alone decides.
No kernel may reach another device: no remote copies, remote signals or barrier semaphores. Data moves between devices by JAX's collectives and lax.ppermute only.
A program may use at most 64 MiB of HBM per device.

v0:
```python
import jax
import jax.numpy as jnp
from jax import lax
from jax.sharding import PartitionSpec as P

ORB = 56
DEGREE = 3


filter_low = 0.0
filter_high = 8.0


def body(vectors, tiles, tile_pos, diag_blocks):
    tile_data = tiles[0, 0]
    block_rows = tile_pos[0, 0, 0]
    block_cols = tile_pos[0, 0, 1]
    total_rows, width = vectors.shape
    group_blocks = total_rows // ORB
    slice_blocks = diag_blocks.shape[0]
    slice_rows = slice_blocks * ORB
    column_blocks_n = slice_blocks * lax.axis_size("row")
    start_row = lax.axis_index("col") * slice_rows

    def apply_operator(field):
        own_rows = lax.dynamic_slice_in_dim(field, start_row, slice_rows, 0)
        column_field = lax.all_gather(own_rows, "row", axis=0, tiled=True)
        field_blocks = field.reshape(group_blocks, ORB, width)
        column_blocks = column_field.reshape(column_blocks_n, ORB, width)
        direct = jnp.einsum(
            "tab,tbk->tak", tile_data, column_blocks[block_cols], precision=lax.Precision.HIGHEST
        )
        mirror = jnp.einsum(
            "tba,tbk->tak", tile_data, field_blocks[block_rows], precision=lax.Precision.HIGHEST
        )
        mirror_sum = jax.ops.segment_sum(mirror, block_cols, num_segments=column_blocks_n).reshape(
            column_blocks_n * ORB, width
        )
        own_diag = jnp.einsum(
            "sab,sbk->sak",
            diag_blocks,
            own_rows.reshape(-1, ORB, width),
            precision=lax.Precision.HIGHEST,
        ).reshape(slice_rows, width)
        mirror_own = lax.psum_scatter(mirror_sum, "row", scatter_dimension=0, tiled=True)
        direct_sum = jax.ops.segment_sum(direct, block_rows, num_segments=group_blocks).reshape(
            total_rows, width
        )
        present = lax.dynamic_slice_in_dim(direct_sum, start_row, slice_rows, 0)
        partial_sum = lax.dynamic_update_slice_in_dim(direct_sum, present + own_diag, start_row, 0)
        summed = lax.psum(partial_sum, "col")
        return summed + lax.all_gather(mirror_own, "col", axis=0, tiled=True)

    centre = 0.5 * (filter_high + filter_low)
    half_width = 0.5 * (filter_high - filter_low)
    previous = vectors
    current = (apply_operator(vectors) - centre * vectors) / half_width
    for step in range(DEGREE - 1):
        image = apply_operator(current)
        following = 2.0 * (image - centre * current) / half_width - previous
        previous, current = (current, following)
    return current


def solution(mesh):
    return jax.shard_map(
        body,
        mesh=mesh,
        in_specs=(
            P("row", None),
            P("row", "col", None, None, None),
            P("row", "col", None, None),
            P(("row", "col"), None, None),
        ),
        out_specs=P("row", None),
        check_vma=False,
    )
```

profile of v0, /device:TPU:2, one launch (start us, length us, event | category | flops | bytes accessed | tf_op | source)
XLA Modules:
  0.0 1037.9 jit_solution(11324285643475083261)
XLA Ops:
  8.2 1.7 gather_fusion.1
  10.7 1.1 scatter_fusion.1
  12.7 21.4 %all_gather.18 = f32[896,128]{1,0:T(8,128)S(1)} all-gather(f32[56,128]{1,0:T(8,128)S(1)} %constant_dynamic-slice_fusion.2), channel_id=1, replica_groups=mesh['row'=16,'col'=32] {'row'}, dimensions={0}, use_global_device_ids=true | all-gather | bytes 487424 | tf_op jit(solution)/shard_map/all_gather | solution.py:27
  35.3 1.1 scatter_fusion
  37.6 39.4 %reduce-scatter.13.cloned.1.call-done = f32[56,128]{1,0:T(8,128)} async-done(((f32[896,128]{1,0:T(8,128)}), f32[56,128]{1,0:T(8,128)}) %reduce-scatter.13.cloned.1.call-update) | async-done | bytes 28688
  77.0 89.2 %all_gather.19 = f32[1792,128]{1,0:T(8,128)S(1)} all-gather(f32[56,128]{1,0:T(8,128)} %reduce-scatter.13.cloned.1.call-done), channel_id=1, replica_groups=mesh['row'=16,'col'=32] {'col'}, dimensions={0}, use_global_device_ids=true | all-gather | bytes 946176 | tf_op jit(solution)/shard_map/all_gather | solution.py:52
  166.3 188.1 %all-reduce.7.cloned.1.call-done = f32[1792,128]{1,0:T(8,128)} async-done(((f32[1792,128]{1,0:T(8,128)}), f32[1792,128]{1,0:T(8,128)}) %all-reduce.7.cloned.1.call-update) | async-done | bytes 917520 | tf_op jit(solution)/shard_map/psum | solution.py:51
  354.4 1.4 broadcast_multiply_fusion
  356.4 1.4 convolution_bitcast_fusion.2
  357.8 1.9 scatter_fusion.3
  360.6 18.1 %all_gather.20 = f32[896,128]{1,0:T(8,128)S(1)} all-gather(f32[56,128]{1,0:T(8,128)S(1)} %constant_dynamic-slice_fusion), channel_id=1, replica_groups=mesh['row'=16,'col'=32] {'row'}, dimensions={0}, use_global_device_ids=true | all-gather | bytes 487424 | tf_op jit(solution)/shard_map/all_gather | solution.py:27
  380.0 1.1 scatter_fusion.2
  383.1 31.7 %reduce-scatter.15.cloned.1.call-done = f32[56,128]{1,0:T(8,128)} async-done(((f32[896,128]{1,0:T(8,128)}), f32[56,128]{1,0:T(8,128)}) %reduce-scatter.15.cloned.1.call-update) | async-done | bytes 28688
  414.7 94.9 %all_gather.21 = f32[1792,128]{1,0:T(8,128)} all-gather(f32[56,128]{1,0:T(8,128)} %reduce-scatter.15.cloned.1.call-done), channel_id=1, replica_groups=mesh['row'=16,'col'=32] {'col'}, dimensions={0}, use_global_device_ids=true | all-gather | bytes 946176 | tf_op jit(solution)/shard_map/all_gather | solution.py:52
  509.6 182.4 %all-reduce.9.cloned.1.call-done = f32[1792,128]{1,0:T(8,128)} async-done(((f32[1792,128]{1,0:T(8,128)}), f32[1792,128]{1,0:T(8,128)}) %all-reduce.9.cloned.1.call-update) | async-done | bytes 917520 | tf_op jit(solution)/shard_map/psum | solution.py:51
  692.0 2.1 multiply_subtract_fusion.1
  695.4 1.1 scatter_fusion.5
  697.4 18.2 %all_gather.22 = f32[896,128]{1,0:T(8,128)S(1)} all-gather(f32[56,128]{1,0:T(8,128)S(1)} %constant_dynamic-slice_fusion.1), channel_id=1, replica_groups=mesh['row'=16,'col'=32] {'row'}, dimensions={0}, use_global_device_ids=true | all-gather | bytes 487424 | tf_op jit(solution)/shard_map/all_gather | solution.py:27
  716.8 1.1 scatter_fusion.4
  718.1 1.0 copy-done.1
  719.1 32.3 %reduce-scatter.17.cloned.1.call-done = f32[56,128]{1,0:T(8,128)} async-done(((f32[896,128]{1,0:T(8,128)}), f32[56,128]{1,0:T(8,128)}) %reduce-scatter.17.cloned.1.call-update) | async-done | bytes 28688
  751.4 89.6 %all_gather.23 = f32[1792,128]{1,0:T(8,128)S(1)} all-gather(f32[56,128]{1,0:T(8,128)} %reduce-scatter.17.cloned.1.call-done), channel_id=1, replica_groups=mesh['row'=16,'col'=32] {'col'}, dimensions={0}, use_global_device_ids=true | all-gather | bytes 946176 | tf_op jit(solution)/shard_map/all_gather | solution.py:52
  841.0 187.2 %all-reduce.11.cloned.1.call-done = f32[1792,128]{1,0:T(8,128)} async-done(((f32[1792,128]{1,0:T(8,128)}), f32[1792,128]{1,0:T(8,128)}) %all-reduce.11.cloned.1.call-update) | async-done | bytes 917520 | tf_op jit(solution)/shard_map/psum | solution.py:51
  1028.2 2.3 multiply_subtract_fusion
  (61 shorter events, 12.9 us)
Async XLA Ops:
  7.4 2.6 copy-start
  7.4 0.8 copy-start.11
  7.4 69.7 %reduce-scatter.13.cloned.1.call-start = ((), (), s32[]{:S(2)}) async-start(), calls=%async_computation.6 | async-start | bytes 487424
  10.7 2.0 copy-start.7
  11.8 0.8 copy-start.5
  12.6 341.7 %all-reduce.7.cloned.1.call-start = ((), (), s32[]{:S(2)}) async-start(), calls=%async_computation.3 | async-start | bytes 1835008 | tf_op jit(solution)/shard_map/psum | solution.py:51
  35.3 1.1 copy-start.10
  36.6 0.9 copy-start.2
  37.6 377.1 %reduce-scatter.15.cloned.1.call-start = ((), (), s32[]{:S(2)}) async-start(), calls=%async_computation.7 | async-start | bytes 487424
  355.8 4.8 copy-start.8
  359.7 0.8 copy-start.6
  360.5 331.5 %all-reduce.9.cloned.1.call-start = ((), (), s32[]{:S(2)}) async-start(), calls=%async_computation.4 | async-start | bytes 1835008 | tf_op jit(solution)/shard_map/psum | solution.py:51
  382.1 0.9 copy-start.3
  383.0 368.4 %reduce-scatter.17.cloned.1.call-start = ((), (), s32[]{:S(2)}) async-start(), calls=%async_computation.8 | async-start | bytes 487424
  696.5 0.8 copy-start.4
  697.3 330.9 %all-reduce.11.cloned.1.call-start = ((), (), s32[]{:S(2)}) async-start(), calls=%async_computation.5 | async-start | bytes 1835008 | tf_op jit(solution)/shard_map/psum | solution.py:51
  718.1 1.0 copy-start.1
  718.1 310.1 %copy-start.9 = (f32[1792,128]{1,0:T(8,128)S(1)}, f32[1792,128]{1,0:T(8,128)}, u32[]{:S(2)}) copy-start(f32[1792,128]{1,0:T(8,128)} %copy-done.8) | copy-start | bytes 2752516
Sparse Core Ops, SparseCore 0:
  12.7 64.2 reduce-scatter.12
  360.6 54.0 reduce-scatter.14
  697.5 53.9 reduce-scatter.16
Sparse Core Ops, SparseCore 1:
  37.7 316.6 all-reduce.6
  383.1 308.9 all-reduce.8
  719.2 309.0 all-reduce.10
where the time goes:
time: 1040 us
  waiting for transfers between devices  661 us (64%)
  blocking collectives  331 us (32%)
  between operations  15.1 us (1%)
  other arithmetic  14.1 us (1%)
    psum x3, waiting for transfers between devices, apply_operator(): summed = lax.psum(partial_sum, 'col')  558 us
    all_gather x3, blocking collectives, apply_operator(): return summed + lax.all_gather(mirror_own, 'col', axis=0, tiled=True)  274 us
    unnamed x9, waiting for transfers between devices  103 us
    all_gather x3, blocking collectives, apply_operator(): column_field = lax.all_gather(own_rows, 'row', axis=0, tiled=True)  57.6 us
  transfers between devices with their start and end apart: 6, of which 6 were waited for; matrix products, arithmetic and copies ran while one was open for 1% of the time, Pallas kernels for 0%

commit v1 on v0

v1 whole, which is shorter than its diff:
```python
import functools

import jax
import jax.numpy as jnp
from jax import lax
from jax.experimental import pallas as pl
from jax.experimental.pallas import tpu as pltpu
from jax.sharding import Mesh, PartitionSpec as P

ORB = 56
DEGREE = 3
LANES = 128
N_X, N_ZL, N_CORE, N_ZH, N_Y = 4, 2, 2, 4, 8
N_R = N_X * N_ZL
TILES = 10
SLOTS = TILES + 1
SOURCES = N_CORE * N_ZH
WIDE = 640
VS = 16
ROW_AX = ("x", "zl")
GROUPS = 8

filter_low = 0.0
filter_high = 8.0

f32 = jnp.float32
bf16 = jnp.bfloat16


def params():
    return pltpu.CompilerParams(vmem_limit_bytes=40 * 1024 * 1024)


def vmem(n):
    return [pl.BlockSpec(memory_space=pltpu.VMEM)] * n


def lane_iota(rows=ORB):
    return lax.broadcasted_iota(jnp.int32, (rows, LANES), 1)


def roll_to(x, source, target):
    shift = (target - source) % LANES
    return x if shift == 0 else pltpu.roll(x, shift, 1)


def pack_kernel(tiles_ref, diag_ref, pos_ref, out_ref):
    lane = lane_iota()
    pieces = [tiles_ref[t] for t in range(TILES)] + [diag_ref[...]]
    wide = [
        jnp.concatenate([p, jnp.zeros((ORB, LANES - ORB), f32)], axis=1) for p in pieces
    ]
    places = jnp.broadcast_to(pos_ref[...], (ORB, LANES))
    for q in range(WIDE // LANES):
        total = jnp.zeros((ORB, LANES), f32)
        for t in range(SLOTS):
            start = t * ORB - q * LANES
            if start <= -ORB or start >= LANES:
                continue
            inside = (lane >= max(start, 0)) & (lane < min(start + ORB, LANES))
            total = jnp.where(inside, roll_to(wide[t], 0, start), total)
        if q == WIDE // LANES - 1:
            start = SLOTS * ORB - q * LANES
            total = jnp.where(lane >= start, roll_to(places, 0, start), total)
        out_ref[:, q * LANES : (q + 1) * LANES] = total


def pack(tile_data, diag, places):
    return pl.pallas_call(
        pack_kernel,
        out_shape=jax.ShapeDtypeStruct((ORB, WIDE), f32),
        in_specs=vmem(3),
        out_specs=vmem(1)[0],
        compiler_params=params(),
        name="pack",
    )(tile_data, diag, places)


def two_terms(x):
    high = x.astype(bf16).astype(f32)
    low = x - high
    return (high + pltpu.roll(low, 64, 1)).astype(bf16)


def unpack_kernel(in_ref, plain_ref, turned_ref):
    lane = lane_iota()

    def one_source(s, carry):
        for t in range(SLOTS):
            start = t * ORB
            q, off = start // LANES, start % LANES
            x = roll_to(in_ref[s, :, q * LANES : (q + 1) * LANES], off, 0)
            if off + ORB > LANES:
                y = roll_to(in_ref[s, :, (q + 1) * LANES : (q + 2) * LANES], off, 0)
                x = jnp.where(lane < LANES - off, x, y)
            x = jnp.where(lane < ORB, x, 0.0)
            plain_ref[s * SLOTS + t] = two_terms(x)
            square = jnp.concatenate([x, jnp.zeros((LANES - ORB, LANES), f32)], axis=0)
            turned_ref[s * SLOTS + t] = two_terms(square.T[:ORB])
        return carry

    lax.fori_loop(0, SOURCES, one_source, 0)


def unpack(packed):
    shape = jax.ShapeDtypeStruct((SOURCES * SLOTS, ORB, LANES), bf16)
    return pl.pallas_call(
        unpack_kernel,
        out_shape=(shape, shape),
        in_specs=vmem(1),
        out_specs=tuple(vmem(2)),
        compiler_params=params(),
        name="unpack",
    )(packed)


def slice_kernel(zh_ref, in_ref, out_ref):
    lane = lane_iota()
    start = zh_ref[0] * (2 * VS)
    for yp in range(N_Y // 2):
        for k in range(N_CORE):
            total = jnp.zeros((ORB, LANES), f32)
            for half in range(2):
                for z in range(N_ZH):
                    target = half * 64 + z * VS
                    x = in_ref[z * N_Y + 2 * yp + half]
                    shift = lax.rem(target - k * VS + LANES - start + LANES, LANES)
                    x = pltpu.roll(x, shift, 1)
                    inside = (lane >= target) & (lane < target + VS)
                    total = jnp.where(inside, x, total)
            out_ref[k, yp] = total


def slice_vectors(zh, blocks):
    return pl.pallas_call(
        slice_kernel,
        out_shape=jax.ShapeDtypeStruct((N_CORE, N_Y // 2, ORB, LANES), f32),
        in_specs=[pl.BlockSpec(memory_space=pltpu.SMEM)] + vmem(1),
        out_specs=vmem(1)[0],
        compiler_params=params(),
        name="slice_vectors",
    )(zh, blocks)


def join_kernel(in_ref, out_ref):
    lane = lane_iota()
    for yp in range(N_Y // 2):
        a, b = in_ref[0, yp], in_ref[1, yp]
        out_ref[2 * yp] = jnp.where(lane < 64, a, pltpu.roll(b, 64, 1))
        out_ref[2 * yp + 1] = jnp.where(lane < 64, pltpu.roll(a, 64, 1), b)


def join_cores(both):
    return pl.pallas_call(
        join_kernel,
        out_shape=jax.ShapeDtypeStruct((N_Y, ORB, LANES), f32),
        in_specs=vmem(1),
        out_specs=vmem(1)[0],
        compiler_params=params(),
        name="join_cores",
    )(both)


def product_kernel(
    pos_ref, me_ref, cols_ref, rows_ref, plain_ref, turned_ref,
    out_cols_ref, out_rows_ref, vc_ref, vr_ref, acc_c_ref, acc_r_ref,
):
    for src, dst in ((cols_ref, vc_ref), (rows_ref, vr_ref)):
        for chunk in range(GROUPS):
            x = src[chunk].T
            high = x.astype(bf16)
            low = (x - high.astype(f32)).astype(bf16)
            for o in range(GROUPS):
                dst[chunk * GROUPS + o, 0:VS] = high[o * VS : (o + 1) * VS]
                dst[chunk * GROUPS + o, VS : 2 * VS] = low[o * VS : (o + 1) * VS]
    acc_c_ref[...] = jnp.zeros_like(acc_c_ref)
    acc_r_ref[...] = jnp.zeros_like(acc_r_ref)
    my_r, my_y = me_ref[0], me_ref[1]

    def times(v, block):
        both = jnp.dot(v, block, preferred_element_type=f32)
        return both[:VS] + both[VS:]

    def one_source(s, carry):
        core_s, zh_s = s // N_ZH, s % N_ZH
        for t in range(SLOTS):
            n = s * SLOTS + t
            if t < TILES:
                i, g = pos_ref[s, t], pos_ref[s, TILES + t]
                row = (i % N_Y) * GROUPS + core_s * N_ZH + i // N_Y
                col = (g // N_CORE) * GROUPS + (g % N_CORE) * N_ZH + zh_s
                acc_r_ref[row] += times(vc_ref[col], turned_ref[n])
                acc_c_ref[col] += times(vr_ref[row], plain_ref[n])
            else:
                acc_r_ref[my_y * GROUPS + s] += times(vc_ref[my_r * GROUPS + s], turned_ref[n])
        return carry

    lax.fori_loop(0, SOURCES, one_source, 0)
    for acc, out in ((acc_c_ref, out_cols_ref), (acc_r_ref, out_rows_ref)):
        for chunk in range(GROUPS):
            x = acc[chunk * GROUPS : (chunk + 1) * GROUPS].reshape(LANES, LANES)
            x = x + pltpu.roll(x, 64, 1)
            out[chunk] = x.T[:ORB]


def product(places, me, cols, rows, plain, turned):
    shape = jax.ShapeDtypeStruct((GROUPS, ORB, LANES), f32)
    smem = pl.BlockSpec(memory_space=pltpu.SMEM)
    return pl.pallas_call(
        product_kernel,
        out_shape=(shape, shape),
        in_specs=[smem, smem] + vmem(4),
        out_specs=tuple(vmem(2)),
        scratch_shapes=[
            pltpu.VMEM((GROUPS * GROUPS, 2 * VS, ORB), bf16),
            pltpu.VMEM((GROUPS * GROUPS, 2 * VS, ORB), bf16),
            pltpu.VMEM((GROUPS * GROUPS, VS, LANES), f32),
            pltpu.VMEM((GROUPS * GROUPS, VS, LANES), f32),
        ],
        compiler_params=params(),
        name="product",
    )(places, me, cols, rows, plain, turned)


def spread_kernel(in_ref, out_ref):
    lane = lane_iota()
    for y in range(N_Y):
        for z in range(N_ZH):
            total = jnp.zeros((ORB, LANES), f32)
            for h in range(N_ZH):
                for k in range(N_CORE):
                    target = h * 2 * VS + k * VS
                    x = roll_to(in_ref[h, y], k * 64 + z * VS, target)
                    inside = (lane >= target) & (lane < target + VS)
                    total = jnp.where(inside, x, total)
            out_ref[z * N_Y + y] = total


def spread(gathered):
    return pl.pallas_call(
        spread_kernel,
        out_shape=jax.ShapeDtypeStruct((N_ZH * N_Y, ORB, LANES), f32),
        in_specs=vmem(1),
        out_specs=vmem(1)[0],
        compiler_params=params(),
        name="spread",
    )(gathered)


def exchange(x, axes):
    return lax.all_to_all(x, axes, split_axis=0, concat_axis=0, tiled=True)


def gather(x, axes, n):
    return exchange(jnp.broadcast_to(x[None], (n,) + x.shape), axes)


def body(vectors, tiles, tile_pos, diag_blocks):
    zh = lax.axis_index("zh")
    y = lax.axis_index("y")
    r = lax.axis_index("x") * N_ZL + lax.axis_index("zl")
    core = lax.axis_index("core")
    me = jnp.stack([r, y]).astype(jnp.int32)

    places = jnp.pad(tile_pos.reshape(1, 2 * TILES).astype(f32), ((0, 0), (0, LANES - 2 * TILES)))
    packed = pack(tiles[0, 0], diag_blocks[0], places)
    packed = gather(packed, "zh", N_ZH)

    sliced = slice_vectors(zh.reshape(1).astype(jnp.int32), vectors.reshape(-1, ORB, LANES))
    rows = join_cores(exchange(sliced, "core"))
    current = lax.dynamic_slice_in_dim(rows, y, 1, 0)[0]
    cols = gather(current, ROW_AX, N_R)

    packed = gather(packed, "core", N_CORE).reshape(SOURCES, ORB, WIDE)
    where = packed[:, 0, SLOTS * ORB : SLOTS * ORB + 2 * TILES].astype(jnp.int32)
    plain, turned = unpack(packed)

    centre = 0.5 * (filter_high + filter_low)
    half_width = 0.5 * (filter_high - filter_low)
    previous = None
    for step in range(DEGREE):
        out_cols, out_rows = product(where, me, cols, rows, plain, turned)
        got_rows = exchange(out_rows, "y")
        got_cols = exchange(out_cols, ROW_AX)
        image = jnp.sum(got_cols, 0) + jnp.sum(got_rows, 0)
        shifted = (image - centre * current) / half_width
        following = shifted if previous is None else 2.0 * shifted - previous
        previous, current = current, following
        if step < DEGREE - 1:
            rows = gather(current, "y", N_Y)
            cols = gather(current, ROW_AX, N_R)

    lane = lane_iota()
    swapped = jnp.concatenate([current[:, 64:], current[:, :64]], axis=1)
    mine = (lane // 64) == core
    first = jnp.where(core == 0, current, swapped)
    second = jnp.where(core == 1, current, swapped)
    halves = jnp.where(mine[None], jnp.stack([first, second]), 0.0)
    result = jnp.sum(exchange(halves, "core"), 0)
    result = gather(result, ("zh", "y"), N_ZH * N_Y).reshape(N_ZH, N_Y, ORB, LANES)
    return spread(result).reshape(vectors.shape)


def solution(mesh):
    fine = Mesh(
        mesh.devices.reshape(N_X, N_ZL, N_CORE, N_ZH, N_Y), ("x", "zl", "core", "zh", "y")
    )
    row, col = ("x", "zl", "core"), ("zh", "y")
    return jax.shard_map(
        body,
        mesh=fine,
        in_specs=(
            P(row, None),
            P(row, col, None, None, None),
            P(row, col, None, None),
            P(row + col, None, None),
        ),
        out_specs=P(row, None),
        check_vma=False,
    )
```

time: 1040 us -> 236 us (0.23)
  the two profiles are of different devices: /device:TPU:2 before, /device:TPU:1 now
where the time goes in v1:
time: 236 us; the launch traced here: 232 us
  blocking collectives  110 us (47%)
  waiting for transfers between devices  46.1 us (20%)
  starting transfers between devices  40.5 us (17%)
  Pallas kernels  29 us (12%)
  local copies, waits for them, and re-layouts  5.04 us (2%)
    all_to_all x9, blocking collectives, exchange(): return lax.all_to_all(x, axes, split_axis=0, concat_axis=0, tiled=True)  110 us
    all_to_all x7, waiting for transfers between devices, exchange(): return lax.all_to_all(x, axes, split_axis=0, concat_axis=0, tiled=True)  46.1 us
    all_to_all x7, starting transfers between devices, exchange(): return lax.all_to_all(x, axes, split_axis=0, concat_axis=0, tiled=True)  40.5 us
    pallas_call x3, Pallas kernels, product(): pl.pallas_call(product_kernel, out_shape=(shape, shape), in_specs=[smem,...  13.4 us
    pallas_call x1, Pallas kernels, unpack(): pl.pallas_call(unpack_kernel, out_shape=(shape, shape), in_specs=vmem(1),...  11.4 us
  transfers between devices with their start and end apart: 7, of which 6 were waited for; matrix products, arithmetic and copies ran while one was open for 1% of the time, Pallas kernels for 5%

profile of v1, /device:TPU:1, one launch (start us, length us, event | category | flops | bytes accessed | tf_op | source)
XLA Modules:
  0.0 232.0 jit_solution(6600363102717385176)
XLA Ops:
  2.4 10.3 %all-to-all-start.2 = ((f32[2,4,56,128]{3,2,1,0:T(8,128)}), f32[2,4,56,128]{3,2,1,0:T(8,128)S(1)}, u32[]{:S(2)}, u32[]{:S(2)}) async-start(f32[2,4,56,128]{3,2,1,0:T(8,128)} %slice_vectors.1), calls=%async_computation.2 | async-start | bytes 458752 | tf_op jit(solution)/shard_map/all_to_all | solution.py:251
  14.8 4.6 %all-to-all-start = ((f32[4,56,640]{2,1,0:T(8,128)}), f32[4,56,640]{2,1,0:T(8,128)S(1)}, u32[]{:S(2)}, u32[]{:S(2)}) async-start(f32[4,56,640]{2,1,0:T(8,128)} %broadcast_in_dim.27), calls=%async_computation | async-start | bytes 1146880 | tf_op jit(solution)/shard_map/all_to_all | solution.py:251
  19.5 12.5 %all-to-all-done = f32[4,56,640]{2,1,0:T(8,128)S(1)} async-done(((f32[4,56,640]{2,1,0:T(8,128)}), f32[4,56,640]{2,1,0:T(8,128)S(1)}, u32[]{:S(2)}, u32[]{:S(2)}) %all-to-all-start) | async-done | bytes 573472 | tf_op jit(solution)/shard_map/all_to_all | solution.py:251
  32.4 6.6 %all_to_all.80 = f32[2,4,56,640]{3,1,2,0:T(4,128)S(1)} all-to-all(f32[2,4,56,640]{3,1,2,0:T(4,128)S(1)} %broadcast_in_dim.28), channel_id=1, replica_groups=mesh['x'=4,'zl'=2,'core'=2,'zh'=4,'y'=8] {'core'}, dimensions={0} | all-to-all | bytes 2293760 | tf_op jit(solution)/shard_map/all_to_all | solution.py:251
  39.7 8.5 %all-to-all-start.3 = ((f32[8,56,128]{2,1,0:T(8,128)}), f32[8,56,128]{2,1,0:T(8,128)S(1)}, u32[]{:S(2)}, u32[]{:S(2)}) async-start(f32[8,56,128]{2,1,0:T(8,128)} %broadcast_in_dim.30), calls=%async_computation.3 | async-start | bytes 458752 | tf_op jit(solution)/shard_map/all_to_all | solution.py:251
  50.0 11.4 %unpack.1 = (bf16[88,56,128]{2,1,0:T(8,128)(2,1)S(1)}, bf16[88,56,128]{2,1,0:T(8,128)(2,1)S(1)}) custom-call(f32[8,56,640]{2,1,0:T(8,128)S(1)} %copy.8.in_ref), custom_call_target="tpu_custom_call" | custom-call | tf_op jit(solution)/shard_map/unpack/pallas_call | solution.py:107
  62.2 4.5 %product.3 = (f32[8,56,128]{2,1,0:T(8,128)S(1)}, f32[8,56,128]{2,1,0:T(8,128)}) custom-call(s32[8,20]{1,0:T(8,128)S(1)} %fusion.4.pos_ref, s32[2]{0:T(128)S(1)} %pad_add_fusion.me_ref, f32[8,56,128]{2,1,0:T(8,128)S(1)} %all-to-all-done.3.cols_ref, f32[8,56,128]{2,1,0:T(8,128)S(1)} %join_cores.1.rows_ref, ...), custom_call_target="tpu_custom_call" | custom-call | tf_op jit(solution)/shard_map/product/pallas_call | solution.py:209
  66.7 10.9 %all_to_all.81 = f32[8,56,128]{2,1,0:T(8,128)S(1)} all-to-all(f32[8,56,128]{2,1,0:T(8,128)S(1)} %get-tuple-element.15), channel_id=1, replica_groups=mesh['x'=4,'zl'=2,'core'=2,'zh'=4,'y'=8] {'x','zl'}, dimensions={0} | all-to-all | bytes 458752 | tf_op jit(solution)/shard_map/all_to_all | solution.py:251
  77.6 6.8 %all-to-all-start.5 = ((f32[8,56,128]{2,1,0:T(8,128)}), f32[8,56,128]{2,1,0:T(8,128)S(1)}, u32[]{:S(2)}, u32[]{:S(2)}) async-start(f32[8,56,128]{2,1,0:T(8,128)} %get-tuple-element.16), calls=%async_computation.5 | async-start | bytes 458752 | tf_op jit(solution)/shard_map/all_to_all | solution.py:251
  84.4 9.0 %all-to-all-done.5 = f32[8,56,128]{2,1,0:T(8,128)S(1)} async-done(((f32[8,56,128]{2,1,0:T(8,128)}), f32[8,56,128]{2,1,0:T(8,128)S(1)}, u32[]{:S(2)}, u32[]{:S(2)}) %all-to-all-start.5) | async-done | bytes 229408 | tf_op jit(solution)/shard_map/all_to_all | solution.py:251
  93.5 8.4 %all_to_all.82.cols_ref = f32[8,56,128]{2,1,0:T(8,128)S(1)} all-to-all(f32[8,56,128]{2,1,0:T(8,128)S(1)} %broadcast_in_dim.36), channel_id=1, replica_groups=mesh['x'=4,'zl'=2,'core'=2,'zh'=4,'y'=8] {'x','zl'}, dimensions={0} | all-to-all | bytes 458752 | tf_op jit(solution)/shard_map/all_to_all | solution.py:251
  101.9 11.4 %all_to_all.83.rows_ref = f32[8,56,128]{2,1,0:T(8,128)S(1)} all-to-all(f32[8,56,128]{2,1,0:T(8,128)S(1)} %broadcast_in_dim.36), channel_id=1, replica_groups=mesh['x'=4,'zl'=2,'core'=2,'zh'=4,'y'=8] {'y'}, dimensions={0} | all-to-all | bytes 458752 | tf_op jit(solution)/shard_map/all_to_all | solution.py:251
  113.3 4.5 %product.4 = (f32[8,56,128]{2,1,0:T(8,128)S(1)}, f32[8,56,128]{2,1,0:T(8,128)}) custom-call(s32[8,20]{1,0:T(8,128)S(1)} %fusion.4.pos_ref, s32[2]{0:T(128)S(1)} %pad_add_fusion.me_ref, f32[8,56,128]{2,1,0:T(8,128)S(1)} %all_to_all.82.cols_ref, f32[8,56,128]{2,1,0:T(8,128)S(1)} %all_to_all.83.rows_ref, bf16[88,56,128]{2,1,0:T(8,128)(2,1)S(1)} %get-tuple-element.13.plain_ref, ...), custom_call_target="tpu_custom_call" | custom-call | tf_op jit(solution)/shard_map/product/pallas_call | solution.py:209
  117.7 8.4 %all_to_all.84 = f32[8,56,128]{2,1,0:T(8,128)S(1)} all-to-all(f32[8,56,128]{2,1,0:T(8,128)S(1)} %get-tuple-element.17), channel_id=1, replica_groups=mesh['x'=4,'zl'=2,'core'=2,'zh'=4,'y'=8] {'x','zl'}, dimensions={0} | all-to-all | bytes 458752 | tf_op jit(solution)/shard_map/all_to_all | solution.py:251
  126.1 3.4 %all-to-all-start.9 = ((f32[8,56,128]{2,1,0:T(8,128)}), f32[8,56,128]{2,1,0:T(8,128)S(1)}, u32[]{:S(2)}, u32[]{:S(2)}) async-start(f32[8,56,128]{2,1,0:T(8,128)} %get-tuple-element.18), calls=%async_computation.9 | async-start | bytes 458752 | tf_op jit(solution)/shard_map/all_to_all | solution.py:251
  129.5 8.9 %all-to-all-done.9 = f32[8,56,128]{2,1,0:T(8,128)S(1)} async-done(((f32[8,56,128]{2,1,0:T(8,128)}), f32[8,56,128]{2,1,0:T(8,128)S(1)}, u32[]{:S(2)}, u32[]{:S(2)}) %all-to-all-start.9) | async-done | bytes 229408 | tf_op jit(solution)/shard_map/all_to_all | solution.py:251
  138.5 8.4 %all_to_all.85.cols_ref = f32[8,56,128]{2,1,0:T(8,128)S(1)} all-to-all(f32[8,56,128]{2,1,0:T(8,128)S(1)} %broadcast_in_dim.38), channel_id=1, replica_groups=mesh['x'=4,'zl'=2,'core'=2,'zh'=4,'y'=8] {'x','zl'}, dimensions={0} | all-to-all | bytes 458752 | tf_op jit(solution)/shard_map/all_to_all | solution.py:251
  146.8 11.4 %all_to_all.86.rows_ref = f32[8,56,128]{2,1,0:T(8,128)S(1)} all-to-all(f32[8,56,128]{2,1,0:T(8,128)S(1)} %broadcast_in_dim.38), channel_id=1, replica_groups=mesh['x'=4,'zl'=2,'core'=2,'zh'=4,'y'=8] {'y'}, dimensions={0} | all-to-all | bytes 458752 | tf_op jit(solution)/shard_map/all_to_all | solution.py:251
  158.2 4.5 %product.5 = (f32[8,56,128]{2,1,0:T(8,128)}, f32[8,56,128]{2,1,0:T(8,128)}) custom-call(s32[8,20]{1,0:T(8,128)S(1)} %fusion.4.pos_ref, s32[2]{0:T(128)S(1)} %pad_add_fusion.me_ref, f32[8,56,128]{2,1,0:T(8,128)S(1)} %all_to_all.85.cols_ref, f32[8,56,128]{2,1,0:T(8,128)S(1)} %all_to_all.86.rows_ref, bf16[88,56,128]{2,1,0:T(8,128)(2,1)S(1)} %get-tuple-element.13.plain_ref, ...), custom_call_target="tpu_custom_call" | custom-call | tf_op jit(solution)/shard_map/product/pallas_call | solution.py:209
  162.7 3.4 %all-to-all-start.12 = ((f32[8,56,128]{2,1,0:T(8,128)}), f32[8,56,128]{2,1,0:T(8,128)S(1)}, u32[]{:S(2)}, u32[]{:S(2)}) async-start(f32[8,56,128]{2,1,0:T(8,128)} %get-tuple-element.19), calls=%async_computation.12 | async-start | bytes 458752 | tf_op jit(solution)/shard_map/all_to_all | solution.py:251
  166.1 5.9 %all-to-all-done.12 = f32[8,56,128]{2,1,0:T(8,128)S(1)} async-done(((f32[8,56,128]{2,1,0:T(8,128)}), f32[8,56,128]{2,1,0:T(8,128)S(1)}, u32[]{:S(2)}, u32[]{:S(2)}) %all-to-all-start.12) | async-done | bytes 229408 | tf_op jit(solution)/shard_map/all_to_all | solution.py:251
  175.5 8.8 %all-to-all-done.13 = f32[8,56,128]{2,1,0:T(8,128)S(1)} async-done(((f32[8,56,128]{2,1,0:T(8,128)}), f32[8,56,128]{2,1,0:T(8,128)S(1)}, u32[]{:S(2)}, u32[]{:S(2)}) %all-to-all-start.13) | async-done | bytes 229408 | tf_op jit(solution)/shard_map/all_to_all | solution.py:251
  184.6 16.7 %all_to_all.87 = f32[2,56,128]{2,1,0:T(8,128)S(1)} all-to-all(f32[2,56,128]{2,1,0:T(8,128)S(1)} %maximum_select_fusion), channel_id=1, replica_groups=mesh['x'=4,'zl'=2,'core'=2,'zh'=4,'y'=8] {'core'}, dimensions={0} | all-to-all | bytes 114688 | tf_op jit(solution)/shard_map/all_to_all | solution.py:251
  201.4 28.0 %all_to_all.88 = f32[32,56,128]{2,1,0:T(8,128)S(1)} all-to-all(f32[32,56,128]{2,1,0:T(8,128)S(1)} %broadcast_in_dim.72), channel_id=1, replica_groups=mesh['x'=4,'zl'=2,'core'=2,'zh'=4,'y'=8] {'zh','y'}, dimensions={0} | all-to-all | bytes 1835008 | tf_op jit(solution)/shard_map/all_to_all | solution.py:251
  (50 shorter events, 14.7 us)
Async XLA Ops:
  0.0 12.7 %copy-start.4 = (s32[1,1,2,10]{3,2,1,0:T(2,128)S(1)}, s32[1,1,2,10]{3,2,1,0:T(2,128)}, u32[]{:S(2)}) copy-start(s32[1,1,2,10]{3,2,1,0:T(2,128)} %param.6) | copy-start | bytes 244
  0.0 1.2 copy-start
  1.2 11.6 %copy-start.1 = (f32[1,1,10,56,56]{4,3,2,1,0:T(8,128)S(1)}, f32[1,1,10,56,56]{4,3,2,1,0:T(8,128)}, u32[]{:S(2)}) copy-start(f32[1,1,10,56,56]{4,3,2,1,0:T(8,128)} %param.5) | copy-start | bytes 376324
  1.2 11.6 %copy-start.2 = (f32[1,56,56]{2,1,0:T(8,128)S(1)}, f32[1,56,56]{2,1,0:T(8,128)}, u32[]{:S(2)}) copy-start(f32[1,56,56]{2,1,0:T(8,128)} %param.7) | copy-start | bytes 37636
  2.4 11.5 %all-to-all-start.2 = ((f32[2,4,56,128]{3,2,1,0:T(8,128)}), f32[2,4,56,128]{3,2,1,0:T(8,128)S(1)}, u32[]{:S(2)}, u32[]{:S(2)}) async-start(f32[2,4,56,128]{3,2,1,0:T(8,128)} %slice_vectors.1), calls=%async_computation.2 | async-start | bytes 458752 | tf_op jit(solution)/shard_map/all_to_all | solution.py:251
  14.8 17.3 %all-to-all-start = ((f32[4,56,640]{2,1,0:T(8,128)}), f32[4,56,640]{2,1,0:T(8,128)S(1)}, u32[]{:S(2)}, u32[]{:S(2)}) async-start(f32[4,56,640]{2,1,0:T(8,128)} %broadcast_in_dim.27), calls=%async_computation | async-start | bytes 1146880 | tf_op jit(solution)/shard_map/all_to_all | solution.py:251
  39.7 22.5 %all-to-all-start.3 = ((f32[8,56,128]{2,1,0:T(8,128)}), f32[8,56,128]{2,1,0:T(8,128)S(1)}, u32[]{:S(2)}, u32[]{:S(2)}) async-start(f32[8,56,128]{2,1,0:T(8,128)} %broadcast_in_dim.30), calls=%async_computation.3 | async-start | bytes 458752 | tf_op jit(solution)/shard_map/all_to_all | solution.py:251
  48.8 1.0 copy-start.3
  77.6 15.9 %all-to-all-start.5 = ((f32[8,56,128]{2,1,0:T(8,128)}), f32[8,56,128]{2,1,0:T(8,128)S(1)}, u32[]{:S(2)}, u32[]{:S(2)}) async-start(f32[8,56,128]{2,1,0:T(8,128)} %get-tuple-element.16), calls=%async_computation.5 | async-start | bytes 458752 | tf_op jit(solution)/shard_map/all_to_all | solution.py:251
  126.1 12.3 %all-to-all-start.9 = ((f32[8,56,128]{2,1,0:T(8,128)}), f32[8,56,128]{2,1,0:T(8,128)S(1)}, u32[]{:S(2)}, u32[]{:S(2)}) async-start(f32[8,56,128]{2,1,0:T(8,128)} %get-tuple-element.18), calls=%async_computation.9 | async-start | bytes 458752 | tf_op jit(solution)/shard_map/all_to_all | solution.py:251
  162.7 9.3 %all-to-all-start.12 = ((f32[8,56,128]{2,1,0:T(8,128)}), f32[8,56,128]{2,1,0:T(8,128)S(1)}, u32[]{:S(2)}, u32[]{:S(2)}) async-start(f32[8,56,128]{2,1,0:T(8,128)} %get-tuple-element.19), calls=%async_computation.12 | async-start | bytes 458752 | tf_op jit(solution)/shard_map/all_to_all | solution.py:251
  172.0 12.3 %all-to-all-start.13 = ((f32[8,56,128]{2,1,0:T(8,128)}), f32[8,56,128]{2,1,0:T(8,128)S(1)}, u32[]{:S(2)}, u32[]{:S(2)}) async-start(f32[8,56,128]{2,1,0:T(8,128)} %get-tuple-element.20), calls=%async_computation.13 | async-start | bytes 458752 | tf_op jit(solution)/shard_map/all_to_all | solution.py:251

commit v2 on v1

--- a/solution.py
+++ b/solution.py
@@ -17,6 +17,7 @@
 SOURCES = N_CORE * N_ZH
 WIDE = 640
 VS = 16
+PLACE = SLOTS * ORB - (WIDE - LANES)
 ROW_AX = ("x", "zl")
 GROUPS = 8
 
@@ -82,7 +83,7 @@
     return (high + pltpu.roll(low, 64, 1)).astype(bf16)
 
 
-def unpack_kernel(in_ref, plain_ref, turned_ref):
+def unpack_kernel(in_ref, blocks_ref, places_ref):
     lane = lane_iota()
 
     def one_source(s, carry):
@@ -93,20 +94,23 @@
             if off + ORB > LANES:
                 y = roll_to(in_ref[s, :, (q + 1) * LANES : (q + 2) * LANES], off, 0)
                 x = jnp.where(lane < LANES - off, x, y)
-            x = jnp.where(lane < ORB, x, 0.0)
-            plain_ref[s * SLOTS + t] = two_terms(x)
-            square = jnp.concatenate([x, jnp.zeros((LANES - ORB, LANES), f32)], axis=0)
-            turned_ref[s * SLOTS + t] = two_terms(square.T[:ORB])
+            blocks_ref[s * SLOTS + t] = two_terms(jnp.where(lane < ORB, x, 0.0))
         return carry
 
     lax.fori_loop(0, SOURCES, one_source, 0)
+    for s in range(SOURCES):
+        last = in_ref[s, 0:1, WIDE - LANES : WIDE]
+        shown = lax.broadcasted_iota(jnp.int32, (1, LANES), 1) >= PLACE
+        places_ref[s : s + 1] = jnp.where(shown, last, 0.0).astype(jnp.int32)
 
 
 def unpack(packed):
-    shape = jax.ShapeDtypeStruct((SOURCES * SLOTS, ORB, LANES), bf16)
     return pl.pallas_call(
         unpack_kernel,
-        out_shape=(shape, shape),
+        out_shape=(
+            jax.ShapeDtypeStruct((SOURCES * SLOTS, ORB, LANES), bf16),
+            jax.ShapeDtypeStruct((SOURCES, LANES), jnp.int32),
+        ),
         in_specs=vmem(1),
         out_specs=tuple(vmem(2)),
         compiler_params=params(),
@@ -142,84 +146,104 @@
     )(zh, blocks)
 
 
-def join_kernel(in_ref, out_ref):
-    lane = lane_iota()
+def join_kernel(core_ref, mine_ref, other_ref, out_ref):
+    lane = lane_iota()
+    is_zero = core_ref[0] == 0
     for yp in range(N_Y // 2):
-        a, b = in_ref[0, yp], in_ref[1, yp]
+        mine, other = mine_ref[yp], other_ref[yp]
+        a = jnp.where(is_zero, mine, other)
+        b = jnp.where(is_zero, other, mine)
         out_ref[2 * yp] = jnp.where(lane < 64, a, pltpu.roll(b, 64, 1))
         out_ref[2 * yp + 1] = jnp.where(lane < 64, pltpu.roll(a, 64, 1), b)
 
 
-def join_cores(both):
+def join_cores(core, mine, other):
     return pl.pallas_call(
         join_kernel,
         out_shape=jax.ShapeDtypeStruct((N_Y, ORB, LANES), f32),
-        in_specs=vmem(1),
+        in_specs=[pl.BlockSpec(memory_space=pltpu.SMEM)] + vmem(2),
         out_specs=vmem(1)[0],
         compiler_params=params(),
         name="join_cores",
-    )(both)
-
-
-def product_kernel(
-    pos_ref, me_ref, cols_ref, rows_ref, plain_ref, turned_ref,
-    out_cols_ref, out_rows_ref, vc_ref, vr_ref, acc_c_ref, acc_r_ref,
-):
-    for src, dst in ((cols_ref, vc_ref), (rows_ref, vr_ref)):
-        for chunk in range(GROUPS):
-            x = src[chunk].T
-            high = x.astype(bf16)
-            low = (x - high.astype(f32)).astype(bf16)
-            for o in range(GROUPS):
-                dst[chunk * GROUPS + o, 0:VS] = high[o * VS : (o + 1) * VS]
-                dst[chunk * GROUPS + o, VS : 2 * VS] = low[o * VS : (o + 1) * VS]
-    acc_c_ref[...] = jnp.zeros_like(acc_c_ref)
-    acc_r_ref[...] = jnp.zeros_like(acc_r_ref)
+    )(core, mine, other)
+
+
+def split_terms(src_ref, dst_ref):
+    gap = jnp.zeros((64 - ORB, LANES), f32)
+    for chunk in range(GROUPS):
+        x = src_ref[chunk]
+        x = jnp.concatenate([x, gap, x, gap], axis=0).T
+        high = x.astype(bf16)
+        low = (x - high.astype(f32)).astype(bf16)
+        for o in range(GROUPS):
+            dst_ref[chunk * GROUPS + o, 0:VS] = high[o * VS : (o + 1) * VS]
+            dst_ref[chunk * GROUPS + o, VS : 2 * VS] = low[o * VS : (o + 1) * VS]
+
+
+def row_col(pos_ref, s, t):
+    i, g = pos_ref[s, PLACE + t], pos_ref[s, PLACE + TILES + t]
+    row = (i & 7) * GROUPS + (s // N_ZH) * N_ZH + (i >> 3)
+    col = (g >> 1) * GROUPS + (g & 1) * N_ZH + s % N_ZH
+    return row, col
+
+
+def mirror_kernel(pos_ref, rows_ref, blocks_ref, out_ref, v_ref, acc_ref):
+    split_terms(rows_ref, v_ref)
+    acc_ref[...] = jnp.zeros_like(acc_ref)
+
+    def one_source(s, carry):
+        for t in range(TILES):
+            row, col = row_col(pos_ref, s, t)
+            both = jnp.dot(v_ref[row][:, :ORB], blocks_ref[s * SLOTS + t], preferred_element_type=f32)
+            acc_ref[col] += both[:VS] + both[VS:]
+        return carry
+
+    lax.fori_loop(0, SOURCES, one_source, 0)
+    for chunk in range(GROUPS):
+        x = acc_ref[chunk * GROUPS : (chunk + 1) * GROUPS].reshape(LANES, LANES)
+        x = x + pltpu.roll(x, 64, 1)
+        out_ref[chunk] = x.T[:ORB]
+
+
+def direct_kernel(pos_ref, me_ref, cols_ref, blocks_ref, out_ref, v_ref, acc_ref):
+    split_terms(cols_ref, v_ref)
+    acc_ref[...] = jnp.zeros_like(acc_ref)
     my_r, my_y = me_ref[0], me_ref[1]
 
-    def times(v, block):
-        both = jnp.dot(v, block, preferred_element_type=f32)
-        return both[:VS] + both[VS:]
-
     def one_source(s, carry):
-        core_s, zh_s = s // N_ZH, s % N_ZH
         for t in range(SLOTS):
-            n = s * SLOTS + t
             if t < TILES:
-                i, g = pos_ref[s, t], pos_ref[s, TILES + t]
-                row = (i % N_Y) * GROUPS + core_s * N_ZH + i // N_Y
-                col = (g // N_CORE) * GROUPS + (g % N_CORE) * N_ZH + zh_s
-                acc_r_ref[row] += times(vc_ref[col], turned_ref[n])
-                acc_c_ref[col] += times(vr_ref[row], plain_ref[n])
+                row, col = row_col(pos_ref, s, t)
             else:
-                acc_r_ref[my_y * GROUPS + s] += times(vc_ref[my_r * GROUPS + s], turned_ref[n])
+                row, col = my_y * GROUPS + s, my_r * GROUPS + s
+            both = lax.dot_general(
+                v_ref[col], blocks_ref[s * SLOTS + t], (((1,), (1,)), ((), ())),
+                preferred_element_type=f32,
+            )
+            acc_ref[row, :, 0:ORB] += both[:VS] + both[VS:]
         return carry
 
     lax.fori_loop(0, SOURCES, one_source, 0)
-    for acc, out in ((acc_c_ref, out_cols_ref), (acc_r_ref, out_rows_ref)):
-        for chunk in range(GROUPS):
-            x = acc[chunk * GROUPS : (chunk + 1) * GROUPS].reshape(LANES, LANES)
-            x = x + pltpu.roll(x, 64, 1)
-            out[chunk] = x.T[:ORB]
-
-
-def product(places, me, cols, rows, plain, turned):
-    shape = jax.ShapeDtypeStruct((GROUPS, ORB, LANES), f32)
+    for chunk in range(GROUPS):
+        x = acc_ref[chunk * GROUPS : (chunk + 1) * GROUPS].reshape(LANES, LANES)
+        out_ref[chunk] = x.T[:ORB]
+
+
+def product(kernel, name, scalars, field, blocks):
     smem = pl.BlockSpec(memory_space=pltpu.SMEM)
     return pl.pallas_call(
-        product_kernel,
-        out_shape=(shape, shape),
-        in_specs=[smem, smem] + vmem(4),
-        out_specs=tuple(vmem(2)),
+        kernel,
+        out_shape=jax.ShapeDtypeStruct((GROUPS, ORB, LANES), f32),
+        in_specs=[smem] * len(scalars) + vmem(2),
+        out_specs=vmem(1)[0],
         scratch_shapes=[
-            pltpu.VMEM((GROUPS * GROUPS, 2 * VS, ORB), bf16),
-            pltpu.VMEM((GROUPS * GROUPS, 2 * VS, ORB), bf16),
-            pltpu.VMEM((GROUPS * GROUPS, VS, LANES), f32),
+            pltpu.VMEM((GROUPS * GROUPS, 2 * VS, LANES), bf16),
             pltpu.VMEM((GROUPS * GROUPS, VS, LANES), f32),
         ],
         compiler_params=params(),
-        name="product",
-    )(places, me, cols, rows, plain, turned)
+        cost_estimate=pl.CostEstimate(flops=200000000, bytes_accessed=4000000, transcendentals=0),
+        name=name,
+    )(*scalars, field, blocks)
 
 
 def spread_kernel(in_ref, out_ref):
@@ -267,21 +291,25 @@
     packed = gather(packed, "zh", N_ZH)
 
     sliced = slice_vectors(zh.reshape(1).astype(jnp.int32), vectors.reshape(-1, ORB, LANES))
-    rows = join_cores(exchange(sliced, "core"))
-    current = lax.dynamic_slice_in_dim(rows, y, 1, 0)[0]
-    cols = gather(current, ROW_AX, N_R)
-
-    packed = gather(packed, "core", N_CORE).reshape(SOURCES, ORB, WIDE)
-    where = packed[:, 0, SLOTS * ORB : SLOTS * ORB + 2 * TILES].astype(jnp.int32)
-    plain, turned = unpack(packed)
+    mine = lax.dynamic_index_in_dim(sliced, core, 0, keepdims=False)
+    other = lax.dynamic_index_in_dim(sliced, 1 - core, 0, keepdims=False)
+    other = lax.ppermute(other, "core", [(0, 1), (1, 0)])
+    rows = join_cores(core.reshape(1).astype(jnp.int32), mine, other)
+    current = lax.dynamic_index_in_dim(rows, y, 0, keepdims=False)
+    cols = lax.all_gather(current, ROW_AX, axis=0, tiled=False)
+    packed, cols = lax.optimization_barrier((packed, cols))
+
+    packed = gather(packed.reshape(N_ZH * ORB, WIDE), "core", N_CORE)
+    blocks, where = unpack(packed.reshape(SOURCES, ORB, WIDE))
 
     centre = 0.5 * (filter_high + filter_low)
     half_width = 0.5 * (filter_high - filter_low)
     previous = None
     for step in range(DEGREE):
-        out_cols, out_rows = product(where, me, cols, rows, plain, turned)
+        out_cols = product(mirror_kernel, "mirror", (where,), rows, blocks)
+        got_cols = exchange(out_cols, ROW_AX)
+        out_rows = product(direct_kernel, "direct", (where, me), cols, blocks)
         got_rows = exchange(out_rows, "y")
-        got_cols = exchange(out_cols, ROW_AX)
         image = jnp.sum(got_cols, 0) + jnp.sum(got_rows, 0)
         shifted = (image - centre * current) / half_width
         following = shifted if previous is None else 2.0 * shifted - previous

time: 236 us -> 234 us (level)
  the two profiles are of different devices: /device:TPU:1 before, /device:TPU:8 now
where the time goes in v2:
time: 234 us; the launch traced here: 233 us
  blocking collectives  101 us (43%)
  starting transfers between devices  49.9 us (21%)
  waiting for transfers between devices  49.4 us (21%)
  Pallas kernels  26.8 us (11%)
  local copies, waits for them, and re-layouts  4.3 us (2%)
    all_to_all x5, blocking collectives, exchange(): return lax.all_to_all(x, axes, split_axis=0, concat_axis=0, tiled=True)  65.4 us
    all_to_all x9, waiting for transfers between devices, exchange(): return lax.all_to_all(x, axes, split_axis=0, concat_axis=0, tiled=True)  48.2 us
    all_to_all x9, starting transfers between devices, exchange(): return lax.all_to_all(x, axes, split_axis=0, concat_axis=0, tiled=True)  48 us
    all_gather x1, blocking collectives, body(): cols = lax.all_gather(current, ROW_AX, axis=0, tiled=False)  35.5 us
    pallas_call x6, Pallas kernels, product(): pl.pallas_call(kernel, out_shape=jax.ShapeDtypeStruct((GROUPS, ORB, LANES...  20 us
  transfers between devices with their start and end apart: 10, of which 9 were waited for; matrix products, arithmetic and copies ran while one was open for 0% of the time, Pallas kernels for 7%

profile of v2, /device:TPU:8, one launch (start us, length us, event | category | flops | bytes accessed | tf_op | source)
XLA Modules:
  0.0 232.6 jit_solution(9954293256668244420)
XLA Ops:
  3.5 10.3 %all-to-all-start = ((f32[4,56,640]{2,1,0:T(8,128)}), f32[4,56,640]{2,1,0:T(8,128)S(1)}, u32[]{:S(2)}, u32[]{:S(2)}) async-start(f32[4,56,640]{2,1,0:T(8,128)} %broadcast_in_dim.25), calls=%async_computation | async-start | bytes 1146880 | tf_op jit(solution)/shard_map/all_to_all | solution.py:275
  17.7 35.5 %all_gather.4.cols_ref = f32[8,56,128]{2,1,0:T(8,128)S(1)} all-gather(f32[1,56,128]{2,1,0:T(8,128)S(1)} %constant_dynamic-slice_fusion), channel_id=1, replica_groups=mesh['x'=4,'zl'=2,'core'=2,'zh'=4,'y'=8] {'x','zl'}, dimensions={0}, use_global_device_ids=true | all-gather | bytes 258048 | tf_op jit(solution)/shard_map/all_gather | solution.py:299
  53.3 4.6 %all_to_all.70 = f32[2,224,640]{2,1,0:T(8,128)S(1)} all-to-all(f32[2,224,640]{2,1,0:T(8,128)S(1)} %broadcast_in_dim.27), channel_id=1, replica_groups=mesh['x'=4,'zl'=2,'core'=2,'zh'=4,'y'=8] {'core'}, dimensions={0} | all-to-all | bytes 2293760 | tf_op jit(solution)/shard_map/all_to_all | solution.py:275
  61.3 3.4 %direct.3 = f32[8,56,128]{2,1,0:T(8,128)} custom-call(s32[8,128]{1,0:T(8,128)S(1)} %get-tuple-element.10.pos_ref, s32[2]{0:T(128)S(1)} %pad_add_fusion.me_ref, f32[8,56,128]{2,1,0:T(8,128)S(1)} %all_gather.4.cols_ref, bf16[88,56,128]{2,1,0:T(8,128)(2,1)S(1)} %get-tuple-element.11.blocks_ref), custom_call_target="tpu_custom_call" | custom-call | flops 200000000 | bytes 4000000 | tf_op jit(solution)/shard_map/direct/pallas_call | solution.py:234
  64.7 7.5 %all-to-all-start.3 = ((f32[8,56,128]{2,1,0:T(8,128)}), f32[8,56,128]{2,1,0:T(8,128)S(1)}, u32[]{:S(2)}, u32[]{:S(2)}) async-start(f32[8,56,128]{2,1,0:T(8,128)} %direct.3), calls=%async_computation.3 | async-start | bytes 458752 | tf_op jit(solution)/shard_map/all_to_all | solution.py:275
  75.5 6.8 %all-to-all-done.3 = f32[8,56,128]{2,1,0:T(8,128)S(1)} async-done(((f32[8,56,128]{2,1,0:T(8,128)}), f32[8,56,128]{2,1,0:T(8,128)S(1)}, u32[]{:S(2)}, u32[]{:S(2)}) %all-to-all-start.3) | async-done | bytes 229408 | tf_op jit(solution)/shard_map/all_to_all | solution.py:275
  82.3 3.4 %all-to-all-start.2 = ((f32[8,56,128]{2,1,0:T(8,128)}), f32[8,56,128]{2,1,0:T(8,128)S(1)}, u32[]{:S(2)}, u32[]{:S(2)}) async-start(f32[8,56,128]{2,1,0:T(8,128)} %mirror.3), calls=%async_computation.2 | async-start | bytes 458752 | tf_op jit(solution)/shard_map/all_to_all | solution.py:275
  85.7 7.0 %all-to-all-done.2 = f32[8,56,128]{2,1,0:T(8,128)S(1)} async-done(((f32[8,56,128]{2,1,0:T(8,128)}), f32[8,56,128]{2,1,0:T(8,128)S(1)}, u32[]{:S(2)}, u32[]{:S(2)}) %all-to-all-start.2) | async-done | bytes 229408 | tf_op jit(solution)/shard_map/all_to_all | solution.py:275
  93.5 10.4 %all_to_all.71.cols_ref = f32[8,56,128]{2,1,0:T(8,128)S(1)} all-to-all(f32[8,56,128]{2,1,0:T(8,128)} %broadcast_in_dim.33), channel_id=1, replica_groups=mesh['x'=4,'zl'=2,'core'=2,'zh'=4,'y'=8] {'x','zl'}, dimensions={0} | all-to-all | bytes 458752 | tf_op jit(solution)/shard_map/all_to_all | solution.py:275
  103.9 4.8 %all-to-all-start.4 = ((f32[8,56,128]{2,1,0:T(8,128)}), f32[8,56,128]{2,1,0:T(8,128)S(1)}, u32[]{:S(2)}, u32[]{:S(2)}) async-start(f32[8,56,128]{2,1,0:T(8,128)} %broadcast_in_dim.33), calls=%async_computation.4 | async-start | bytes 458752 | tf_op jit(solution)/shard_map/all_to_all | solution.py:275
  108.6 3.4 %direct.4 = f32[8,56,128]{2,1,0:T(8,128)} custom-call(s32[8,128]{1,0:T(8,128)S(1)} %get-tuple-element.10.pos_ref, s32[2]{0:T(128)S(1)} %pad_add_fusion.me_ref, f32[8,56,128]{2,1,0:T(8,128)S(1)} %all_to_all.71.cols_ref, bf16[88,56,128]{2,1,0:T(8,128)(2,1)S(1)} %get-tuple-element.11.blocks_ref), custom_call_target="tpu_custom_call" | custom-call | flops 200000000 | bytes 4000000 | tf_op jit(solution)/shard_map/direct/pallas_call | solution.py:234
  112.1 5.0 %all-to-all-done.4.rows_ref = f32[8,56,128]{2,1,0:T(8,128)S(1)} async-done(((f32[8,56,128]{2,1,0:T(8,128)}), f32[8,56,128]{2,1,0:T(8,128)S(1)}, u32[]{:S(2)}, u32[]{:S(2)}) %all-to-all-start.4) | async-done | bytes 229408 | tf_op jit(solution)/shard_map/all_to_all | solution.py:275
  117.1 5.0 %all-to-all-start.7 = ((f32[8,56,128]{2,1,0:T(8,128)}), f32[8,56,128]{2,1,0:T(8,128)S(1)}, u32[]{:S(2)}, u32[]{:S(2)}) async-start(f32[8,56,128]{2,1,0:T(8,128)} %direct.4), calls=%async_computation.7 | async-start | bytes 458752 | tf_op jit(solution)/shard_map/all_to_all | solution.py:275
  125.3 5.2 %all-to-all-done.7 = f32[8,56,128]{2,1,0:T(8,128)S(1)} async-done(((f32[8,56,128]{2,1,0:T(8,128)}), f32[8,56,128]{2,1,0:T(8,128)S(1)}, u32[]{:S(2)}, u32[]{:S(2)}) %all-to-all-start.7) | async-done | bytes 229408 | tf_op jit(solution)/shard_map/all_to_all | solution.py:275
  134.0 7.0 %all-to-all-done.5 = f32[8,56,128]{2,1,0:T(8,128)S(1)} async-done(((f32[8,56,128]{2,1,0:T(8,128)}), f32[8,56,128]{2,1,0:T(8,128)S(1)}, u32[]{:S(2)}, u32[]{:S(2)}) %all-to-all-start.5) | async-done | bytes 229408 | tf_op jit(solution)/shard_map/all_to_all | solution.py:275
  141.7 10.4 %all_to_all.72.cols_ref = f32[8,56,128]{2,1,0:T(8,128)S(1)} all-to-all(f32[8,56,128]{2,1,0:T(8,128)} %broadcast_in_dim.35), channel_id=1, replica_groups=mesh['x'=4,'zl'=2,'core'=2,'zh'=4,'y'=8] {'x','zl'}, dimensions={0} | all-to-all | bytes 458752 | tf_op jit(solution)/shard_map/all_to_all | solution.py:275
  152.2 5.0 %all-to-all-start.8 = ((f32[8,56,128]{2,1,0:T(8,128)}), f32[8,56,128]{2,1,0:T(8,128)S(1)}, u32[]{:S(2)}, u32[]{:S(2)}) async-start(f32[8,56,128]{2,1,0:T(8,128)} %broadcast_in_dim.35), calls=%async_computation.8 | async-start | bytes 458752 | tf_op jit(solution)/shard_map/all_to_all | solution.py:275
  157.2 3.4 %direct.5 = f32[8,56,128]{2,1,0:T(8,128)} custom-call(s32[8,128]{1,0:T(8,128)S(1)} %get-tuple-element.10.pos_ref, s32[2]{0:T(128)S(1)} %pad_add_fusion.me_ref, f32[8,56,128]{2,1,0:T(8,128)S(1)} %all_to_all.72.cols_ref, bf16[88,56,128]{2,1,0:T(8,128)(2,1)S(1)} %get-tuple-element.11.blocks_ref), custom_call_target="tpu_custom_call" | custom-call | flops 200000000 | bytes 4000000 | tf_op jit(solution)/shard_map/direct/pallas_call | solution.py:234
  160.6 5.0 %all-to-all-done.8.rows_ref = f32[8,56,128]{2,1,0:T(8,128)S(1)} async-done(((f32[8,56,128]{2,1,0:T(8,128)}), f32[8,56,128]{2,1,0:T(8,128)S(1)}, u32[]{:S(2)}, u32[]{:S(2)}) %all-to-all-start.8) | async-done | bytes 229408 | tf_op jit(solution)/shard_map/all_to_all | solution.py:275
  165.6 5.1 %all-to-all-start.11 = ((f32[8,56,128]{2,1,0:T(8,128)}), f32[8,56,128]{2,1,0:T(8,128)S(1)}, u32[]{:S(2)}, u32[]{:S(2)}) async-start(f32[8,56,128]{2,1,0:T(8,128)} %direct.5), calls=%async_computation.11 | async-start | bytes 458752 | tf_op jit(solution)/shard_map/all_to_all | solution.py:275
  174.0 5.2 %all-to-all-done.11 = f32[8,56,128]{2,1,0:T(8,128)S(1)} async-done(((f32[8,56,128]{2,1,0:T(8,128)}), f32[8,56,128]{2,1,0:T(8,128)S(1)}, u32[]{:S(2)}, u32[]{:S(2)}) %all-to-all-start.11) | async-done | bytes 229408 | tf_op jit(solution)/shard_map/all_to_all | solution.py:275
  182.7 7.0 %all-to-all-done.9 = f32[8,56,128]{2,1,0:T(8,128)S(1)} async-done(((f32[8,56,128]{2,1,0:T(8,128)}), f32[8,56,128]{2,1,0:T(8,128)S(1)}, u32[]{:S(2)}, u32[]{:S(2)}) %all-to-all-start.9) | async-done | bytes 229408 | tf_op jit(solution)/shard_map/all_to_all | solution.py:275
  189.9 3.8 %all_to_all.73 = f32[2,56,128]{2,1,0:T(8,128)S(1)} all-to-all(f32[2,56,128]{2,1,0:T(8,128)S(1)} %maximum_select_fusion), channel_id=1, replica_groups=mesh['x'=4,'zl'=2,'core'=2,'zh'=4,'y'=8] {'core'}, dimensions={0} | all-to-all | bytes 114688 | tf_op jit(solution)/shard_map/all_to_all | solution.py:275
  193.8 36.1 %all_to_all.74 = f32[32,56,128]{2,1,0:T(8,128)S(1)} all-to-all(f32[32,56,128]{2,1,0:T(8,128)S(1)} %broadcast_in_dim.65), channel_id=1, replica_groups=mesh['x'=4,'zl'=2,'core'=2,'zh'=4,'y'=8] {'zh','y'}, dimensions={0} | all-to-all | bytes 1835008 | tf_op jit(solution)/shard_map/all_to_all | solution.py:275
  (47 shorter events, 31.8 us)
Async XLA Ops:
  0.8 1.0 copy-start.1
  1.7 0.7 copy-start.2
  2.5 11.3 %copy-start = (f32[1792,128]{1,0:T(8,128)S(1)}, f32[1792,128]{1,0:T(8,128)}, u32[]{:S(2)}) copy-start(f32[1792,128]{1,0:T(8,128)} %param.4) | copy-start | bytes 2752516
  3.5 49.8 %all-to-all-start = ((f32[4,56,640]{2,1,0:T(8,128)}), f32[4,56,640]{2,1,0:T(8,128)S(1)}, u32[]{:S(2)}, u32[]{:S(2)}) async-start(f32[4,56,640]{2,1,0:T(8,128)} %broadcast_in_dim.25), calls=%async_computation | async-start | bytes 1146880 | tf_op jit(solution)/shard_map/all_to_all | solution.py:275
  14.4 3.2 %collective-permute-start = (f32[4,56,128]{2,1,0:T(8,128)S(1)}, f32[4,56,128]{2,1,0:T(8,128)S(1)}, u32[]{:S(2)}, u32[]{:S(2)}) collective-permute-start(f32[4,56,128]{2,1,0:T(8,128)S(1)} %get-tuple-element.17), channel_id=1, source_target_pairs={{0,32},{32,0},{1,33},{33,1},{2,34},{34,2},{3,35},{35,3},{4,36},{36... | collective-permute-start | bytes 344072 | tf_op jit(solution)/shard_map/ppermute | solution.py:296
  64.7 17.6 %all-to-all-start.3 = ((f32[8,56,128]{2,1,0:T(8,128)}), f32[8,56,128]{2,1,0:T(8,128)S(1)}, u32[]{:S(2)}, u32[]{:S(2)}) async-start(f32[8,56,128]{2,1,0:T(8,128)} %direct.3), calls=%async_computation.3 | async-start | bytes 458752 | tf_op jit(solution)/shard_map/all_to_all | solution.py:275
  82.3 10.5 %all-to-all-start.2 = ((f32[8,56,128]{2,1,0:T(8,128)}), f32[8,56,128]{2,1,0:T(8,128)S(1)}, u32[]{:S(2)}, u32[]{:S(2)}) async-start(f32[8,56,128]{2,1,0:T(8,128)} %mirror.3), calls=%async_computation.2 | async-start | bytes 458752 | tf_op jit(solution)/shard_map/all_to_all | solution.py:275
  103.9 13.2 %all-to-all-start.4 = ((f32[8,56,128]{2,1,0:T(8,128)}), f32[8,56,128]{2,1,0:T(8,128)S(1)}, u32[]{:S(2)}, u32[]{:S(2)}) async-start(f32[8,56,128]{2,1,0:T(8,128)} %broadcast_in_dim.33), calls=%async_computation.4 | async-start | bytes 458752 | tf_op jit(solution)/shard_map/all_to_all | solution.py:275
  117.1 13.4 %all-to-all-start.7 = ((f32[8,56,128]{2,1,0:T(8,128)}), f32[8,56,128]{2,1,0:T(8,128)S(1)}, u32[]{:S(2)}, u32[]{:S(2)}) async-start(f32[8,56,128]{2,1,0:T(8,128)} %direct.4), calls=%async_computation.7 | async-start | bytes 458752 | tf_op jit(solution)/shard_map/all_to_all | solution.py:275
  130.5 10.5 %all-to-all-start.5 = ((f32[8,56,128]{2,1,0:T(8,128)}), f32[8,56,128]{2,1,0:T(8,128)S(1)}, u32[]{:S(2)}, u32[]{:S(2)}) async-start(f32[8,56,128]{2,1,0:T(8,128)} %mirror.4), calls=%async_computation.5 | async-start | bytes 458752 | tf_op jit(solution)/shard_map/all_to_all | solution.py:275
  152.2 13.5 %all-to-all-start.8 = ((f32[8,56,128]{2,1,0:T(8,128)}), f32[8,56,128]{2,1,0:T(8,128)S(1)}, u32[]{:S(2)}, u32[]{:S(2)}) async-start(f32[8,56,128]{2,1,0:T(8,128)} %broadcast_in_dim.35), calls=%async_computation.8 | async-start | bytes 458752 | tf_op jit(solution)/shard_map/all_to_all | solution.py:275
  165.6 13.6 %all-to-all-start.11 = ((f32[8,56,128]{2,1,0:T(8,128)}), f32[8,56,128]{2,1,0:T(8,128)S(1)}, u32[]{:S(2)}, u32[]{:S(2)}) async-start(f32[8,56,128]{2,1,0:T(8,128)} %direct.5), calls=%async_computation.11 | async-start | bytes 458752 | tf_op jit(solution)/shard_map/all_to_all | solution.py:275
  179.2 10.5 %all-to-all-start.9 = ((f32[8,56,128]{2,1,0:T(8,128)}), f32[8,56,128]{2,1,0:T(8,128)S(1)}, u32[]{:S(2)}, u32[]{:S(2)}) async-start(f32[8,56,128]{2,1,0:T(8,128)} %mirror.5), calls=%async_computation.9 | async-start | bytes 458752 | tf_op jit(solution)/shard_map/all_to_all | solution.py:275

commit v3 on v2

--- a/solution.py
+++ b/solution.py
@@ -51,7 +51,10 @@
     wide = [
         jnp.concatenate([p, jnp.zeros((ORB, LANES - ORB), f32)], axis=1) for p in pieces
     ]
-    places = jnp.broadcast_to(pos_ref[...], (ORB, LANES))
+    gap = jnp.zeros((1, LANES - 2 * TILES), f32)
+    both = pos_ref[...].astype(f32)
+    places = jnp.concatenate([both[0:1], both[1:2], gap], axis=1)
+    places = jnp.broadcast_to(places, (ORB, LANES))
     for q in range(WIDE // LANES):
         total = jnp.zeros((ORB, LANES), f32)
         for t in range(SLOTS):
@@ -286,8 +289,7 @@
     core = lax.axis_index("core")
     me = jnp.stack([r, y]).astype(jnp.int32)
 
-    places = jnp.pad(tile_pos.reshape(1, 2 * TILES).astype(f32), ((0, 0), (0, LANES - 2 * TILES)))
-    packed = pack(tiles[0, 0], diag_blocks[0], places)
+    packed = pack(tiles[0, 0], diag_blocks[0], tile_pos[0, 0])
     packed = gather(packed, "zh", N_ZH)
 
     sliced = slice_vectors(zh.reshape(1).astype(jnp.int32), vectors.reshape(-1, ORB, LANES))
@@ -296,10 +298,10 @@
     other = lax.ppermute(other, "core", [(0, 1), (1, 0)])
     rows = join_cores(core.reshape(1).astype(jnp.int32), mine, other)
     current = lax.dynamic_index_in_dim(rows, y, 0, keepdims=False)
-    cols = lax.all_gather(current, ROW_AX, axis=0, tiled=False)
-    packed, cols = lax.optimization_barrier((packed, cols))
-
+    packed, rows = lax.optimization_barrier((packed, rows))
     packed = gather(packed.reshape(N_ZH * ORB, WIDE), "core", N_CORE)
+    packed, first = lax.optimization_barrier((packed, current))
+    cols = gather(first, ROW_AX, N_R)
     blocks, where = unpack(packed.reshape(SOURCES, ORB, WIDE))
 
     centre = 0.5 * (filter_high + filter_low)

time: 234 us -> 216 us (0.923)
  the two profiles are of different devices: /device:TPU:8 before, /device:TPU:1 now
where the time goes in v3:
time: 216 us; the launch traced here: 212 us
  blocking collectives  70.7 us (33%)
  waiting for transfers between devices  54.1 us (25%)
  starting transfers between devices  53.8 us (25%)
  Pallas kernels  26.8 us (12%)
  local copies, waits for them, and re-layouts  5.59 us (3%)
    all_to_all x5, blocking collectives, exchange(): return lax.all_to_all(x, axes, split_axis=0, concat_axis=0, tiled=True)  70.7 us
    all_to_all x10, waiting for transfers between devices, exchange(): return lax.all_to_all(x, axes, split_axis=0, concat_axis=0, tiled=True)  53.2 us
    all_to_all x10, starting transfers between devices, exchange(): return lax.all_to_all(x, axes, split_axis=0, concat_axis=0, tiled=True)  50.9 us
    pallas_call x6, Pallas kernels, product(): pl.pallas_call(kernel, out_shape=jax.ShapeDtypeStruct((GROUPS, ORB, LANES...  20.1 us
  transfers between devices with their start and end apart: 11, of which 10 were waited for; matrix products, arithmetic and copies ran while one was open for 0% of the time, Pallas kernels for 11%

profile of v3, /device:TPU:1, one launch (start us, length us, event | category | flops | bytes accessed | tf_op | source)
XLA Modules:
  0.0 211.6 jit_solution(4443857994276923325)
XLA Ops:
  3.4 10.8 %all-to-all-start = ((f32[4,56,640]{2,1,0:T(8,128)}), f32[4,56,640]{2,1,0:T(8,128)S(1)}, u32[]{:S(2)}, u32[]{:S(2)}) async-start(f32[4,56,640]{2,1,0:T(8,128)} %broadcast_in_dim.27), calls=%async_computation | async-start | bytes 1146880 | tf_op jit(solution)/shard_map/all_to_all | solution.py:278
  18.8 8.0 %all-to-all-done = f32[4,56,640]{2,1,0:T(8,128)S(1)} async-done(((f32[4,56,640]{2,1,0:T(8,128)}), f32[4,56,640]{2,1,0:T(8,128)S(1)}, u32[]{:S(2)}, u32[]{:S(2)}) %all-to-all-start) | async-done | bytes 573472 | tf_op jit(solution)/shard_map/all_to_all | solution.py:278
  26.9 7.5 %all_to_all.75 = f32[2,224,640]{2,1,0:T(8,128)S(1)} all-to-all(f32[2,224,640]{2,1,0:T(8,128)S(1)} %broadcast_in_dim.29), channel_id=1, replica_groups=mesh['x'=4,'zl'=2,'core'=2,'zh'=4,'y'=8] {'core'}, dimensions={0} | all-to-all | bytes 2293760 | tf_op jit(solution)/shard_map/all_to_all | solution.py:278
  35.1 7.7 %all-to-all-start.3 = ((f32[8,56,128]{2,1,0:T(8,128)}), f32[8,56,128]{2,1,0:T(8,128)S(1)}, u32[]{:S(2)}, u32[]{:S(2)}) async-start(f32[8,56,128]{2,1,0:T(8,128)} %broadcast_in_dim.30), calls=%async_computation.3 | async-start | bytes 458752 | tf_op jit(solution)/shard_map/all_to_all | solution.py:278
  49.3 5.1 %all-to-all-start.2 = ((f32[8,56,128]{2,1,0:T(8,128)}), f32[8,56,128]{2,1,0:T(8,128)S(1)}, u32[]{:S(2)}, u32[]{:S(2)}) async-start(f32[8,56,128]{2,1,0:T(8,128)} %mirror.3), calls=%async_computation.2 | async-start | bytes 458752 | tf_op jit(solution)/shard_map/all_to_all | solution.py:278
  54.5 3.4 %direct.3 = f32[8,56,128]{2,1,0:T(8,128)} custom-call(s32[8,128]{1,0:T(8,128)S(1)} %get-tuple-element.13.pos_ref, s32[2]{0:T(128)S(1)} %pad_add_fusion.me_ref, f32[8,56,128]{2,1,0:T(8,128)S(1)} %all-to-all-done.3.cols_ref, bf16[88,56,128]{2,1,0:T(8,128)(2,1)S(1)} %get-tuple-element.15.blocks_ref), custom_call_target="tpu_custom_call" | custom-call | flops 200000000 | bytes 4000000 | tf_op jit(solution)/shard_map/direct/pallas_call | solution.py:237
  60.4 6.8 %all-to-all-start.4 = ((f32[8,56,128]{2,1,0:T(8,128)}), f32[8,56,128]{2,1,0:T(8,128)S(1)}, u32[]{:S(2)}, u32[]{:S(2)}) async-start(f32[8,56,128]{2,1,0:T(8,128)} %direct.3), calls=%async_computation.4 | async-start | bytes 458752 | tf_op jit(solution)/shard_map/all_to_all | solution.py:278
  67.3 9.0 %all-to-all-done.4 = f32[8,56,128]{2,1,0:T(8,128)S(1)} async-done(((f32[8,56,128]{2,1,0:T(8,128)}), f32[8,56,128]{2,1,0:T(8,128)S(1)}, u32[]{:S(2)}, u32[]{:S(2)}) %all-to-all-start.4) | async-done | bytes 229408 | tf_op jit(solution)/shard_map/all_to_all | solution.py:278
  77.0 9.3 %all_to_all.76.cols_ref = f32[8,56,128]{2,1,0:T(8,128)S(1)} all-to-all(f32[8,56,128]{2,1,0:T(8,128)} %broadcast_in_dim.36), channel_id=1, replica_groups=mesh['x'=4,'zl'=2,'core'=2,'zh'=4,'y'=8] {'x','zl'}, dimensions={0} | all-to-all | bytes 458752 | tf_op jit(solution)/shard_map/all_to_all | solution.py:278
  86.3 3.4 %all-to-all-start.5 = ((f32[8,56,128]{2,1,0:T(8,128)}), f32[8,56,128]{2,1,0:T(8,128)S(1)}, u32[]{:S(2)}, u32[]{:S(2)}) async-start(f32[8,56,128]{2,1,0:T(8,128)} %broadcast_in_dim.36), calls=%async_computation.5 | async-start | bytes 458752 | tf_op jit(solution)/shard_map/all_to_all | solution.py:278
  89.7 3.4 %direct.4 = f32[8,56,128]{2,1,0:T(8,128)} custom-call(s32[8,128]{1,0:T(8,128)S(1)} %get-tuple-element.13.pos_ref, s32[2]{0:T(128)S(1)} %pad_add_fusion.me_ref, f32[8,56,128]{2,1,0:T(8,128)S(1)} %all_to_all.76.cols_ref, bf16[88,56,128]{2,1,0:T(8,128)(2,1)S(1)} %get-tuple-element.15.blocks_ref), custom_call_target="tpu_custom_call" | custom-call | flops 200000000 | bytes 4000000 | tf_op jit(solution)/shard_map/direct/pallas_call | solution.py:237
  93.2 5.5 %all-to-all-done.5.rows_ref = f32[8,56,128]{2,1,0:T(8,128)S(1)} async-done(((f32[8,56,128]{2,1,0:T(8,128)}), f32[8,56,128]{2,1,0:T(8,128)S(1)}, u32[]{:S(2)}, u32[]{:S(2)}) %all-to-all-start.5) | async-done | bytes 229408 | tf_op jit(solution)/shard_map/all_to_all | solution.py:278
  105.3 5.6 %all-to-all-done.8 = f32[8,56,128]{2,1,0:T(8,128)S(1)} async-done(((f32[8,56,128]{2,1,0:T(8,128)}), f32[8,56,128]{2,1,0:T(8,128)S(1)}, u32[]{:S(2)}, u32[]{:S(2)}) %all-to-all-start.8) | async-done | bytes 229408 | tf_op jit(solution)/shard_map/all_to_all | solution.py:278
  110.9 3.4 %all-to-all-start.6 = ((f32[8,56,128]{2,1,0:T(8,128)}), f32[8,56,128]{2,1,0:T(8,128)S(1)}, u32[]{:S(2)}, u32[]{:S(2)}) async-start(f32[8,56,128]{2,1,0:T(8,128)} %mirror.4), calls=%async_computation.6 | async-start | bytes 458752 | tf_op jit(solution)/shard_map/all_to_all | solution.py:278
  114.4 5.9 %all-to-all-done.6 = f32[8,56,128]{2,1,0:T(8,128)S(1)} async-done(((f32[8,56,128]{2,1,0:T(8,128)}), f32[8,56,128]{2,1,0:T(8,128)S(1)}, u32[]{:S(2)}, u32[]{:S(2)}) %all-to-all-start.6) | async-done | bytes 229408 | tf_op jit(solution)/shard_map/all_to_all | solution.py:278
  121.0 9.3 %all_to_all.77.cols_ref = f32[8,56,128]{2,1,0:T(8,128)S(1)} all-to-all(f32[8,56,128]{2,1,0:T(8,128)} %broadcast_in_dim.38), channel_id=1, replica_groups=mesh['x'=4,'zl'=2,'core'=2,'zh'=4,'y'=8] {'x','zl'}, dimensions={0} | all-to-all | bytes 458752 | tf_op jit(solution)/shard_map/all_to_all | solution.py:278
  130.2 3.4 %all-to-all-start.9 = ((f32[8,56,128]{2,1,0:T(8,128)}), f32[8,56,128]{2,1,0:T(8,128)S(1)}, u32[]{:S(2)}, u32[]{:S(2)}) async-start(f32[8,56,128]{2,1,0:T(8,128)} %broadcast_in_dim.38), calls=%async_computation.9 | async-start | bytes 458752 | tf_op jit(solution)/shard_map/all_to_all | solution.py:278
  133.7 3.4 %direct.5 = f32[8,56,128]{2,1,0:T(8,128)} custom-call(s32[8,128]{1,0:T(8,128)S(1)} %get-tuple-element.13.pos_ref, s32[2]{0:T(128)S(1)} %pad_add_fusion.me_ref, f32[8,56,128]{2,1,0:T(8,128)S(1)} %all_to_all.77.cols_ref, bf16[88,56,128]{2,1,0:T(8,128)(2,1)S(1)} %get-tuple-element.15.blocks_ref), custom_call_target="tpu_custom_call" | custom-call | flops 200000000 | bytes 4000000 | tf_op jit(solution)/shard_map/direct/pallas_call | solution.py:237
  137.1 5.5 %all-to-all-done.9.rows_ref = f32[8,56,128]{2,1,0:T(8,128)S(1)} async-done(((f32[8,56,128]{2,1,0:T(8,128)}), f32[8,56,128]{2,1,0:T(8,128)S(1)}, u32[]{:S(2)}, u32[]{:S(2)}) %all-to-all-start.9) | async-done | bytes 229408 | tf_op jit(solution)/shard_map/all_to_all | solution.py:278
  149.2 5.4 %all-to-all-done.12 = f32[8,56,128]{2,1,0:T(8,128)S(1)} async-done(((f32[8,56,128]{2,1,0:T(8,128)}), f32[8,56,128]{2,1,0:T(8,128)S(1)}, u32[]{:S(2)}, u32[]{:S(2)}) %all-to-all-start.12) | async-done | bytes 229408 | tf_op jit(solution)/shard_map/all_to_all | solution.py:278
  154.6 3.4 %all-to-all-start.10 = ((f32[8,56,128]{2,1,0:T(8,128)}), f32[8,56,128]{2,1,0:T(8,128)S(1)}, u32[]{:S(2)}, u32[]{:S(2)}) async-start(f32[8,56,128]{2,1,0:T(8,128)} %mirror.5), calls=%async_computation.10 | async-start | bytes 458752 | tf_op jit(solution)/shard_map/all_to_all | solution.py:278
  158.1 5.8 %all-to-all-done.10 = f32[8,56,128]{2,1,0:T(8,128)S(1)} async-done(((f32[8,56,128]{2,1,0:T(8,128)}), f32[8,56,128]{2,1,0:T(8,128)S(1)}, u32[]{:S(2)}, u32[]{:S(2)}) %all-to-all-start.10) | async-done | bytes 229408 | tf_op jit(solution)/shard_map/all_to_all | solution.py:278
  164.2 16.7 %all_to_all.78 = f32[2,56,128]{2,1,0:T(8,128)S(1)} all-to-all(f32[2,56,128]{2,1,0:T(8,128)S(1)} %maximum_select_fusion), channel_id=1, replica_groups=mesh['x'=4,'zl'=2,'core'=2,'zh'=4,'y'=8] {'core'}, dimensions={0} | all-to-all | bytes 114688 | tf_op jit(solution)/shard_map/all_to_all | solution.py:278
  181.0 28.0 %all_to_all.79 = f32[32,56,128]{2,1,0:T(8,128)S(1)} all-to-all(f32[32,56,128]{2,1,0:T(8,128)S(1)} %broadcast_in_dim.72), channel_id=1, replica_groups=mesh['x'=4,'zl'=2,'core'=2,'zh'=4,'y'=8] {'zh','y'}, dimensions={0} | all-to-all | bytes 1835008 | tf_op jit(solution)/shard_map/all_to_all | solution.py:278
  (48 shorter events, 35.6 us)
Async XLA Ops:
  0.0 1.0 copy-start.1
  1.0 0.7 copy-start.2
  1.7 0.7 copy-start.3
  2.4 11.8 %copy-start = (f32[1792,128]{1,0:T(8,128)S(1)}, f32[1792,128]{1,0:T(8,128)}, u32[]{:S(2)}) copy-start(f32[1792,128]{1,0:T(8,128)} %param.4) | copy-start | bytes 2752516
  3.4 23.4 %all-to-all-start = ((f32[4,56,640]{2,1,0:T(8,128)}), f32[4,56,640]{2,1,0:T(8,128)S(1)}, u32[]{:S(2)}, u32[]{:S(2)}) async-start(f32[4,56,640]{2,1,0:T(8,128)} %broadcast_in_dim.27), calls=%async_computation | async-start | bytes 1146880 | tf_op jit(solution)/shard_map/all_to_all | solution.py:278
  14.8 3.8 %collective-permute-start = (f32[4,56,128]{2,1,0:T(8,128)S(1)}, f32[4,56,128]{2,1,0:T(8,128)S(1)}, u32[]{:S(2)}, u32[]{:S(2)}) collective-permute-start(f32[4,56,128]{2,1,0:T(8,128)S(1)} %get-tuple-element.21), channel_id=1, source_target_pairs={{0,32},{32,0},{1,33},{33,1},{2,34},{34,2},{3,35},{35,3},{4,36},{36... | collective-permute-start | bytes 344072 | tf_op jit(solution)/shard_map/ppermute | solution.py:298
  35.1 14.2 %all-to-all-start.3 = ((f32[8,56,128]{2,1,0:T(8,128)}), f32[8,56,128]{2,1,0:T(8,128)S(1)}, u32[]{:S(2)}, u32[]{:S(2)}) async-start(f32[8,56,128]{2,1,0:T(8,128)} %broadcast_in_dim.30), calls=%async_computation.3 | async-start | bytes 458752 | tf_op jit(solution)/shard_map/all_to_all | solution.py:278
  49.3 11.1 %all-to-all-start.2 = ((f32[8,56,128]{2,1,0:T(8,128)}), f32[8,56,128]{2,1,0:T(8,128)S(1)}, u32[]{:S(2)}, u32[]{:S(2)}) async-start(f32[8,56,128]{2,1,0:T(8,128)} %mirror.3), calls=%async_computation.2 | async-start | bytes 458752 | tf_op jit(solution)/shard_map/all_to_all | solution.py:278
  60.4 15.9 %all-to-all-start.4 = ((f32[8,56,128]{2,1,0:T(8,128)}), f32[8,56,128]{2,1,0:T(8,128)S(1)}, u32[]{:S(2)}, u32[]{:S(2)}) async-start(f32[8,56,128]{2,1,0:T(8,128)} %direct.3), calls=%async_computation.4 | async-start | bytes 458752 | tf_op jit(solution)/shard_map/all_to_all | solution.py:278
  86.3 12.3 %all-to-all-start.5 = ((f32[8,56,128]{2,1,0:T(8,128)}), f32[8,56,128]{2,1,0:T(8,128)S(1)}, u32[]{:S(2)}, u32[]{:S(2)}) async-start(f32[8,56,128]{2,1,0:T(8,128)} %broadcast_in_dim.36), calls=%async_computation.5 | async-start | bytes 458752 | tf_op jit(solution)/shard_map/all_to_all | solution.py:278
  98.6 12.3 %all-to-all-start.8 = ((f32[8,56,128]{2,1,0:T(8,128)}), f32[8,56,128]{2,1,0:T(8,128)S(1)}, u32[]{:S(2)}, u32[]{:S(2)}) async-start(f32[8,56,128]{2,1,0:T(8,128)} %direct.4), calls=%async_computation.8 | async-start | bytes 458752 | tf_op jit(solution)/shard_map/all_to_all | solution.py:278
  110.9 9.3 %all-to-all-start.6 = ((f32[8,56,128]{2,1,0:T(8,128)}), f32[8,56,128]{2,1,0:T(8,128)S(1)}, u32[]{:S(2)}, u32[]{:S(2)}) async-start(f32[8,56,128]{2,1,0:T(8,128)} %mirror.4), calls=%async_computation.6 | async-start | bytes 458752 | tf_op jit(solution)/shard_map/all_to_all | solution.py:278
  130.2 12.3 %all-to-all-start.9 = ((f32[8,56,128]{2,1,0:T(8,128)}), f32[8,56,128]{2,1,0:T(8,128)S(1)}, u32[]{:S(2)}, u32[]{:S(2)}) async-start(f32[8,56,128]{2,1,0:T(8,128)} %broadcast_in_dim.38), calls=%async_computation.9 | async-start | bytes 458752 | tf_op jit(solution)/shard_map/all_to_all | solution.py:278
  142.6 12.0 %all-to-all-start.12 = ((f32[8,56,128]{2,1,0:T(8,128)}), f32[8,56,128]{2,1,0:T(8,128)S(1)}, u32[]{:S(2)}, u32[]{:S(2)}) async-start(f32[8,56,128]{2,1,0:T(8,128)} %direct.5), calls=%async_computation.12 | async-start | bytes 458752 | tf_op jit(solution)/shard_map/all_to_all | solution.py:278
  154.6 9.3 %all-to-all-start.10 = ((f32[8,56,128]{2,1,0:T(8,128)}), f32[8,56,128]{2,1,0:T(8,128)S(1)}, u32[]{:S(2)}, u32[]{:S(2)}) async-start(f32[8,56,128]{2,1,0:T(8,128)} %mirror.5), calls=%async_computation.10 | async-start | bytes 458752 | tf_op jit(solution)/shard_map/all_to_all | solution.py:278

commit v4 on v3

--- a/solution.py
+++ b/solution.py
@@ -14,12 +14,12 @@
 N_R = N_X * N_ZL
 TILES = 10
 SLOTS = TILES + 1
-SOURCES = N_CORE * N_ZH
+SOURCES = N_CORE * N_Y
 WIDE = 640
-VS = 16
+VS = 8
 PLACE = SLOTS * ORB - (WIDE - LANES)
 ROW_AX = ("x", "zl")
-GROUPS = 8
+GROUPS = N_CORE * N_Y
 
 filter_low = 0.0
 filter_high = 8.0
@@ -121,49 +121,49 @@
     )(packed)
 
 
-def slice_kernel(zh_ref, in_ref, out_ref):
-    lane = lane_iota()
-    start = zh_ref[0] * (2 * VS)
-    for yp in range(N_Y // 2):
+def slice_kernel(y_ref, in_ref, out_ref):
+    lane = lane_iota()
+    start = y_ref[0] * (2 * VS)
+    for zp in range(N_ZH // 2):
         for k in range(N_CORE):
             total = jnp.zeros((ORB, LANES), f32)
             for half in range(2):
-                for z in range(N_ZH):
-                    target = half * 64 + z * VS
-                    x = in_ref[z * N_Y + 2 * yp + half]
+                for y in range(N_Y):
+                    target = half * 64 + y * VS
+                    x = in_ref[(2 * zp + half) * N_Y + y]
                     shift = lax.rem(target - k * VS + LANES - start + LANES, LANES)
                     x = pltpu.roll(x, shift, 1)
                     inside = (lane >= target) & (lane < target + VS)
                     total = jnp.where(inside, x, total)
-            out_ref[k, yp] = total
-
-
-def slice_vectors(zh, blocks):
+            out_ref[k, zp] = total
+
+
+def slice_vectors(y, blocks):
     return pl.pallas_call(
         slice_kernel,
-        out_shape=jax.ShapeDtypeStruct((N_CORE, N_Y // 2, ORB, LANES), f32),
+        out_shape=jax.ShapeDtypeStruct((N_CORE, N_ZH // 2, ORB, LANES), f32),
         in_specs=[pl.BlockSpec(memory_space=pltpu.SMEM)] + vmem(1),
         out_specs=vmem(1)[0],
         compiler_params=params(),
         name="slice_vectors",
-    )(zh, blocks)
+    )(y, blocks)
 
 
 def join_kernel(core_ref, mine_ref, other_ref, out_ref):
     lane = lane_iota()
     is_zero = core_ref[0] == 0
-    for yp in range(N_Y // 2):
-        mine, other = mine_ref[yp], other_ref[yp]
+    for zp in range(N_ZH // 2):
+        mine, other = mine_ref[zp], other_ref[zp]
         a = jnp.where(is_zero, mine, other)
         b = jnp.where(is_zero, other, mine)
-        out_ref[2 * yp] = jnp.where(lane < 64, a, pltpu.roll(b, 64, 1))
-        out_ref[2 * yp + 1] = jnp.where(lane < 64, pltpu.roll(a, 64, 1), b)
+        out_ref[2 * zp] = jnp.where(lane < 64, a, pltpu.roll(b, 64, 1))
+        out_ref[2 * zp + 1] = jnp.where(lane < 64, pltpu.roll(a, 64, 1), b)
 
 
 def join_cores(core, mine, other):
     return pl.pallas_call(
         join_kernel,
-        out_shape=jax.ShapeDtypeStruct((N_Y, ORB, LANES), f32),
+        out_shape=jax.ShapeDtypeStruct((N_ZH, ORB, LANES), f32),
         in_specs=[pl.BlockSpec(memory_space=pltpu.SMEM)] + vmem(2),
         out_specs=vmem(1)[0],
         compiler_params=params(),
@@ -173,20 +173,21 @@
 
 def split_terms(src_ref, dst_ref):
     gap = jnp.zeros((64 - ORB, LANES), f32)
-    for chunk in range(GROUPS):
+    for chunk in range(src_ref.shape[0]):
         x = src_ref[chunk]
         x = jnp.concatenate([x, gap, x, gap], axis=0).T
-        high = x.astype(bf16)
-        low = (x - high.astype(f32)).astype(bf16)
+        high = x.astype(bf16).astype(f32)
+        low = x - high
         for o in range(GROUPS):
-            dst_ref[chunk * GROUPS + o, 0:VS] = high[o * VS : (o + 1) * VS]
-            dst_ref[chunk * GROUPS + o, VS : 2 * VS] = low[o * VS : (o + 1) * VS]
+            rows = slice(o * VS, (o + 1) * VS)
+            both = jnp.concatenate([high[rows], low[rows]], axis=0)
+            dst_ref[chunk * GROUPS + o] = both.astype(bf16)
 
 
 def row_col(pos_ref, s, t):
     i, g = pos_ref[s, PLACE + t], pos_ref[s, PLACE + TILES + t]
-    row = (i & 7) * GROUPS + (s // N_ZH) * N_ZH + (i >> 3)
-    col = (g >> 1) * GROUPS + (g & 1) * N_ZH + s % N_ZH
+    row = (i >> 3) * GROUPS + (s >> 3) * N_Y + (i & 7)
+    col = (g >> 1) * GROUPS + (g & 1) * N_Y + (s & 7)
     return row, col
 
 
@@ -202,7 +203,7 @@
         return carry
 
     lax.fori_loop(0, SOURCES, one_source, 0)
-    for chunk in range(GROUPS):
+    for chunk in range(out_ref.shape[0]):
         x = acc_ref[chunk * GROUPS : (chunk + 1) * GROUPS].reshape(LANES, LANES)
         x = x + pltpu.roll(x, 64, 1)
         out_ref[chunk] = x.T[:ORB]
@@ -211,14 +212,14 @@
 def direct_kernel(pos_ref, me_ref, cols_ref, blocks_ref, out_ref, v_ref, acc_ref):
     split_terms(cols_ref, v_ref)
     acc_ref[...] = jnp.zeros_like(acc_ref)
-    my_r, my_y = me_ref[0], me_ref[1]
+    my_r, my_zh = me_ref[0], me_ref[1]
 
     def one_source(s, carry):
         for t in range(SLOTS):
             if t < TILES:
                 row, col = row_col(pos_ref, s, t)
             else:
-                row, col = my_y * GROUPS + s, my_r * GROUPS + s
+                row, col = my_zh * GROUPS + s, my_r * GROUPS + s
             both = lax.dot_general(
                 v_ref[col], blocks_ref[s * SLOTS + t], (((1,), (1,)), ((), ())),
                 preferred_element_type=f32,
@@ -227,21 +228,21 @@
         return carry
 
     lax.fori_loop(0, SOURCES, one_source, 0)
-    for chunk in range(GROUPS):
+    for chunk in range(out_ref.shape[0]):
         x = acc_ref[chunk * GROUPS : (chunk + 1) * GROUPS].reshape(LANES, LANES)
         out_ref[chunk] = x.T[:ORB]
 
 
-def product(kernel, name, scalars, field, blocks):
+def product(kernel, name, scalars, field, blocks, chunks):
     smem = pl.BlockSpec(memory_space=pltpu.SMEM)
     return pl.pallas_call(
         kernel,
-        out_shape=jax.ShapeDtypeStruct((GROUPS, ORB, LANES), f32),
+        out_shape=jax.ShapeDtypeStruct((chunks, ORB, LANES), f32),
         in_specs=[smem] * len(scalars) + vmem(2),
         out_specs=vmem(1)[0],
         scratch_shapes=[
-            pltpu.VMEM((GROUPS * GROUPS, 2 * VS, LANES), bf16),
-            pltpu.VMEM((GROUPS * GROUPS, VS, LANES), f32),
+            pltpu.VMEM((field.shape[0] * GROUPS, 2 * VS, LANES), bf16),
+            pltpu.VMEM((chunks * GROUPS, VS, LANES), f32),
         ],
         compiler_params=params(),
         cost_estimate=pl.CostEstimate(flops=200000000, bytes_accessed=4000000, transcendentals=0),
@@ -249,18 +250,46 @@
     )(*scalars, field, blocks)
 
 
+def halve_kernel(core_ref, in_ref, out_ref):
+    lane = lane_iota()
+    core = core_ref[0]
+    mine = ((lane >> 3) & 1) == core
+    for z in range(N_ZH):
+        for k in range(N_CORE):
+            x = in_ref[z] if k == 0 else pltpu.roll(in_ref[z], 64, 1)
+            x = jnp.where(lane < 64, x, 0.0)
+            for step in (32, 16, 8):
+                block = lane & (4 * step - 1)
+                moved = pltpu.roll(x, step, 1)
+                x = jnp.where(block < step, x, jnp.where((block >= 2 * step) & (block < 3 * step), moved, 0.0))
+            out_ref[k, z] = jnp.where(mine, pltpu.roll(x, core * VS, 1), 0.0)
+
+
+def halve(core, current):
+    return pl.pallas_call(
+        halve_kernel,
+        out_shape=jax.ShapeDtypeStruct((N_CORE, N_ZH, ORB, LANES), f32),
+        in_specs=[pl.BlockSpec(memory_space=pltpu.SMEM)] + vmem(1),
+        out_specs=vmem(1)[0],
+        compiler_params=params(),
+        name="halve",
+    )(core, current)
+
+
 def spread_kernel(in_ref, out_ref):
     lane = lane_iota()
-    for y in range(N_Y):
-        for z in range(N_ZH):
-            total = jnp.zeros((ORB, LANES), f32)
-            for h in range(N_ZH):
-                for k in range(N_CORE):
-                    target = h * 2 * VS + k * VS
-                    x = roll_to(in_ref[h, y], k * 64 + z * VS, target)
-                    inside = (lane >= target) & (lane < target + VS)
-                    total = jnp.where(inside, x, total)
-            out_ref[z * N_Y + y] = total
+    for z in range(N_ZH):
+        x = [in_ref[y, z] for y in range(N_Y)]
+        for d in (4, 2, 1):
+            upper = (lane & (16 * d)) != 0
+            for a in range(N_Y):
+                if a & d:
+                    continue
+                low, high = x[a], x[a + d]
+                x[a] = jnp.where(upper, pltpu.roll(high, 16 * d, 1), low)
+                x[a + d] = jnp.where(upper, high, pltpu.roll(low, LANES - 16 * d, 1))
+        for y in range(N_Y):
+            out_ref[z * N_Y + y] = x[y]
 
 
 def spread(gathered):
@@ -287,47 +316,44 @@
     y = lax.axis_index("y")
     r = lax.axis_index("x") * N_ZL + lax.axis_index("zl")
     core = lax.axis_index("core")
-    me = jnp.stack([r, y]).astype(jnp.int32)
+    me = jnp.stack([r, zh]).astype(jnp.int32)
 
     packed = pack(tiles[0, 0], diag_blocks[0], tile_pos[0, 0])
-    packed = gather(packed, "zh", N_ZH)
-
-    sliced = slice_vectors(zh.reshape(1).astype(jnp.int32), vectors.reshape(-1, ORB, LANES))
+    packed = gather(packed, "y", N_Y)
+
+    sliced = slice_vectors(y.reshape(1).astype(jnp.int32), vectors.reshape(-1, ORB, LANES))
     mine = lax.dynamic_index_in_dim(sliced, core, 0, keepdims=False)
     other = lax.dynamic_index_in_dim(sliced, 1 - core, 0, keepdims=False)
     other = lax.ppermute(other, "core", [(0, 1), (1, 0)])
-    rows = join_cores(core.reshape(1).astype(jnp.int32), mine, other)
-    current = lax.dynamic_index_in_dim(rows, y, 0, keepdims=False)
-    packed, rows = lax.optimization_barrier((packed, rows))
-    packed = gather(packed.reshape(N_ZH * ORB, WIDE), "core", N_CORE)
-    packed, first = lax.optimization_barrier((packed, current))
-    cols = gather(first, ROW_AX, N_R)
+    core_ref = core.reshape(1).astype(jnp.int32)
+    current = join_cores(core_ref, mine, other)
+
+    own = lax.dynamic_index_in_dim(current, zh, 0, keepdims=False)
+    packed, current, own = lax.optimization_barrier((packed, current, own))
+    packed = gather(packed.reshape(N_Y * ORB, WIDE), "core", N_CORE)
+    packed, own = lax.optimization_barrier((packed, own))
+    cols = gather(own, ROW_AX, N_R)
     blocks, where = unpack(packed.reshape(SOURCES, ORB, WIDE))
 
     centre = 0.5 * (filter_high + filter_low)
     half_width = 0.5 * (filter_high - filter_low)
+    at_own = (lax.broadcasted_iota(jnp.int32, (N_ZH, 1, 1), 0) == zh)
     previous = None
     for step in range(DEGREE):
-        out_cols = product(mirror_kernel, "mirror", (where,), rows, blocks)
+        out_cols = product(mirror_kernel, "mirror", (where,), current, blocks, N_R)
+        out_cols, cols = lax.optimization_barrier((out_cols, cols))
         got_cols = exchange(out_cols, ROW_AX)
-        out_rows = product(direct_kernel, "direct", (where, me), cols, blocks)
-        got_rows = exchange(out_rows, "y")
-        image = jnp.sum(got_cols, 0) + jnp.sum(got_rows, 0)
+        out_rows = product(direct_kernel, "direct", (where, me), cols, blocks, N_ZH)
+        partial = out_rows + jnp.where(at_own, jnp.sum(got_cols, 0)[None], 0.0)
+        image = jnp.sum(gather(partial, "zh", N_ZH).reshape(N_ZH, N_ZH, ORB, LANES), 0)
         shifted = (image - centre * current) / half_width
         following = shifted if previous is None else 2.0 * shifted - previous
         previous, current = current, following
         if step < DEGREE - 1:
-            rows = gather(current, "y", N_Y)
-            cols = gather(current, ROW_AX, N_R)
-
-    lane = lane_iota()
-    swapped = jnp.concatenate([current[:, 64:], current[:, :64]], axis=1)
-    mine = (lane // 64) == core
-    first = jnp.where(core == 0, current, swapped)
-    second = jnp.where(core == 1, current, swapped)
-    halves = jnp.where(mine[None], jnp.stack([first, second]), 0.0)
-    result = jnp.sum(exchange(halves, "core"), 0)
-    result = gather(result, ("zh", "y"), N_ZH * N_Y).reshape(N_ZH, N_Y, ORB, LANES)
+            cols = gather(lax.dynamic_index_in_dim(current, zh, 0, keepdims=False), ROW_AX, N_R)
+
+    result = jnp.sum(exchange(halve(core_ref, current), "core"), 0)
+    result = gather(result, "y", N_Y).reshape(N_Y, N_ZH, ORB, LANES)
     return spread(result).reshape(vectors.shape)
 
 

time: 216 us -> 217 us (level); the launches traced: 212 us -> 216 us
  blocking collectives: 70.7 us -> 96.7 us
  waiting for transfers between devices: 54.1 us -> 31 us
  starting transfers between devices: 53.8 us -> 41.4 us
  Pallas kernels: 26.8 us -> 37.2 us
    all_to_all x5 -> x6, blocking collectives: 70.7 us -> 96.7 us  [exchange(): return lax.all_to_all(x, axes, split_axis=0, concat_axis=0, tiled=True)]
    all_to_all x10 -> x7, waiting for transfers between devices: 53.2 us -> 30.1 us  [exchange(): return lax.all_to_all(x, axes, split_axis=0, concat_axis=0, tiled=True)]
    all_to_all x10 -> x7, starting transfers between devices: 50.9 us -> 36.7 us  [exchange(): return lax.all_to_all(x, axes, split_axis=0, concat_axis=0, tiled=True)]
    pallas_call x8 -> x9, Pallas kernels: 20.7 us -> 28.5 us  [the longest x6 27.4 us: product(): pl.pallas_call(kernel, out_shape=jax.ShapeDtypeStruct((chunks, ORB, LANES...]
    pallas_call x1, Pallas kernels: 3.27 us -> 6.55 us  [unpack(): pl.pallas_call(unpack_kernel, out_shape=(jax.ShapeDtypeStruct((SOURCES *...]
  transfers between devices with their start and end apart: 11 -> 8, of which waited for: 10 -> 7; matrix products, arithmetic and copies ran while one was open for 0% -> 0% of each run, Pallas kernels for 11% -> 16%
where the time goes in v4:
time: 217 us; the launch traced here: 216 us
  blocking collectives  96.7 us (45%)
  starting transfers between devices  41.4 us (19%)
  Pallas kernels  37.2 us (17%)
  waiting for transfers between devices  31 us (14%)
  local copies, waits for them, and re-layouts  7.66 us (4%)
    all_to_all x6, blocking collectives, exchange(): return lax.all_to_all(x, axes, split_axis=0, concat_axis=0, tiled=True)  96.7 us
    all_to_all x7, starting transfers between devices, exchange(): return lax.all_to_all(x, axes, split_axis=0, concat_axis=0, tiled=True)  36.7 us
    all_to_all x7, waiting for transfers between devices, exchange(): return lax.all_to_all(x, axes, split_axis=0, concat_axis=0, tiled=True)  30.1 us
    pallas_call x6, Pallas kernels, product(): pl.pallas_call(kernel, out_shape=jax.ShapeDtypeStruct((chunks, ORB, LANES...  27.4 us
    pallas_call x1, Pallas kernels, unpack(): pl.pallas_call(unpack_kernel, out_shape=(jax.ShapeDtypeStruct((SOURCES *...  6.55 us
    ppermute x1, starting transfers between devices, body(): other = lax.ppermute(other, 'core', [(0, 1), (1, 0)])  4.72 us
  transfers between devices with their start and end apart: 8, of which 7 were waited for; matrix products, arithmetic and copies ran while one was open for 0% of the time, Pallas kernels for 16%

profile of v4, /device:TPU:1, one launch (start us, length us, event | category | flops | bytes accessed | tf_op | source)
XLA Modules:
  0.0 215.6 jit_solution(7147326698017389516)
XLA Ops:
  3.7 7.7 %all-to-all-start = ((f32[8,56,640]{2,1,0:T(8,128)}), f32[8,56,640]{2,1,0:T(8,128)S(1)}, u32[]{:S(2)}, u32[]{:S(2)}) async-start(f32[8,56,640]{2,1,0:T(8,128)} %broadcast_in_dim.100), calls=%async_computation | async-start | bytes 2293760 | tf_op jit(solution)/shard_map/all_to_all | solution.py:307
  11.9 4.7 %collective-permute-start = (f32[2,56,128]{2,1,0:T(8,128)S(1)}, f32[2,56,128]{2,1,0:T(8,128)S(1)}, u32[]{:S(2)}, u32[]{:S(2)}) collective-permute-start(f32[2,56,128]{2,1,0:T(8,128)S(1)} %get-tuple-element.31), channel_id=1, source_target_pairs={{0,32},{32,0},{1,33},{33,1},{2,34},{34,2},{3,35},{35,3},{4,36},{36... | collective-permute-start | bytes 172040 | tf_op jit(solution)/shard_map/ppermute | solution.py:327
  17.6 23.2 %all-to-all-done = f32[8,56,640]{2,1,0:T(8,128)S(1)} async-done(((f32[8,56,640]{2,1,0:T(8,128)}), f32[8,56,640]{2,1,0:T(8,128)S(1)}, u32[]{:S(2)}, u32[]{:S(2)}) %all-to-all-start) | async-done | bytes 1146912 | tf_op jit(solution)/shard_map/all_to_all | solution.py:307
  41.0 8.4 %all_to_all.65 = f32[2,448,640]{2,1,0:T(8,128)} all-to-all(f32[2,448,640]{2,1,0:T(8,128)S(1)} %broadcast_in_dim.102), channel_id=1, replica_groups=mesh['x'=4,'zl'=2,'core'=2,'zh'=4,'y'=8] {'core'}, dimensions={0} | all-to-all | bytes 4587520 | tf_op jit(solution)/shard_map/all_to_all | solution.py:307
  50.1 5.9 %all-to-all-start.2 = ((f32[8,56,128]{2,1,0:T(8,128)}), f32[8,56,128]{2,1,0:T(8,128)S(1)}, u32[]{:S(2)}, u32[]{:S(2)}) async-start(f32[8,56,128]{2,1,0:T(8,128)} %broadcast_in_dim.103), calls=%async_computation.2 | async-start | bytes 458752 | tf_op jit(solution)/shard_map/all_to_all | solution.py:307
  56.0 1.6 copy-done
  57.6 6.6 %unpack.1 = (bf16[176,56,128]{2,1,0:T(8,128)(2,1)S(1)}, s32[16,128]{1,0:T(8,128)S(1)}) custom-call(f32[16,56,640]{2,1,0:T(8,128)S(1)} %bitcast.21), custom_call_target="tpu_custom_call" | custom-call | tf_op jit(solution)/shard_map/unpack/pallas_call | solution.py:111
  64.2 4.6 %mirror.3 = f32[8,56,128]{2,1,0:T(8,128)} custom-call(s32[16,128]{1,0:T(8,128)S(1)} %get-tuple-element.21.pos_ref, f32[4,56,128]{2,1,0:T(8,128)S(1)} %join_cores.1.rows_ref, bf16[176,56,128]{2,1,0:T(8,128)(2,1)S(1)} %get-tuple-element.23.blocks_ref), custom_call_target="tpu_custom_call" | custom-call | flops 200000000 | bytes 4000000 | tf_op jit(solution)/shard_map/mirror/pallas_call | solution.py:238
  68.8 5.1 %all-to-all-start.3 = ((f32[8,56,128]{2,1,0:T(8,128)}), f32[8,56,128]{2,1,0:T(8,128)S(1)}, u32[]{:S(2)}, u32[]{:S(2)}) async-start(f32[8,56,128]{2,1,0:T(8,128)} %mirror.3), calls=%async_computation.3 | async-start | bytes 458752 | tf_op jit(solution)/shard_map/all_to_all | solution.py:307
  74.0 4.5 %direct.3 = f32[4,56,128]{2,1,0:T(8,128)S(1)} custom-call(s32[16,128]{1,0:T(8,128)S(1)} %get-tuple-element.21.pos_ref, s32[2]{0:T(128)S(1)} %pad_add_fusion.me_ref, f32[8,56,128]{2,1,0:T(8,128)S(1)} %all-to-all-done.2.cols_ref, bf16[176,56,128]{2,1,0:T(8,128)(2,1)S(1)} %get-tuple-element.23.blocks_ref), custom_call_target="tpu_custom_call" | custom-call | flops 200000000 | bytes 4000000 | tf_op jit(solution)/shard_map/direct/pallas_call | solution.py:238
  80.1 20.9 %all_to_all.66 = f32[4,4,56,128]{3,2,1,0:T(8,128)S(1)} all-to-all(f32[4,4,56,128]{3,2,1,0:T(8,128)S(1)} %broadcast_in_dim.107), channel_id=1, replica_groups=mesh['x'=4,'zl'=2,'core'=2,'zh'=4,'y'=8] {'zh'}, dimensions={0} | all-to-all | bytes 917504 | tf_op jit(solution)/shard_map/all_to_all | solution.py:307
  101.8 6.1 %all-to-all-start.5 = ((f32[8,56,128]{2,1,0:T(8,128)}), f32[8,56,128]{2,1,0:T(8,128)S(1)}, u32[]{:S(2)}, u32[]{:S(2)}) async-start(f32[8,56,128]{2,1,0:T(8,128)} %broadcast_in_dim.109), calls=%async_computation.5 | async-start | bytes 458752 | tf_op jit(solution)/shard_map/all_to_all | solution.py:307
  107.9 4.6 %mirror.4 = f32[8,56,128]{2,1,0:T(8,128)} custom-call(s32[16,128]{1,0:T(8,128)S(1)} %get-tuple-element.21.pos_ref, f32[4,56,128]{2,1,0:T(8,128)S(1)} %fusion.rows_ref, bf16[176,56,128]{2,1,0:T(8,128)(2,1)S(1)} %get-tuple-element.23.blocks_ref), custom_call_target="tpu_custom_call" | custom-call | flops 200000000 | bytes 4000000 | tf_op jit(solution)/shard_map/mirror/pallas_call | solution.py:238
  113.9 4.0 %all-to-all-start.6 = ((f32[8,56,128]{2,1,0:T(8,128)}), f32[8,56,128]{2,1,0:T(8,128)}, u32[]{:S(2)}, u32[]{:S(2)}) async-start(f32[8,56,128]{2,1,0:T(8,128)} %mirror.4), calls=%async_computation.6 | async-start | bytes 458752 | tf_op jit(solution)/shard_map/all_to_all | solution.py:307
  117.9 4.5 %direct.4 = f32[4,56,128]{2,1,0:T(8,128)S(1)} custom-call(s32[16,128]{1,0:T(8,128)S(1)} %get-tuple-element.21.pos_ref, s32[2]{0:T(128)S(1)} %pad_add_fusion.me_ref, f32[8,56,128]{2,1,0:T(8,128)S(1)} %all-to-all-done.5.cols_ref, bf16[176,56,128]{2,1,0:T(8,128)(2,1)S(1)} %get-tuple-element.23.blocks_ref), custom_call_target="tpu_custom_call" | custom-call | flops 200000000 | bytes 4000000 | tf_op jit(solution)/shard_map/direct/pallas_call | solution.py:238
  124.9 13.5 %all_to_all.67 = f32[4,4,56,128]{3,2,1,0:T(8,128)S(1)} all-to-all(f32[4,4,56,128]{3,2,1,0:T(8,128)S(1)} %broadcast_in_dim.111), channel_id=1, replica_groups=mesh['x'=4,'zl'=2,'core'=2,'zh'=4,'y'=8] {'zh'}, dimensions={0} | all-to-all | bytes 917504 | tf_op jit(solution)/shard_map/all_to_all | solution.py:307
  139.2 4.1 %all-to-all-start.8 = ((f32[8,56,128]{2,1,0:T(8,128)}), f32[8,56,128]{2,1,0:T(8,128)S(1)}, u32[]{:S(2)}, u32[]{:S(2)}) async-start(f32[8,56,128]{2,1,0:T(8,128)} %broadcast_in_dim.113), calls=%async_computation.8 | async-start | bytes 458752 | tf_op jit(solution)/shard_map/all_to_all | solution.py:307
  143.3 4.6 %mirror.5 = f32[8,56,128]{2,1,0:T(8,128)} custom-call(s32[16,128]{1,0:T(8,128)S(1)} %get-tuple-element.21.pos_ref, f32[4,56,128]{2,1,0:T(8,128)S(1)} %multiply_subtract_fusion.1.rows_ref, bf16[176,56,128]{2,1,0:T(8,128)(2,1)S(1)} %get-tuple-element.23.blocks_ref), custom_call_target="tpu_custom_call" | custom-call | flops 200000000 | bytes 4000000 | tf_op jit(solution)/shard_map/mirror/pallas_call | solution.py:238
  149.2 3.8 %all-to-all-start.9 = ((f32[8,56,128]{2,1,0:T(8,128)}), f32[8,56,128]{2,1,0:T(8,128)S(1)}, u32[]{:S(2)}, u32[]{:S(2)}) async-start(f32[8,56,128]{2,1,0:T(8,128)} %mirror.5), calls=%async_computation.9 | async-start | bytes 458752 | tf_op jit(solution)/shard_map/all_to_all | solution.py:307
  153.1 4.5 %direct.5 = f32[4,56,128]{2,1,0:T(8,128)S(1)} custom-call(s32[16,128]{1,0:T(8,128)S(1)} %get-tuple-element.21.pos_ref, s32[2]{0:T(128)S(1)} %pad_add_fusion.me_ref, f32[8,56,128]{2,1,0:T(8,128)S(1)} %all-to-all-done.8.cols_ref, bf16[176,56,128]{2,1,0:T(8,128)(2,1)S(1)} %get-tuple-element.23.blocks_ref), custom_call_target="tpu_custom_call" | custom-call | flops 200000000 | bytes 4000000 | tf_op jit(solution)/shard_map/direct/pallas_call | solution.py:238
  159.2 14.2 %all_to_all.68 = f32[4,4,56,128]{3,2,1,0:T(8,128)S(1)} all-to-all(f32[4,4,56,128]{3,2,1,0:T(8,128)S(1)} %broadcast_in_dim.115), channel_id=1, replica_groups=mesh['x'=4,'zl'=2,'core'=2,'zh'=4,'y'=8] {'zh'}, dimensions={0} | all-to-all | bytes 917504 | tf_op jit(solution)/shard_map/all_to_all | solution.py:307
  173.9 10.8 %all_to_all.69 = f32[2,4,56,128]{3,2,1,0:T(8,128)S(1)} all-to-all(f32[2,4,56,128]{3,2,1,0:T(8,128)S(1)} %halve.1), channel_id=1, replica_groups=mesh['x'=4,'zl'=2,'core'=2,'zh'=4,'y'=8] {'core'}, dimensions={0} | all-to-all | bytes 458752 | tf_op jit(solution)/shard_map/all_to_all | solution.py:307
  184.8 28.8 %all_to_all.70.in_ref = f32[8,4,56,128]{3,2,1,0:T(8,128)S(1)} all-to-all(f32[8,4,56,128]{3,2,1,0:T(8,128)S(1)} %broadcast_in_dim.116), channel_id=1, replica_groups=mesh['x'=4,'zl'=2,'core'=2,'zh'=4,'y'=8] {'y'}, dimensions={0} | all-to-all | bytes 1835008 | tf_op jit(solution)/shard_map/all_to_all | solution.py:307
  213.6 1.9 spread.1
  (48 shorter events, 16.6 us)
Async XLA Ops:
  0.0 11.3 %copy-start.1 = (f32[1792,128]{1,0:T(8,128)S(1)}, f32[1792,128]{1,0:T(8,128)}, u32[]{:S(2)}) copy-start(f32[1792,128]{1,0:T(8,128)} %param.4) | copy-start | bytes 2752516
  0.0 1.0 copy-start.2
  1.0 0.7 copy-start.3
  1.8 0.7 copy-start.4
  3.7 37.1 %all-to-all-start = ((f32[8,56,640]{2,1,0:T(8,128)}), f32[8,56,640]{2,1,0:T(8,128)S(1)}, u32[]{:S(2)}, u32[]{:S(2)}) async-start(f32[8,56,640]{2,1,0:T(8,128)} %broadcast_in_dim.100), calls=%async_computation | async-start | bytes 2293760 | tf_op jit(solution)/shard_map/all_to_all | solution.py:307
  11.9 5.6 %collective-permute-start = (f32[2,56,128]{2,1,0:T(8,128)S(1)}, f32[2,56,128]{2,1,0:T(8,128)S(1)}, u32[]{:S(2)}, u32[]{:S(2)}) collective-permute-start(f32[2,56,128]{2,1,0:T(8,128)S(1)} %get-tuple-element.31), channel_id=1, source_target_pairs={{0,32},{32,0},{1,33},{33,1},{2,34},{34,2},{3,35},{35,3},{4,36},{36... | collective-permute-start | bytes 172040 | tf_op jit(solution)/shard_map/ppermute | solution.py:327
  50.1 18.7 %all-to-all-start.2 = ((f32[8,56,128]{2,1,0:T(8,128)}), f32[8,56,128]{2,1,0:T(8,128)S(1)}, u32[]{:S(2)}, u32[]{:S(2)}) async-start(f32[8,56,128]{2,1,0:T(8,128)} %broadcast_in_dim.103), calls=%async_computation.2 | async-start | bytes 458752 | tf_op jit(solution)/shard_map/all_to_all | solution.py:307
  55.9 1.6 copy-start
  68.8 11.1 %all-to-all-start.3 = ((f32[8,56,128]{2,1,0:T(8,128)}), f32[8,56,128]{2,1,0:T(8,128)S(1)}, u32[]{:S(2)}, u32[]{:S(2)}) async-start(f32[8,56,128]{2,1,0:T(8,128)} %mirror.3), calls=%async_computation.3 | async-start | bytes 458752 | tf_op jit(solution)/shard_map/all_to_all | solution.py:307
  101.8 12.1 %all-to-all-start.5 = ((f32[8,56,128]{2,1,0:T(8,128)}), f32[8,56,128]{2,1,0:T(8,128)S(1)}, u32[]{:S(2)}, u32[]{:S(2)}) async-start(f32[8,56,128]{2,1,0:T(8,128)} %broadcast_in_dim.109), calls=%async_computation.5 | async-start | bytes 458752 | tf_op jit(solution)/shard_map/all_to_all | solution.py:307
  113.9 10.0 %all-to-all-start.6 = ((f32[8,56,128]{2,1,0:T(8,128)}), f32[8,56,128]{2,1,0:T(8,128)}, u32[]{:S(2)}, u32[]{:S(2)}) async-start(f32[8,56,128]{2,1,0:T(8,128)} %mirror.4), calls=%async_computation.6 | async-start | bytes 458752 | tf_op jit(solution)/shard_map/all_to_all | solution.py:307
  139.2 10.0 %all-to-all-start.8 = ((f32[8,56,128]{2,1,0:T(8,128)}), f32[8,56,128]{2,1,0:T(8,128)S(1)}, u32[]{:S(2)}, u32[]{:S(2)}) async-start(f32[8,56,128]{2,1,0:T(8,128)} %broadcast_in_dim.113), calls=%async_computation.8 | async-start | bytes 458752 | tf_op jit(solution)/shard_map/all_to_all | solution.py:307
  149.2 9.8 %all-to-all-start.9 = ((f32[8,56,128]{2,1,0:T(8,128)}), f32[8,56,128]{2,1,0:T(8,128)S(1)}, u32[]{:S(2)}, u32[]{:S(2)}) async-start(f32[8,56,128]{2,1,0:T(8,128)} %mirror.5), calls=%async_computation.9 | async-start | bytes 458752 | tf_op jit(solution)/shard_map/all_to_all | solution.py:307

commit v5 on v4

--- a/solution.py
+++ b/solution.py
@@ -14,7 +14,6 @@
 N_R = N_X * N_ZL
 TILES = 10
 SLOTS = TILES + 1
-SOURCES = N_CORE * N_Y
 WIDE = 640
 VS = 8
 PLACE = SLOTS * ORB - (WIDE - LANES)
@@ -100,8 +99,8 @@
             blocks_ref[s * SLOTS + t] = two_terms(jnp.where(lane < ORB, x, 0.0))
         return carry
 
-    lax.fori_loop(0, SOURCES, one_source, 0)
-    for s in range(SOURCES):
+    lax.fori_loop(0, N_Y, one_source, 0)
+    for s in range(N_Y):
         last = in_ref[s, 0:1, WIDE - LANES : WIDE]
         shown = lax.broadcasted_iota(jnp.int32, (1, LANES), 1) >= PLACE
         places_ref[s : s + 1] = jnp.where(shown, last, 0.0).astype(jnp.int32)
@@ -111,8 +110,8 @@
     return pl.pallas_call(
         unpack_kernel,
         out_shape=(
-            jax.ShapeDtypeStruct((SOURCES * SLOTS, ORB, LANES), bf16),
-            jax.ShapeDtypeStruct((SOURCES, LANES), jnp.int32),
+            jax.ShapeDtypeStruct((N_Y * SLOTS, ORB, LANES), bf16),
+            jax.ShapeDtypeStruct((N_Y, LANES), jnp.int32),
         ),
         in_specs=vmem(1),
         out_specs=tuple(vmem(2)),
@@ -121,37 +120,47 @@
     )(packed)
 
 
-def slice_kernel(y_ref, in_ref, out_ref):
-    lane = lane_iota()
-    start = y_ref[0] * (2 * VS)
-    for zp in range(N_ZH // 2):
-        for k in range(N_CORE):
+def slice_kernel(me_ref, in_ref, mine_ref, other_ref, own_ref):
+    lane = lane_iota()
+    zh, core, start = me_ref[1], me_ref[2], me_ref[3] * (2 * VS)
+
+    def placed(block, k, target):
+        shift = lax.rem(target - k * VS + 2 * LANES - start, LANES)
+        return pltpu.roll(in_ref[block], shift, 1)
+
+    for out_ref, k in ((mine_ref, core), (other_ref, 1 - core)):
+        for zp in range(N_ZH // 2):
             total = jnp.zeros((ORB, LANES), f32)
             for half in range(2):
                 for y in range(N_Y):
                     target = half * 64 + y * VS
-                    x = in_ref[(2 * zp + half) * N_Y + y]
-                    shift = lax.rem(target - k * VS + LANES - start + LANES, LANES)
-                    x = pltpu.roll(x, shift, 1)
                     inside = (lane >= target) & (lane < target + VS)
-                    total = jnp.where(inside, x, total)
-            out_ref[k, zp] = total
-
-
-def slice_vectors(y, blocks):
+                    total = jnp.where(inside, placed((2 * zp + half) * N_Y + y, k, target), total)
+            out_ref[zp] = total
+    total = jnp.zeros((ORB, LANES), f32)
+    for k in range(N_CORE):
+        for y in range(N_Y):
+            target = k * 64 + y * VS
+            inside = (lane >= target) & (lane < target + VS)
+            total = jnp.where(inside, placed(zh * N_Y + y, k, target), total)
+    own_ref[...] = total
+
+
+def slice_vectors(me, blocks):
+    pair = jax.ShapeDtypeStruct((N_ZH // 2, ORB, LANES), f32)
     return pl.pallas_call(
         slice_kernel,
-        out_shape=jax.ShapeDtypeStruct((N_CORE, N_ZH // 2, ORB, LANES), f32),
+        out_shape=(pair, pair, jax.ShapeDtypeStruct((ORB, LANES), f32)),
         in_specs=[pl.BlockSpec(memory_space=pltpu.SMEM)] + vmem(1),
-        out_specs=vmem(1)[0],
+        out_specs=tuple(vmem(3)),
         compiler_params=params(),
         name="slice_vectors",
-    )(y, blocks)
-
-
-def join_kernel(core_ref, mine_ref, other_ref, out_ref):
-    lane = lane_iota()
-    is_zero = core_ref[0] == 0
+    )(me, blocks)
+
+
+def join_kernel(me_ref, mine_ref, other_ref, out_ref):
+    lane = lane_iota()
+    is_zero = me_ref[2] == 0
     for zp in range(N_ZH // 2):
         mine, other = mine_ref[zp], other_ref[zp]
         a = jnp.where(is_zero, mine, other)
@@ -160,7 +169,7 @@
         out_ref[2 * zp + 1] = jnp.where(lane < 64, pltpu.roll(a, 64, 1), b)
 
 
-def join_cores(core, mine, other):
+def join_cores(me, mine, other):
     return pl.pallas_call(
         join_kernel,
         out_shape=jax.ShapeDtypeStruct((N_ZH, ORB, LANES), f32),
@@ -168,7 +177,28 @@
         out_specs=vmem(1)[0],
         compiler_params=params(),
         name="join_cores",
-    )(core, mine, other)
+    )(me, mine, other)
+
+
+def pick_kernel(me_ref, in_ref, out_ref):
+    lane = lane_iota()
+    is_zero = me_ref[2] == 0
+    for r in range(N_R):
+        a, b = in_ref[2 * r], in_ref[2 * r + 1]
+        first = jnp.where(is_zero, a, pltpu.roll(a, 64, 1))
+        second = jnp.where(is_zero, pltpu.roll(b, 64, 1), b)
+        out_ref[r] = jnp.where(lane < 64, first, second)
+
+
+def pick_half(me, gathered):
+    return pl.pallas_call(
+        pick_kernel,
+        out_shape=jax.ShapeDtypeStruct((N_R, ORB, LANES), f32),
+        in_specs=[pl.BlockSpec(memory_space=pltpu.SMEM)] + vmem(1),
+        out_specs=vmem(1)[0],
+        compiler_params=params(),
+        name="pick_half",
+    )(me, gathered)
 
 
 def split_terms(src_ref, dst_ref):
@@ -184,50 +214,54 @@
             dst_ref[chunk * GROUPS + o] = both.astype(bf16)
 
 
-def row_col(pos_ref, s, t):
+def row_col(pos_ref, core_s, s, t):
     i, g = pos_ref[s, PLACE + t], pos_ref[s, PLACE + TILES + t]
-    row = (i >> 3) * GROUPS + (s >> 3) * N_Y + (i & 7)
-    col = (g >> 1) * GROUPS + (g & 1) * N_Y + (s & 7)
+    row = (i >> 3) * GROUPS + core_s * N_Y + (i & 7)
+    col = (g >> 1) * GROUPS + (g & 1) * N_Y + s
     return row, col
 
 
-def mirror_kernel(pos_ref, rows_ref, blocks_ref, out_ref, v_ref, acc_ref):
+def mirror_kernel(me_ref, pos_a_ref, pos_b_ref, rows_ref, blocks_a_ref, blocks_b_ref, out_ref, v_ref, acc_ref):
     split_terms(rows_ref, v_ref)
     acc_ref[...] = jnp.zeros_like(acc_ref)
-
-    def one_source(s, carry):
-        for t in range(TILES):
-            row, col = row_col(pos_ref, s, t)
-            both = jnp.dot(v_ref[row][:, :ORB], blocks_ref[s * SLOTS + t], preferred_element_type=f32)
-            acc_ref[col] += both[:VS] + both[VS:]
-        return carry
-
-    lax.fori_loop(0, SOURCES, one_source, 0)
+    core = me_ref[2]
+    for pos_ref, blocks_ref, core_s in ((pos_a_ref, blocks_a_ref, core), (pos_b_ref, blocks_b_ref, 1 - core)):
+
+        def one_source(s, carry, pos_ref=pos_ref, blocks_ref=blocks_ref, core_s=core_s):
+            for t in range(TILES):
+                row, col = row_col(pos_ref, core_s, s, t)
+                both = jnp.dot(v_ref[row][:, :ORB], blocks_ref[s * SLOTS + t], preferred_element_type=f32)
+                acc_ref[col] += both[:VS] + both[VS:]
+            return carry
+
+        lax.fori_loop(0, N_Y, one_source, 0)
     for chunk in range(out_ref.shape[0]):
         x = acc_ref[chunk * GROUPS : (chunk + 1) * GROUPS].reshape(LANES, LANES)
         x = x + pltpu.roll(x, 64, 1)
         out_ref[chunk] = x.T[:ORB]
 
 
-def direct_kernel(pos_ref, me_ref, cols_ref, blocks_ref, out_ref, v_ref, acc_ref):
+def direct_kernel(me_ref, pos_a_ref, pos_b_ref, cols_ref, blocks_a_ref, blocks_b_ref, out_ref, v_ref, acc_ref):
     split_terms(cols_ref, v_ref)
     acc_ref[...] = jnp.zeros_like(acc_ref)
-    my_r, my_zh = me_ref[0], me_ref[1]
-
-    def one_source(s, carry):
-        for t in range(SLOTS):
-            if t < TILES:
-                row, col = row_col(pos_ref, s, t)
-            else:
-                row, col = my_zh * GROUPS + s, my_r * GROUPS + s
-            both = lax.dot_general(
-                v_ref[col], blocks_ref[s * SLOTS + t], (((1,), (1,)), ((), ())),
-                preferred_element_type=f32,
-            )
-            acc_ref[row, :, 0:ORB] += both[:VS] + both[VS:]
-        return carry
-
-    lax.fori_loop(0, SOURCES, one_source, 0)
+    my_r, my_zh, core = me_ref[0], me_ref[1], me_ref[2]
+    for pos_ref, blocks_ref, core_s in ((pos_a_ref, blocks_a_ref, core), (pos_b_ref, blocks_b_ref, 1 - core)):
+
+        def one_source(s, carry, pos_ref=pos_ref, blocks_ref=blocks_ref, core_s=core_s):
+            for t in range(SLOTS):
+                if t < TILES:
+                    row, col = row_col(pos_ref, core_s, s, t)
+                else:
+                    row = my_zh * GROUPS + core_s * N_Y + s
+                    col = my_r * GROUPS + core_s * N_Y + s
+                both = lax.dot_general(
+                    v_ref[col], blocks_ref[s * SLOTS + t], (((1,), (1,)), ((), ())),
+                    preferred_element_type=f32,
+                )
+                acc_ref[row, :, 0:ORB] += both[:VS] + both[VS:]
+            return carry
+
+        lax.fori_loop(0, N_Y, one_source, 0)
     for chunk in range(out_ref.shape[0]):
         x = acc_ref[chunk * GROUPS : (chunk + 1) * GROUPS].reshape(LANES, LANES)
         out_ref[chunk] = x.T[:ORB]
@@ -238,7 +272,7 @@
     return pl.pallas_call(
         kernel,
         out_shape=jax.ShapeDtypeStruct((chunks, ORB, LANES), f32),
-        in_specs=[smem] * len(scalars) + vmem(2),
+        in_specs=[smem] * len(scalars) + vmem(1 + len(blocks)),
         out_specs=vmem(1)[0],
         scratch_shapes=[
             pltpu.VMEM((field.shape[0] * GROUPS, 2 * VS, LANES), bf16),
@@ -247,12 +281,12 @@
         compiler_params=params(),
         cost_estimate=pl.CostEstimate(flops=200000000, bytes_accessed=4000000, transcendentals=0),
         name=name,
-    )(*scalars, field, blocks)
-
-
-def halve_kernel(core_ref, in_ref, out_ref):
-    lane = lane_iota()
-    core = core_ref[0]
+    )(*scalars, field, *blocks)
+
+
+def halve_kernel(me_ref, in_ref, out_ref):
+    lane = lane_iota()
+    core = me_ref[2]
     mine = ((lane >> 3) & 1) == core
     for z in range(N_ZH):
         for k in range(N_CORE):
@@ -265,7 +299,7 @@
             out_ref[k, z] = jnp.where(mine, pltpu.roll(x, core * VS, 1), 0.0)
 
 
-def halve(core, current):
+def halve(me, current):
     return pl.pallas_call(
         halve_kernel,
         out_shape=jax.ShapeDtypeStruct((N_CORE, N_ZH, ORB, LANES), f32),
@@ -273,7 +307,7 @@
         out_specs=vmem(1)[0],
         compiler_params=params(),
         name="halve",
-    )(core, current)
+    )(me, current)
 
 
 def spread_kernel(in_ref, out_ref):
@@ -313,37 +347,31 @@
 
 def body(vectors, tiles, tile_pos, diag_blocks):
     zh = lax.axis_index("zh")
-    y = lax.axis_index("y")
     r = lax.axis_index("x") * N_ZL + lax.axis_index("zl")
-    core = lax.axis_index("core")
-    me = jnp.stack([r, zh]).astype(jnp.int32)
+    me = jnp.stack([r, zh, lax.axis_index("core"), lax.axis_index("y")]).astype(jnp.int32)
+    swap = [(0, 1), (1, 0)]
 
     packed = pack(tiles[0, 0], diag_blocks[0], tile_pos[0, 0])
     packed = gather(packed, "y", N_Y)
 
-    sliced = slice_vectors(y.reshape(1).astype(jnp.int32), vectors.reshape(-1, ORB, LANES))
-    mine = lax.dynamic_index_in_dim(sliced, core, 0, keepdims=False)
-    other = lax.dynamic_index_in_dim(sliced, 1 - core, 0, keepdims=False)
-    other = lax.ppermute(other, "core", [(0, 1), (1, 0)])
-    core_ref = core.reshape(1).astype(jnp.int32)
-    current = join_cores(core_ref, mine, other)
-
-    own = lax.dynamic_index_in_dim(current, zh, 0, keepdims=False)
-    packed, current, own = lax.optimization_barrier((packed, current, own))
-    packed = gather(packed.reshape(N_Y * ORB, WIDE), "core", N_CORE)
-    packed, own = lax.optimization_barrier((packed, own))
-    cols = gather(own, ROW_AX, N_R)
-    blocks, where = unpack(packed.reshape(SOURCES, ORB, WIDE))
+    mine, other, own = slice_vectors(me, vectors.reshape(-1, ORB, LANES))
+    cols = pick_half(me, lax.all_gather(own, ("x", "zl", "core"), axis=0, tiled=False))
+    current = join_cores(me, mine, lax.ppermute(other, "core", swap))
+
+    packed, current, cols = lax.optimization_barrier((packed, current, cols))
+    blocks_a, pos_a = unpack(packed)
+    blocks_b, pos_b = unpack(lax.ppermute(packed, "core", swap))
+    where, blocks = (me, pos_a, pos_b), (blocks_a, blocks_b)
 
     centre = 0.5 * (filter_high + filter_low)
     half_width = 0.5 * (filter_high - filter_low)
     at_own = (lax.broadcasted_iota(jnp.int32, (N_ZH, 1, 1), 0) == zh)
     previous = None
     for step in range(DEGREE):
-        out_cols = product(mirror_kernel, "mirror", (where,), current, blocks, N_R)
+        out_cols = product(mirror_kernel, "mirror", where, current, blocks, N_R)
         out_cols, cols = lax.optimization_barrier((out_cols, cols))
         got_cols = exchange(out_cols, ROW_AX)
-        out_rows = product(direct_kernel, "direct", (where, me), cols, blocks, N_ZH)
+        out_rows = product(direct_kernel, "direct", where, cols, blocks, N_ZH)
         partial = out_rows + jnp.where(at_own, jnp.sum(got_cols, 0)[None], 0.0)
         image = jnp.sum(gather(partial, "zh", N_ZH).reshape(N_ZH, N_ZH, ORB, LANES), 0)
         shifted = (image - centre * current) / half_width
@@ -352,7 +380,7 @@
         if step < DEGREE - 1:
             cols = gather(lax.dynamic_index_in_dim(current, zh, 0, keepdims=False), ROW_AX, N_R)
 
-    result = jnp.sum(exchange(halve(core_ref, current), "core"), 0)
+    result = jnp.sum(exchange(halve(me, current), "core"), 0)
     result = gather(result, "y", N_Y).reshape(N_Y, N_ZH, ORB, LANES)
     return spread(result).reshape(vectors.shape)
 

time: 217 us -> 208 us (0.959)
  blocking collectives: 96.7 us -> 86.3 us
  starting transfers between devices: 41.4 us -> 51.4 us
  waiting for transfers between devices: 31 us -> 21.6 us
  Pallas kernels: 37.2 us -> 39.7 us
    all_to_all x6 -> x4, blocking collectives: 96.7 us -> 65.8 us  [exchange(): return lax.all_to_all(x, axes, split_axis=0, concat_axis=0, tiled=True)]
    all_gather x0 -> x1, blocking collectives: none -> 20.5 us  [body(): lax.all_gather(own, ('x', 'zl', 'core'), axis=0, tiled=False)]
    all_to_all x7, waiting for transfers between devices: 30.1 us -> 21.6 us  [exchange(): return lax.all_to_all(x, axes, split_axis=0, concat_axis=0, tiled=True)]
    all_to_all x7, starting transfers between devices: 36.7 us -> 42.5 us  [exchange(): return lax.all_to_all(x, axes, split_axis=0, concat_axis=0, tiled=True)]
    ppermute x1 -> x2, starting transfers between devices: 4.72 us -> 8.94 us  [the longest x1 4.72 us: body(): current = join_cores(me, mine, lax.ppermute(other, 'core', swap))]
    pallas_call x2 -> x4, Pallas kernels: 7.09 us -> 8.47 us  [the longest x2 6.55 us: unpack(): pl.pallas_call(unpack_kernel, out_shape=(jax.ShapeDtypeStruct((N_Y * SLOT...]
  transfers between devices with their start and end apart: 8 -> 9, of which waited for: 7 -> 7; matrix products, arithmetic and copies ran while one was open for 0% -> 0% of each run, Pallas kernels for 16% -> 14%
where the time goes in v5:
time: 208 us; the launch traced here: 206 us
  blocking collectives  86.3 us (41%)
  starting transfers between devices  51.4 us (25%)
  Pallas kernels  39.7 us (19%)
  waiting for transfers between devices  21.6 us (10%)
  local copies, waits for them, and re-layouts  5.82 us (3%)
    all_to_all x4, blocking collectives, exchange(): return lax.all_to_all(x, axes, split_axis=0, concat_axis=0, tiled=True)  65.8 us
    all_to_all x7, starting transfers between devices, exchange(): return lax.all_to_all(x, axes, split_axis=0, concat_axis=0, tiled=True)  42.5 us
    pallas_call x6, Pallas kernels, product(): pl.pallas_call(kernel, out_shape=jax.ShapeDtypeStruct((chunks, ORB, LANES...  27.5 us
    all_to_all x7, waiting for transfers between devices, exchange(): return lax.all_to_all(x, axes, split_axis=0, concat_axis=0, tiled=True)  21.6 us
    all_gather x1, blocking collectives, body(): lax.all_gather(own, ('x', 'zl', 'core'), axis=0, tiled=False)  20.5 us
    pallas_call x2, Pallas kernels, unpack(): pl.pallas_call(unpack_kernel, out_shape=(jax.ShapeDtypeStruct((N_Y * SLOT...  6.55 us
    ppermute x1, starting transfers between devices, body(): current = join_cores(me, mine, lax.ppermute(other, 'core', swap))  4.72 us
    ppermute x1, starting transfers between devices, body(): blocks_b, pos_b = unpack(lax.ppermute(packed, 'core', swap))  4.23 us
  transfers between devices with their start and end apart: 9, of which 7 were waited for; matrix products, arithmetic and copies ran while one was open for 0% of the time, Pallas kernels for 14%

profile of v5, /device:TPU:1, one launch (start us, length us, event | category | flops | bytes accessed | tf_op | source)
XLA Modules:
  0.0 206.5 jit_solution(5740359412628378293)
XLA Ops:
  3.6 7.8 %all-to-all-start = ((f32[8,56,640]{2,1,0:T(8,128)}), f32[8,56,640]{2,1,0:T(8,128)S(1)}, u32[]{:S(2)}, u32[]{:S(2)}) async-start(f32[8,56,640]{2,1,0:T(8,128)} %broadcast_in_dim.87), calls=%async_computation | async-start | bytes 2293760 | tf_op jit(solution)/shard_map/all_to_all | solution.py:341
  12.7 4.7 %collective-permute-start = (f32[2,56,128]{2,1,0:T(8,128)S(1)}, f32[2,56,128]{2,1,0:T(8,128)S(1)}, u32[]{:S(2)}, u32[]{:S(2)}) collective-permute-start(f32[2,56,128]{2,1,0:T(8,128)S(1)} %get-tuple-element.22), channel_id=1, source_target_pairs={{0,32},{32,0},{1,33},{33,1},{2,34},{34,2},{3,35},{35,3},{4,36},{36... | collective-permute-start | bytes 172040 | tf_op jit(solution)/shard_map/ppermute | solution.py:359
  17.4 20.5 %all-gather = f32[896,128]{1,0:T(8,128)S(1)} all-gather(f32[56,128]{1,0:T(8,128)S(1)} %get-tuple-element.23), channel_id=2, replica_groups=mesh['x'=4,'zl'=2,'core'=2,'zh'=4,'y'=8] {'x','zl','core'}, dimensions={0}, use_global_device_ids=true | all-gather | bytes 487424 | tf_op jit(solution)/shard_map/all_gather | solution.py:358
  40.9 4.2 %collective-permute-start.1 = (f32[8,56,640]{2,1,0:T(8,128)S(1)}, f32[8,56,640]{2,1,0:T(8,128)S(1)}, u32[]{:S(2)}, u32[]{:S(2)}) collective-permute-start(f32[8,56,640]{2,1,0:T(8,128)S(1)} %all-to-all-done.in_ref), channel_id=1, source_target_pairs={{0,32},{32,0},{1,33},{33,1},{2,34},{34,2},{3,35},{35,3},{4,36},{36... | collective-permute-start | bytes 3440648 | tf_op jit(solution)/shard_map/ppermute | solution.py:363
  45.1 3.3 %unpack.2 = (bf16[88,56,128]{2,1,0:T(8,128)(2,1)S(1)}, s32[8,128]{1,0:T(8,128)S(1)}) custom-call(f32[8,56,640]{2,1,0:T(8,128)S(1)} %all-to-all-done.in_ref), custom_call_target="tpu_custom_call" | custom-call | tf_op jit(solution)/shard_map/unpack/pallas_call | solution.py:110
  48.4 3.3 %unpack.3 = (bf16[88,56,128]{2,1,0:T(8,128)(2,1)S(1)}, s32[8,128]{1,0:T(8,128)S(1)}) custom-call(f32[8,56,640]{2,1,0:T(8,128)S(1)} %collective-permute-done.1.in_ref), custom_call_target="tpu_custom_call" | custom-call | tf_op jit(solution)/shard_map/unpack/pallas_call | solution.py:110
  51.7 4.7 %mirror.3 = f32[8,56,128]{2,1,0:T(8,128)} custom-call(s32[4]{0:T(128)S(1)} %pad_add_fusion.me_ref, s32[8,128]{1,0:T(8,128)S(1)} %get-tuple-element.25.pos_a_ref, s32[8,128]{1,0:T(8,128)S(1)} %get-tuple-element.26.pos_b_ref, f32[4,56,128]{2,1,0:T(8,128)S(1)} %join_cores.1.rows_ref, bf16[88,56,128]{2,1,0:T(8,128)(2,1)S(1)} %get-tuple-element.28.blocks_a_ref, ...), custom_call_target="tpu_custom_call" | custom-call | flops 200000000 | bytes 4000000 | tf_op jit(solution)/shard_map/mirror/pallas_call | solution.py:272
  56.3 5.8 %all-to-all-start.1 = ((f32[8,56,128]{2,1,0:T(8,128)}), f32[8,56,128]{2,1,0:T(8,128)S(1)}, u32[]{:S(2)}, u32[]{:S(2)}) async-start(f32[8,56,128]{2,1,0:T(8,128)} %mirror.3), calls=%async_computation.1 | async-start | bytes 458752 | tf_op jit(solution)/shard_map/all_to_all | solution.py:341
  62.2 4.5 %direct.3 = f32[4,56,128]{2,1,0:T(8,128)S(1)} custom-call(s32[4]{0:T(128)S(1)} %pad_add_fusion.me_ref, s32[8,128]{1,0:T(8,128)S(1)} %get-tuple-element.25.pos_a_ref, s32[8,128]{1,0:T(8,128)S(1)} %get-tuple-element.26.pos_b_ref, f32[8,56,128]{2,1,0:T(8,128)S(1)} %pick_half.1.cols_ref, bf16[88,56,128]{2,1,0:T(8,128)(2,1)S(1)} %get-tuple-element.28.blocks_a_ref, ...), custom_call_target="tpu_custom_call" | custom-call | flops 200000000 | bytes 4000000 | tf_op jit(solution)/shard_map/direct/pallas_call | solution.py:272
  66.7 2.2 %all-to-all-done.1 = f32[8,56,128]{2,1,0:T(8,128)S(1)} async-done(((f32[8,56,128]{2,1,0:T(8,128)}), f32[8,56,128]{2,1,0:T(8,128)S(1)}, u32[]{:S(2)}, u32[]{:S(2)}) %all-to-all-start.1) | async-done | bytes 229408 | tf_op jit(solution)/shard_map/all_to_all | solution.py:341
  69.8 9.1 %all-to-all-start.2 = ((f32[4,4,56,128]{3,2,1,0:T(8,128)}), f32[4,4,56,128]{3,2,1,0:T(8,128)S(1)}, u32[]{:S(2)}, u32[]{:S(2)}) async-start(f32[4,4,56,128]{3,2,1,0:T(8,128)} %broadcast_in_dim.91), calls=%async_computation.2 | async-start | bytes 917504 | tf_op jit(solution)/shard_map/all_to_all | solution.py:341
  78.9 12.2 %all-to-all-done.2 = f32[4,4,56,128]{3,2,1,0:T(8,128)S(1)} async-done(((f32[4,4,56,128]{3,2,1,0:T(8,128)}), f32[4,4,56,128]{3,2,1,0:T(8,128)S(1)}, u32[]{:S(2)}, u32[]{:S(2)}) %all-to-all-start.2) | async-done | bytes 458784 | tf_op jit(solution)/shard_map/all_to_all | solution.py:341
  91.9 5.3 %all-to-all-start.3 = ((f32[8,56,128]{2,1,0:T(8,128)}), f32[8,56,128]{2,1,0:T(8,128)S(1)}, u32[]{:S(2)}, u32[]{:S(2)}) async-start(f32[8,56,128]{2,1,0:T(8,128)} %broadcast_in_dim.93), calls=%async_computation.3 | async-start | bytes 458752 | tf_op jit(solution)/shard_map/all_to_all | solution.py:341
  97.2 4.7 %mirror.4 = f32[8,56,128]{2,1,0:T(8,128)} custom-call(s32[4]{0:T(128)S(1)} %pad_add_fusion.me_ref, s32[8,128]{1,0:T(8,128)S(1)} %get-tuple-element.25.pos_a_ref, s32[8,128]{1,0:T(8,128)S(1)} %get-tuple-element.26.pos_b_ref, f32[4,56,128]{2,1,0:T(8,128)S(1)} %fusion.rows_ref, bf16[88,56,128]{2,1,0:T(8,128)(2,1)S(1)} %get-tuple-element.28.blocks_a_ref, ...), custom_call_target="tpu_custom_call" | custom-call | flops 200000000 | bytes 4000000 | tf_op jit(solution)/shard_map/mirror/pallas_call | solution.py:272
  103.2 4.0 %all-to-all-start.4 = ((f32[8,56,128]{2,1,0:T(8,128)}), f32[8,56,128]{2,1,0:T(8,128)}, u32[]{:S(2)}, u32[]{:S(2)}) async-start(f32[8,56,128]{2,1,0:T(8,128)} %mirror.4), calls=%async_computation.4 | async-start | bytes 458752 | tf_op jit(solution)/shard_map/all_to_all | solution.py:341
  107.2 4.5 %direct.4 = f32[4,56,128]{2,1,0:T(8,128)S(1)} custom-call(s32[4]{0:T(128)S(1)} %pad_add_fusion.me_ref, s32[8,128]{1,0:T(8,128)S(1)} %get-tuple-element.25.pos_a_ref, s32[8,128]{1,0:T(8,128)S(1)} %get-tuple-element.26.pos_b_ref, f32[8,56,128]{2,1,0:T(8,128)S(1)} %all-to-all-done.3.cols_ref, bf16[88,56,128]{2,1,0:T(8,128)(2,1)S(1)} %get-tuple-element.28.blocks_a_ref, ...), custom_call_target="tpu_custom_call" | custom-call | flops 200000000 | bytes 4000000 | tf_op jit(solution)/shard_map/direct/pallas_call | solution.py:272
  114.3 15.1 %all_to_all.55 = f32[4,4,56,128]{3,2,1,0:T(8,128)S(1)} all-to-all(f32[4,4,56,128]{3,2,1,0:T(8,128)S(1)} %broadcast_in_dim.95), channel_id=1, replica_groups=mesh['x'=4,'zl'=2,'core'=2,'zh'=4,'y'=8] {'zh'}, dimensions={0} | all-to-all | bytes 917504 | tf_op jit(solution)/shard_map/all_to_all | solution.py:341
  130.2 6.6 %all-to-all-start.6 = ((f32[8,56,128]{2,1,0:T(8,128)}), f32[8,56,128]{2,1,0:T(8,128)S(1)}, u32[]{:S(2)}, u32[]{:S(2)}) async-start(f32[8,56,128]{2,1,0:T(8,128)} %broadcast_in_dim.97), calls=%async_computation.6 | async-start | bytes 458752 | tf_op jit(solution)/shard_map/all_to_all | solution.py:341
  136.8 4.6 %mirror.5 = f32[8,56,128]{2,1,0:T(8,128)} custom-call(s32[4]{0:T(128)S(1)} %pad_add_fusion.me_ref, s32[8,128]{1,0:T(8,128)S(1)} %get-tuple-element.25.pos_a_ref, s32[8,128]{1,0:T(8,128)S(1)} %get-tuple-element.26.pos_b_ref, f32[4,56,128]{2,1,0:T(8,128)S(1)} %multiply_subtract_fusion.1.rows_ref, bf16[88,56,128]{2,1,0:T(8,128)(2,1)S(1)} %get-tuple-element.28.blocks_a_ref, ...), custom_call_target="tpu_custom_call" | custom-call | flops 200000000 | bytes 4000000 | tf_op jit(solution)/shard_map/mirror/pallas_call | solution.py:272
  142.8 3.8 %all-to-all-start.7 = ((f32[8,56,128]{2,1,0:T(8,128)}), f32[8,56,128]{2,1,0:T(8,128)S(1)}, u32[]{:S(2)}, u32[]{:S(2)}) async-start(f32[8,56,128]{2,1,0:T(8,128)} %mirror.5), calls=%async_computation.7 | async-start | bytes 458752 | tf_op jit(solution)/shard_map/all_to_all | solution.py:341
  146.6 4.5 %direct.5 = f32[4,56,128]{2,1,0:T(8,128)S(1)} custom-call(s32[4]{0:T(128)S(1)} %pad_add_fusion.me_ref, s32[8,128]{1,0:T(8,128)S(1)} %get-tuple-element.25.pos_a_ref, s32[8,128]{1,0:T(8,128)S(1)} %get-tuple-element.26.pos_b_ref, f32[8,56,128]{2,1,0:T(8,128)S(1)} %all-to-all-done.6.cols_ref, bf16[88,56,128]{2,1,0:T(8,128)(2,1)S(1)} %get-tuple-element.28.blocks_a_ref, ...), custom_call_target="tpu_custom_call" | custom-call | flops 200000000 | bytes 4000000 | tf_op jit(solution)/shard_map/direct/pallas_call | solution.py:272
  152.7 12.9 %all_to_all.56 = f32[4,4,56,128]{3,2,1,0:T(8,128)S(1)} all-to-all(f32[4,4,56,128]{3,2,1,0:T(8,128)S(1)} %broadcast_in_dim.99), channel_id=1, replica_groups=mesh['x'=4,'zl'=2,'core'=2,'zh'=4,'y'=8] {'zh'}, dimensions={0} | all-to-all | bytes 917504 | tf_op jit(solution)/shard_map/all_to_all | solution.py:341
  166.7 8.9 %all_to_all.57 = f32[2,4,56,128]{3,2,1,0:T(8,128)S(1)} all-to-all(f32[2,4,56,128]{3,2,1,0:T(8,128)S(1)} %halve.1), channel_id=1, replica_groups=mesh['x'=4,'zl'=2,'core'=2,'zh'=4,'y'=8] {'core'}, dimensions={0} | all-to-all | bytes 458752 | tf_op jit(solution)/shard_map/all_to_all | solution.py:341
  175.7 28.8 %all_to_all.58.in_ref = f32[8,4,56,128]{3,2,1,0:T(8,128)S(1)} all-to-all(f32[8,4,56,128]{3,2,1,0:T(8,128)S(1)} %broadcast_in_dim.100), channel_id=1, replica_groups=mesh['x'=4,'zl'=2,'core'=2,'zh'=4,'y'=8] {'y'}, dimensions={0} | all-to-all | bytes 1835008 | tf_op jit(solution)/shard_map/all_to_all | solution.py:341
  (45 shorter events, 20.1 us)
Async XLA Ops:
  0.0 1.0 copy-start.1
  1.0 0.7 copy-start.2
  1.7 0.7 copy-start.3
  3.6 7.9 %copy-start = (f32[1792,128]{1,0:T(8,128)S(1)}, f32[1792,128]{1,0:T(8,128)}, u32[]{:S(2)}) copy-start(f32[1792,128]{1,0:T(8,128)} %param.4) | copy-start | bytes 2752516
  3.6 37.2 %all-to-all-start = ((f32[8,56,640]{2,1,0:T(8,128)}), f32[8,56,640]{2,1,0:T(8,128)S(1)}, u32[]{:S(2)}, u32[]{:S(2)}) async-start(f32[8,56,640]{2,1,0:T(8,128)} %broadcast_in_dim.87), calls=%async_computation | async-start | bytes 2293760 | tf_op jit(solution)/shard_map/all_to_all | solution.py:341
  12.7 25.9 %collective-permute-start = (f32[2,56,128]{2,1,0:T(8,128)S(1)}, f32[2,56,128]{2,1,0:T(8,128)S(1)}, u32[]{:S(2)}, u32[]{:S(2)}) collective-permute-start(f32[2,56,128]{2,1,0:T(8,128)S(1)} %get-tuple-element.22), channel_id=1, source_target_pairs={{0,32},{32,0},{1,33},{33,1},{2,34},{34,2},{3,35},{35,3},{4,36},{36... | collective-permute-start | bytes 172040 | tf_op jit(solution)/shard_map/ppermute | solution.py:359
  40.9 7.5 %collective-permute-start.1 = (f32[8,56,640]{2,1,0:T(8,128)S(1)}, f32[8,56,640]{2,1,0:T(8,128)S(1)}, u32[]{:S(2)}, u32[]{:S(2)}) collective-permute-start(f32[8,56,640]{2,1,0:T(8,128)S(1)} %all-to-all-done.in_ref), channel_id=1, source_target_pairs={{0,32},{32,0},{1,33},{33,1},{2,34},{34,2},{3,35},{35,3},{4,36},{36... | collective-permute-start | bytes 3440648 | tf_op jit(solution)/shard_map/ppermute | solution.py:363
  56.3 12.6 %all-to-all-start.1 = ((f32[8,56,128]{2,1,0:T(8,128)}), f32[8,56,128]{2,1,0:T(8,128)S(1)}, u32[]{:S(2)}, u32[]{:S(2)}) async-start(f32[8,56,128]{2,1,0:T(8,128)} %mirror.3), calls=%async_computation.1 | async-start | bytes 458752 | tf_op jit(solution)/shard_map/all_to_all | solution.py:341
  69.8 21.3 %all-to-all-start.2 = ((f32[4,4,56,128]{3,2,1,0:T(8,128)}), f32[4,4,56,128]{3,2,1,0:T(8,128)S(1)}, u32[]{:S(2)}, u32[]{:S(2)}) async-start(f32[4,4,56,128]{3,2,1,0:T(8,128)} %broadcast_in_dim.91), calls=%async_computation.2 | async-start | bytes 917504 | tf_op jit(solution)/shard_map/all_to_all | solution.py:341
  91.9 11.3 %all-to-all-start.3 = ((f32[8,56,128]{2,1,0:T(8,128)}), f32[8,56,128]{2,1,0:T(8,128)S(1)}, u32[]{:S(2)}, u32[]{:S(2)}) async-start(f32[8,56,128]{2,1,0:T(8,128)} %broadcast_in_dim.93), calls=%async_computation.3 | async-start | bytes 458752 | tf_op jit(solution)/shard_map/all_to_all | solution.py:341
  103.2 10.0 %all-to-all-start.4 = ((f32[8,56,128]{2,1,0:T(8,128)}), f32[8,56,128]{2,1,0:T(8,128)}, u32[]{:S(2)}, u32[]{:S(2)}) async-start(f32[8,56,128]{2,1,0:T(8,128)} %mirror.4), calls=%async_computation.4 | async-start | bytes 458752 | tf_op jit(solution)/shard_map/all_to_all | solution.py:341
  130.2 12.6 %all-to-all-start.6 = ((f32[8,56,128]{2,1,0:T(8,128)}), f32[8,56,128]{2,1,0:T(8,128)S(1)}, u32[]{:S(2)}, u32[]{:S(2)}) async-start(f32[8,56,128]{2,1,0:T(8,128)} %broadcast_in_dim.97), calls=%async_computation.6 | async-start | bytes 458752 | tf_op jit(solution)/shard_map/all_to_all | solution.py:341
  142.8 9.8 %all-to-all-start.7 = ((f32[8,56,128]{2,1,0:T(8,128)}), f32[8,56,128]{2,1,0:T(8,128)S(1)}, u32[]{:S(2)}, u32[]{:S(2)}) async-start(f32[8,56,128]{2,1,0:T(8,128)} %mirror.5), calls=%async_computation.7 | async-start | bytes 458752 | tf_op jit(solution)/shard_map/all_to_all | solution.py:341

commit v6 on v5

--- a/solution.py
+++ b/solution.py
@@ -44,7 +44,15 @@
     return x if shift == 0 else pltpu.roll(x, shift, 1)
 
 
-def pack_kernel(tiles_ref, diag_ref, pos_ref, out_ref):
+def pack_kernel(tiles_hbm, diag_hbm, pos_hbm, out_hbm, tiles_ref, diag_ref, pos_ref, out_ref, sems, out_sems):
+    copies = [
+        pltpu.make_async_copy(src, dst, sems.at[k])
+        for k, (src, dst) in enumerate(((tiles_hbm, tiles_ref), (diag_hbm, diag_ref), (pos_hbm, pos_ref)))
+    ]
+    for copy in copies:
+        copy.start()
+    for copy in copies:
+        copy.wait()
     lane = lane_iota()
     pieces = [tiles_ref[t] for t in range(TILES)] + [diag_ref[...]]
     wide = [
@@ -66,40 +74,51 @@
             start = SLOTS * ORB - q * LANES
             total = jnp.where(lane >= start, roll_to(places, 0, start), total)
         out_ref[:, q * LANES : (q + 1) * LANES] = total
+    copies = [pltpu.make_async_copy(out_ref, out_hbm.at[k], out_sems.at[k]) for k in range(N_Y)]
+    for copy in copies:
+        copy.start()
+    for copy in copies:
+        copy.wait()
 
 
 def pack(tile_data, diag, places):
     return pl.pallas_call(
         pack_kernel,
-        out_shape=jax.ShapeDtypeStruct((ORB, WIDE), f32),
-        in_specs=vmem(3),
-        out_specs=vmem(1)[0],
-        compiler_params=params(),
+        out_shape=jax.ShapeDtypeStruct((N_Y, ORB, WIDE), f32),
+        in_specs=[pl.BlockSpec(memory_space=pl.ANY)] * 3,
+        out_specs=pl.BlockSpec(memory_space=pl.ANY),
+        scratch_shapes=[
+            pltpu.VMEM((TILES, ORB, ORB), f32),
+            pltpu.VMEM((ORB, ORB), f32),
+            pltpu.VMEM((2, TILES), jnp.int32),
+            pltpu.VMEM((ORB, WIDE), f32),
+            pltpu.SemaphoreType.DMA((3,)),
+            pltpu.SemaphoreType.DMA((N_Y,)),
+        ],
+        compiler_params=pltpu.CompilerParams(vmem_limit_bytes=56 * 1024 * 1024),
         name="pack",
     )(tile_data, diag, places)
 
 
-def two_terms(x):
-    high = x.astype(bf16).astype(f32)
-    low = x - high
-    return (high + pltpu.roll(low, 64, 1)).astype(bf16)
-
-
 def unpack_kernel(in_ref, blocks_ref, places_ref):
-    lane = lane_iota()
-
-    def one_source(s, carry):
-        for t in range(SLOTS):
-            start = t * ORB
-            q, off = start // LANES, start % LANES
-            x = roll_to(in_ref[s, :, q * LANES : (q + 1) * LANES], off, 0)
-            if off + ORB > LANES:
-                y = roll_to(in_ref[s, :, (q + 1) * LANES : (q + 2) * LANES], off, 0)
-                x = jnp.where(lane < LANES - off, x, y)
-            blocks_ref[s * SLOTS + t] = two_terms(jnp.where(lane < ORB, x, 0.0))
-        return carry
-
-    lax.fori_loop(0, N_Y, one_source, 0)
+    x = in_ref[...].reshape(N_Y * ORB, WIDE)
+    high = x.astype(bf16)
+    low = (x - high.astype(f32)).astype(bf16)
+    for t in range(SLOTS):
+        start = t * ORB
+        q, off = start // LANES, start % LANES
+        width = LANES if off + ORB <= LANES else 2 * LANES
+        source = lax.broadcasted_iota(jnp.int32, (width, LANES), 0)
+        target = lax.broadcasted_iota(jnp.int32, (width, LANES), 1)
+        window = slice(q * LANES, q * LANES + width)
+        total = None
+        for term, at in ((high, 0), (low, 64)):
+            hit = (target >= at) & (target < at + ORB) & (source == target - at + off)
+            part = jnp.dot(term[:, window], jnp.where(hit, 1.0, 0.0).astype(bf16), preferred_element_type=f32)
+            total = part if total is None else total + part
+        total = total.astype(bf16)
+        for s in range(N_Y):
+            blocks_ref[s * SLOTS + t] = total[s * ORB : (s + 1) * ORB]
     for s in range(N_Y):
         last = in_ref[s, 0:1, WIDE - LANES : WIDE]
         shown = lax.broadcasted_iota(jnp.int32, (1, LANES), 1) >= PLACE
@@ -288,21 +307,20 @@
     lane = lane_iota()
     core = me_ref[2]
     mine = ((lane >> 3) & 1) == core
-    for z in range(N_ZH):
-        for k in range(N_CORE):
-            x = in_ref[z] if k == 0 else pltpu.roll(in_ref[z], 64, 1)
-            x = jnp.where(lane < 64, x, 0.0)
-            for step in (32, 16, 8):
-                block = lane & (4 * step - 1)
-                moved = pltpu.roll(x, step, 1)
-                x = jnp.where(block < step, x, jnp.where((block >= 2 * step) & (block < 3 * step), moved, 0.0))
-            out_ref[k, z] = jnp.where(mine, pltpu.roll(x, core * VS, 1), 0.0)
+    for k in range(N_CORE):
+        x = in_ref[...] if k == 0 else pltpu.roll(in_ref[...], 64, 1)
+        x = jnp.where(lane < 64, x, 0.0)
+        for step in (32, 16, 8):
+            block = lane & (4 * step - 1)
+            moved = pltpu.roll(x, step, 1)
+            x = jnp.where(block < step, x, jnp.where((block >= 2 * step) & (block < 3 * step), moved, 0.0))
+        out_ref[k] = jnp.where(mine, pltpu.roll(x, core * VS, 1), 0.0)
 
 
 def halve(me, current):
     return pl.pallas_call(
         halve_kernel,
-        out_shape=jax.ShapeDtypeStruct((N_CORE, N_ZH, ORB, LANES), f32),
+        out_shape=jax.ShapeDtypeStruct((N_CORE, ORB, LANES), f32),
         in_specs=[pl.BlockSpec(memory_space=pltpu.SMEM)] + vmem(1),
         out_specs=vmem(1)[0],
         compiler_params=params(),
@@ -313,7 +331,7 @@
 def spread_kernel(in_ref, out_ref):
     lane = lane_iota()
     for z in range(N_ZH):
-        x = [in_ref[y, z] for y in range(N_Y)]
+        x = [in_ref[z, y] for y in range(N_Y)]
         for d in (4, 2, 1):
             upper = (lane & (16 * d)) != 0
             for a in range(N_Y):
@@ -352,7 +370,7 @@
     swap = [(0, 1), (1, 0)]
 
     packed = pack(tiles[0, 0], diag_blocks[0], tile_pos[0, 0])
-    packed = gather(packed, "y", N_Y)
+    packed = exchange(packed, "y")
 
     mine, other, own = slice_vectors(me, vectors.reshape(-1, ORB, LANES))
     cols = pick_half(me, lax.all_gather(own, ("x", "zl", "core"), axis=0, tiled=False))
@@ -373,7 +391,12 @@
         got_cols = exchange(out_cols, ROW_AX)
         out_rows = product(direct_kernel, "direct", where, cols, blocks, N_ZH)
         partial = out_rows + jnp.where(at_own, jnp.sum(got_cols, 0)[None], 0.0)
-        image = jnp.sum(gather(partial, "zh", N_ZH).reshape(N_ZH, N_ZH, ORB, LANES), 0)
+        if step < DEGREE - 1:
+            image = jnp.sum(gather(partial, "zh", N_ZH).reshape(N_ZH, N_ZH, ORB, LANES), 0)
+        else:
+            image = jnp.sum(exchange(partial, "zh"), 0)
+            current = lax.dynamic_index_in_dim(current, zh, 0, keepdims=False)
+            previous = lax.dynamic_index_in_dim(previous, zh, 0, keepdims=False)
         shifted = (image - centre * current) / half_width
         following = shifted if previous is None else 2.0 * shifted - previous
         previous, current = current, following
@@ -381,7 +404,7 @@
             cols = gather(lax.dynamic_index_in_dim(current, zh, 0, keepdims=False), ROW_AX, N_R)
 
     result = jnp.sum(exchange(halve(me, current), "core"), 0)
-    result = gather(result, "y", N_Y).reshape(N_Y, N_ZH, ORB, LANES)
+    result = gather(result, ("zh", "y"), N_ZH * N_Y).reshape(N_ZH, N_Y, ORB, LANES)
     return spread(result).reshape(vectors.shape)
 
 

time: 208 us -> 200 us (0.962)
  blocking collectives: 86.3 us -> 80.8 us
  local copies, waits for them, and re-layouts: 5.82 us -> 2.33 us
  Pallas kernels: 39.7 us -> 37.2 us
    all_to_all x4, blocking collectives: 65.8 us -> 60.3 us  [exchange(): return lax.all_to_all(x, axes, split_axis=0, concat_axis=0, tiled=True)]
    pallas_call x2, Pallas kernels: 6.55 us -> 2.1 us  [unpack(): pl.pallas_call(unpack_kernel, out_shape=(jax.ShapeDtypeStruct((N_Y * SLOT...]
    unnamed x8 -> x2, local copies, waits for them, and re-layouts: 2.39 us -> 0.01 us
  transfers between devices with their start and end apart: 9 -> 9, of which waited for: 7 -> 8; matrix products, arithmetic and copies ran while one was open for 0% -> 0% of each run, Pallas kernels for 14% -> 13%
where the time goes in v6:
time: 200 us; the launch traced here: 197 us
  blocking collectives  80.8 us (40%)
  starting transfers between devices  52.5 us (26%)
  Pallas kernels  37.2 us (19%)
  waiting for transfers between devices  22.3 us (11%)
  local copies, waits for them, and re-layouts  2.33 us (1%)
    all_to_all x4, blocking collectives, exchange(): return lax.all_to_all(x, axes, split_axis=0, concat_axis=0, tiled=True)  60.3 us
    all_to_all x7, starting transfers between devices, exchange(): return lax.all_to_all(x, axes, split_axis=0, concat_axis=0, tiled=True)  43.6 us
    pallas_call x6, Pallas kernels, product(): pl.pallas_call(kernel, out_shape=jax.ShapeDtypeStruct((chunks, ORB, LANES...  27.5 us
    all_to_all x7, waiting for transfers between devices, exchange(): return lax.all_to_all(x, axes, split_axis=0, concat_axis=0, tiled=True)  20.9 us
    all_gather x1, blocking collectives, body(): lax.all_gather(own, ('x', 'zl', 'core'), axis=0, tiled=False)  20.5 us
    ppermute x1, starting transfers between devices, body(): current = join_cores(me, mine, lax.ppermute(other, 'core', swap))  4.72 us
    ppermute x1, starting transfers between devices, body(): blocks_b, pos_b = unpack(lax.ppermute(packed, 'core', swap))  4.23 us
  transfers between devices with their start and end apart: 9, of which 8 were waited for; matrix products, arithmetic and copies ran while one was open for 0% of the time, Pallas kernels for 13%

profile of v6, /device:TPU:1, one launch (start us, length us, event | category | flops | bytes accessed | tf_op | source)
XLA Modules:
  0.0 196.8 jit_solution(11183896554317675913)
XLA Ops:
  0.0 2.2 %pack.1 = f32[8,56,640]{2,1,0:T(8,128)} custom-call(f32[10,56,56]{2,1,0:T(8,128)} %bitcast.22, f32[56,56]{1,0:T(8,128)} %bitcast.23, s32[2,10]{1,0:T(2,128)} %bitcast.24), custom_call_target="tpu_custom_call" | custom-call | tf_op jit(solution)/shard_map/pack/pallas_call | solution.py:85
  2.2 7.8 %all-to-all-start = ((f32[8,56,640]{2,1,0:T(8,128)}), f32[8,56,640]{2,1,0:T(8,128)S(1)}, u32[]{:S(2)}, u32[]{:S(2)}) async-start(f32[8,56,640]{2,1,0:T(8,128)} %pack.1), calls=%async_computation | async-start | bytes 2293760 | tf_op jit(solution)/shard_map/all_to_all | solution.py:359
  11.3 4.7 %collective-permute-start = (f32[2,56,128]{2,1,0:T(8,128)S(1)}, f32[2,56,128]{2,1,0:T(8,128)S(1)}, u32[]{:S(2)}, u32[]{:S(2)}) collective-permute-start(f32[2,56,128]{2,1,0:T(8,128)S(1)} %get-tuple-element.22), channel_id=1, source_target_pairs={{0,32},{32,0},{1,33},{33,1},{2,34},{34,2},{3,35},{35,3},{4,36},{36... | collective-permute-start | bytes 172040 | tf_op jit(solution)/shard_map/ppermute | solution.py:377
  16.0 20.5 %all-gather = f32[896,128]{1,0:T(8,128)S(1)} all-gather(f32[56,128]{1,0:T(8,128)S(1)} %get-tuple-element.23), channel_id=2, replica_groups=mesh['x'=4,'zl'=2,'core'=2,'zh'=4,'y'=8] {'x','zl','core'}, dimensions={0}, use_global_device_ids=true | all-gather | bytes 487424 | tf_op jit(solution)/shard_map/all_gather | solution.py:376
  39.5 4.2 %collective-permute-start.1 = (f32[8,56,640]{2,1,0:T(8,128)S(1)}, f32[8,56,640]{2,1,0:T(8,128)S(1)}, u32[]{:S(2)}, u32[]{:S(2)}) collective-permute-start(f32[8,56,640]{2,1,0:T(8,128)S(1)} %all-to-all-done.in_ref), channel_id=1, source_target_pairs={{0,32},{32,0},{1,33},{33,1},{2,34},{34,2},{3,35},{35,3},{4,36},{36... | collective-permute-start | bytes 3440648 | tf_op jit(solution)/shard_map/ppermute | solution.py:381
  47.2 4.7 %mirror.3 = f32[8,56,128]{2,1,0:T(8,128)} custom-call(s32[4]{0:T(128)S(1)} %pad_add_fusion.me_ref, s32[8,128]{1,0:T(8,128)S(1)} %get-tuple-element.25.pos_a_ref, s32[8,128]{1,0:T(8,128)S(1)} %get-tuple-element.26.pos_b_ref, f32[4,56,128]{2,1,0:T(8,128)S(1)} %join_cores.1.rows_ref, bf16[88,56,128]{2,1,0:T(8,128)(2,1)S(1)} %get-tuple-element.28.blocks_a_ref, ...), custom_call_target="tpu_custom_call" | custom-call | flops 200000000 | bytes 4000000 | tf_op jit(solution)/shard_map/mirror/pallas_call | solution.py:291
  51.8 5.8 %all-to-all-start.1 = ((f32[8,56,128]{2,1,0:T(8,128)}), f32[8,56,128]{2,1,0:T(8,128)S(1)}, u32[]{:S(2)}, u32[]{:S(2)}) async-start(f32[8,56,128]{2,1,0:T(8,128)} %mirror.3), calls=%async_computation.1 | async-start | bytes 458752 | tf_op jit(solution)/shard_map/all_to_all | solution.py:359
  57.7 4.5 %direct.3 = f32[4,56,128]{2,1,0:T(8,128)S(1)} custom-call(s32[4]{0:T(128)S(1)} %pad_add_fusion.me_ref, s32[8,128]{1,0:T(8,128)S(1)} %get-tuple-element.25.pos_a_ref, s32[8,128]{1,0:T(8,128)S(1)} %get-tuple-element.26.pos_b_ref, f32[8,56,128]{2,1,0:T(8,128)S(1)} %pick_half.1.cols_ref, bf16[88,56,128]{2,1,0:T(8,128)(2,1)S(1)} %get-tuple-element.28.blocks_a_ref, ...), custom_call_target="tpu_custom_call" | custom-call | flops 200000000 | bytes 4000000 | tf_op jit(solution)/shard_map/direct/pallas_call | solution.py:291
  62.2 1.8 all-to-all-done.1
  65.0 9.1 %all-to-all-start.2 = ((f32[4,4,56,128]{3,2,1,0:T(8,128)}), f32[4,4,56,128]{3,2,1,0:T(8,128)S(1)}, u32[]{:S(2)}, u32[]{:S(2)}) async-start(f32[4,4,56,128]{3,2,1,0:T(8,128)} %broadcast_in_dim.78), calls=%async_computation.2 | async-start | bytes 917504 | tf_op jit(solution)/shard_map/all_to_all | solution.py:359
  74.1 12.0 %all-to-all-done.2 = f32[4,4,56,128]{3,2,1,0:T(8,128)S(1)} async-done(((f32[4,4,56,128]{3,2,1,0:T(8,128)}), f32[4,4,56,128]{3,2,1,0:T(8,128)S(1)}, u32[]{:S(2)}, u32[]{:S(2)}) %all-to-all-start.2) | async-done | bytes 458784 | tf_op jit(solution)/shard_map/all_to_all | solution.py:359
  86.8 5.9 %all-to-all-start.3 = ((f32[8,56,128]{2,1,0:T(8,128)}), f32[8,56,128]{2,1,0:T(8,128)S(1)}, u32[]{:S(2)}, u32[]{:S(2)}) async-start(f32[8,56,128]{2,1,0:T(8,128)} %broadcast_in_dim.80), calls=%async_computation.3 | async-start | bytes 458752 | tf_op jit(solution)/shard_map/all_to_all | solution.py:359
  92.8 4.7 %mirror.4 = f32[8,56,128]{2,1,0:T(8,128)} custom-call(s32[4]{0:T(128)S(1)} %pad_add_fusion.me_ref, s32[8,128]{1,0:T(8,128)S(1)} %get-tuple-element.25.pos_a_ref, s32[8,128]{1,0:T(8,128)S(1)} %get-tuple-element.26.pos_b_ref, f32[4,56,128]{2,1,0:T(8,128)S(1)} %fusion.rows_ref, bf16[88,56,128]{2,1,0:T(8,128)(2,1)S(1)} %get-tuple-element.28.blocks_a_ref, ...), custom_call_target="tpu_custom_call" | custom-call | flops 200000000 | bytes 4000000 | tf_op jit(solution)/shard_map/mirror/pallas_call | solution.py:291
  98.7 4.0 %all-to-all-start.4 = ((f32[8,56,128]{2,1,0:T(8,128)}), f32[8,56,128]{2,1,0:T(8,128)}, u32[]{:S(2)}, u32[]{:S(2)}) async-start(f32[8,56,128]{2,1,0:T(8,128)} %mirror.4), calls=%async_computation.4 | async-start | bytes 458752 | tf_op jit(solution)/shard_map/all_to_all | solution.py:359
  102.8 4.5 %direct.4 = f32[4,56,128]{2,1,0:T(8,128)S(1)} custom-call(s32[4]{0:T(128)S(1)} %pad_add_fusion.me_ref, s32[8,128]{1,0:T(8,128)S(1)} %get-tuple-element.25.pos_a_ref, s32[8,128]{1,0:T(8,128)S(1)} %get-tuple-element.26.pos_b_ref, f32[8,56,128]{2,1,0:T(8,128)S(1)} %all-to-all-done.3.cols_ref, bf16[88,56,128]{2,1,0:T(8,128)(2,1)S(1)} %get-tuple-element.28.blocks_a_ref, ...), custom_call_target="tpu_custom_call" | custom-call | flops 200000000 | bytes 4000000 | tf_op jit(solution)/shard_map/direct/pallas_call | solution.py:291
  109.8 13.2 %all_to_all.55 = f32[4,4,56,128]{3,2,1,0:T(8,128)S(1)} all-to-all(f32[4,4,56,128]{3,2,1,0:T(8,128)S(1)} %broadcast_in_dim.82), channel_id=1, replica_groups=mesh['x'=4,'zl'=2,'core'=2,'zh'=4,'y'=8] {'zh'}, dimensions={0} | all-to-all | bytes 917504 | tf_op jit(solution)/shard_map/all_to_all | solution.py:359
  123.8 7.0 %all-to-all-start.6 = ((f32[8,56,128]{2,1,0:T(8,128)}), f32[8,56,128]{2,1,0:T(8,128)S(1)}, u32[]{:S(2)}, u32[]{:S(2)}) async-start(f32[8,56,128]{2,1,0:T(8,128)} %broadcast_in_dim.84), calls=%async_computation.6 | async-start | bytes 458752 | tf_op jit(solution)/shard_map/all_to_all | solution.py:359
  130.9 4.6 %mirror.5 = f32[8,56,128]{2,1,0:T(8,128)} custom-call(s32[4]{0:T(128)S(1)} %pad_add_fusion.me_ref, s32[8,128]{1,0:T(8,128)S(1)} %get-tuple-element.25.pos_a_ref, s32[8,128]{1,0:T(8,128)S(1)} %get-tuple-element.26.pos_b_ref, f32[4,56,128]{2,1,0:T(8,128)S(1)} %multiply_subtract_fusion.rows_ref, bf16[88,56,128]{2,1,0:T(8,128)(2,1)S(1)} %get-tuple-element.28.blocks_a_ref, ...), custom_call_target="tpu_custom_call" | custom-call | flops 200000000 | bytes 4000000 | tf_op jit(solution)/shard_map/mirror/pallas_call | solution.py:291
  136.8 3.8 %all-to-all-start.7 = ((f32[8,56,128]{2,1,0:T(8,128)}), f32[8,56,128]{2,1,0:T(8,128)S(1)}, u32[]{:S(2)}, u32[]{:S(2)}) async-start(f32[8,56,128]{2,1,0:T(8,128)} %mirror.5), calls=%async_computation.7 | async-start | bytes 458752 | tf_op jit(solution)/shard_map/all_to_all | solution.py:359
  140.6 4.5 %direct.5 = f32[4,56,128]{2,1,0:T(8,128)S(1)} custom-call(s32[4]{0:T(128)S(1)} %pad_add_fusion.me_ref, s32[8,128]{1,0:T(8,128)S(1)} %get-tuple-element.25.pos_a_ref, s32[8,128]{1,0:T(8,128)S(1)} %get-tuple-element.26.pos_b_ref, f32[8,56,128]{2,1,0:T(8,128)S(1)} %all-to-all-done.6.cols_ref, bf16[88,56,128]{2,1,0:T(8,128)(2,1)S(1)} %get-tuple-element.28.blocks_a_ref, ...), custom_call_target="tpu_custom_call" | custom-call | flops 200000000 | bytes 4000000 | tf_op jit(solution)/shard_map/direct/pallas_call | solution.py:291
  146.7 9.5 %all_to_all.56 = f32[4,56,128]{2,1,0:T(8,128)S(1)} all-to-all(f32[4,56,128]{2,1,0:T(8,128)S(1)} %select_add_fusion), channel_id=1, replica_groups=mesh['x'=4,'zl'=2,'core'=2,'zh'=4,'y'=8] {'zh'}, dimensions={0} | all-to-all | bytes 229376 | tf_op jit(solution)/shard_map/all_to_all | solution.py:359
  157.2 9.5 %all_to_all.57 = f32[2,56,128]{2,1,0:T(8,128)S(1)} all-to-all(f32[2,56,128]{2,1,0:T(8,128)S(1)} %halve.1), channel_id=1, replica_groups=mesh['x'=4,'zl'=2,'core'=2,'zh'=4,'y'=8] {'core'}, dimensions={0} | all-to-all | bytes 114688 | tf_op jit(solution)/shard_map/all_to_all | solution.py:359
  166.8 28.1 %all_to_all.58 = f32[32,56,128]{2,1,0:T(8,128)S(1)} all-to-all(f32[32,56,128]{2,1,0:T(8,128)S(1)} %broadcast_in_dim.86), channel_id=1, replica_groups=mesh['x'=4,'zl'=2,'core'=2,'zh'=4,'y'=8] {'zh','y'}, dimensions={0} | all-to-all | bytes 1835008 | tf_op jit(solution)/shard_map/all_to_all | solution.py:359
  194.8 1.9 spread.1
  (37 shorter events, 17.7 us)
Async XLA Ops:
  2.2 7.9 %copy-start = (f32[1792,128]{1,0:T(8,128)S(1)}, f32[1792,128]{1,0:T(8,128)}, u32[]{:S(2)}) copy-start(f32[1792,128]{1,0:T(8,128)} %param.4) | copy-start | bytes 2752516
  2.2 37.3 %all-to-all-start = ((f32[8,56,640]{2,1,0:T(8,128)}), f32[8,56,640]{2,1,0:T(8,128)S(1)}, u32[]{:S(2)}, u32[]{:S(2)}) async-start(f32[8,56,640]{2,1,0:T(8,128)} %pack.1), calls=%async_computation | async-start | bytes 2293760 | tf_op jit(solution)/shard_map/all_to_all | solution.py:359
  11.3 25.9 %collective-permute-start = (f32[2,56,128]{2,1,0:T(8,128)S(1)}, f32[2,56,128]{2,1,0:T(8,128)S(1)}, u32[]{:S(2)}, u32[]{:S(2)}) collective-permute-start(f32[2,56,128]{2,1,0:T(8,128)S(1)} %get-tuple-element.22), channel_id=1, source_target_pairs={{0,32},{32,0},{1,33},{33,1},{2,34},{34,2},{3,35},{35,3},{4,36},{36... | collective-permute-start | bytes 172040 | tf_op jit(solution)/shard_map/ppermute | solution.py:377
  39.5 6.6 %collective-permute-start.1 = (f32[8,56,640]{2,1,0:T(8,128)S(1)}, f32[8,56,640]{2,1,0:T(8,128)S(1)}, u32[]{:S(2)}, u32[]{:S(2)}) collective-permute-start(f32[8,56,640]{2,1,0:T(8,128)S(1)} %all-to-all-done.in_ref), channel_id=1, source_target_pairs={{0,32},{32,0},{1,33},{33,1},{2,34},{34,2},{3,35},{35,3},{4,36},{36... | collective-permute-start | bytes 3440648 | tf_op jit(solution)/shard_map/ppermute | solution.py:381
  51.8 12.2 %all-to-all-start.1 = ((f32[8,56,128]{2,1,0:T(8,128)}), f32[8,56,128]{2,1,0:T(8,128)S(1)}, u32[]{:S(2)}, u32[]{:S(2)}) async-start(f32[8,56,128]{2,1,0:T(8,128)} %mirror.3), calls=%async_computation.1 | async-start | bytes 458752 | tf_op jit(solution)/shard_map/all_to_all | solution.py:359
  65.0 21.1 %all-to-all-start.2 = ((f32[4,4,56,128]{3,2,1,0:T(8,128)}), f32[4,4,56,128]{3,2,1,0:T(8,128)S(1)}, u32[]{:S(2)}, u32[]{:S(2)}) async-start(f32[4,4,56,128]{3,2,1,0:T(8,128)} %broadcast_in_dim.78), calls=%async_computation.2 | async-start | bytes 917504 | tf_op jit(solution)/shard_map/all_to_all | solution.py:359
  86.8 11.9 %all-to-all-start.3 = ((f32[8,56,128]{2,1,0:T(8,128)}), f32[8,56,128]{2,1,0:T(8,128)S(1)}, u32[]{:S(2)}, u32[]{:S(2)}) async-start(f32[8,56,128]{2,1,0:T(8,128)} %broadcast_in_dim.80), calls=%async_computation.3 | async-start | bytes 458752 | tf_op jit(solution)/shard_map/all_to_all | solution.py:359
  98.7 10.0 %all-to-all-start.4 = ((f32[8,56,128]{2,1,0:T(8,128)}), f32[8,56,128]{2,1,0:T(8,128)}, u32[]{:S(2)}, u32[]{:S(2)}) async-start(f32[8,56,128]{2,1,0:T(8,128)} %mirror.4), calls=%async_computation.4 | async-start | bytes 458752 | tf_op jit(solution)/shard_map/all_to_all | solution.py:359
  123.8 13.0 %all-to-all-start.6 = ((f32[8,56,128]{2,1,0:T(8,128)}), f32[8,56,128]{2,1,0:T(8,128)S(1)}, u32[]{:S(2)}, u32[]{:S(2)}) async-start(f32[8,56,128]{2,1,0:T(8,128)} %broadcast_in_dim.84), calls=%async_computation.6 | async-start | bytes 458752 | tf_op jit(solution)/shard_map/all_to_all | solution.py:359
  136.8 9.8 %all-to-all-start.7 = ((f32[8,56,128]{2,1,0:T(8,128)}), f32[8,56,128]{2,1,0:T(8,128)S(1)}, u32[]{:S(2)}, u32[]{:S(2)}) async-start(f32[8,56,128]{2,1,0:T(8,128)} %mirror.5), calls=%async_computation.7 | async-start | bytes 458752 | tf_op jit(solution)/shard_map/all_to_all | solution.py:359

commit v7 on v6

--- a/solution.py
+++ b/solution.py
@@ -22,6 +22,8 @@
 
 filter_low = 0.0
 filter_high = 8.0
+centre = 0.5 * (filter_high + filter_low)
+half_width = 0.5 * (filter_high - filter_low)
 
 f32 = jnp.float32
 bf16 = jnp.bfloat16
@@ -303,53 +305,57 @@
     )(*scalars, field, *blocks)
 
 
-def halve_kernel(me_ref, in_ref, out_ref):
-    lane = lane_iota()
-    core = me_ref[2]
+def finish_kernel(me_ref, rows_ref, own_ref, current_ref, previous_ref, out_ref):
+    lane = lane_iota()
+    zh, core = me_ref[1], me_ref[2]
     mine = ((lane >> 3) & 1) == core
-    for k in range(N_CORE):
-        x = in_ref[...] if k == 0 else pltpu.roll(in_ref[...], 64, 1)
-        x = jnp.where(lane < 64, x, 0.0)
-        for step in (32, 16, 8):
-            block = lane & (4 * step - 1)
-            moved = pltpu.roll(x, step, 1)
-            x = jnp.where(block < step, x, jnp.where((block >= 2 * step) & (block < 3 * step), moved, 0.0))
-        out_ref[k] = jnp.where(mine, pltpu.roll(x, core * VS, 1), 0.0)
-
-
-def halve(me, current):
-    return pl.pallas_call(
-        halve_kernel,
-        out_shape=jax.ShapeDtypeStruct((N_CORE, ORB, LANES), f32),
-        in_specs=[pl.BlockSpec(memory_space=pltpu.SMEM)] + vmem(1),
+    scale = 2.0 / half_width
+    own = scale * own_ref[...] - (scale * centre) * current_ref[zh] - previous_ref[zh]
+    for z in range(N_ZH):
+        total = scale * rows_ref[z] + jnp.where(zh == z, own, 0.0)
+        for k in range(N_CORE):
+            x = total if k == 0 else pltpu.roll(total, 64, 1)
+            x = jnp.where(lane < 64, x, 0.0)
+            for step in (32, 16, 8):
+                block = lane & (4 * step - 1)
+                moved = pltpu.roll(x, step, 1)
+                x = jnp.where(block < step, x, jnp.where((block >= 2 * step) & (block < 3 * step), moved, 0.0))
+            out_ref[k * N_ZH + z] = jnp.where(mine, pltpu.roll(x, core * VS, 1), 0.0)
+
+
+def finish(me, rows, own, current, previous):
+    return pl.pallas_call(
+        finish_kernel,
+        out_shape=jax.ShapeDtypeStruct((N_CORE * N_ZH, ORB, LANES), f32),
+        in_specs=[pl.BlockSpec(memory_space=pltpu.SMEM)] + vmem(4),
         out_specs=vmem(1)[0],
         compiler_params=params(),
-        name="halve",
-    )(me, current)
+        name="finish",
+    )(me, rows, own, current, previous)
 
 
 def spread_kernel(in_ref, out_ref):
     lane = lane_iota()
-    for z in range(N_ZH):
-        x = [in_ref[z, y] for y in range(N_Y)]
-        for d in (4, 2, 1):
-            upper = (lane & (16 * d)) != 0
-            for a in range(N_Y):
-                if a & d:
-                    continue
-                low, high = x[a], x[a + d]
-                x[a] = jnp.where(upper, pltpu.roll(high, 16 * d, 1), low)
-                x[a + d] = jnp.where(upper, high, pltpu.roll(low, LANES - 16 * d, 1))
-        for y in range(N_Y):
-            out_ref[z * N_Y + y] = x[y]
+    x = [in_ref[0, y] for y in range(N_Y)]
+    for d in (4, 2, 1):
+        upper = (lane & (16 * d)) != 0
+        for a in range(N_Y):
+            if a & d:
+                continue
+            low, high = x[a], x[a + d]
+            x[a] = jnp.where(upper, pltpu.roll(high, 16 * d, 1), low)
+            x[a + d] = jnp.where(upper, high, pltpu.roll(low, LANES - 16 * d, 1))
+    for y in range(N_Y):
+        out_ref[y] = x[y]
 
 
 def spread(gathered):
     return pl.pallas_call(
         spread_kernel,
         out_shape=jax.ShapeDtypeStruct((N_ZH * N_Y, ORB, LANES), f32),
-        in_specs=vmem(1),
-        out_specs=vmem(1)[0],
+        grid=(N_ZH,),
+        in_specs=[pl.BlockSpec((1, N_Y, ORB, LANES), lambda z: (z, 0, 0, 0))],
+        out_specs=pl.BlockSpec((N_Y, ORB, LANES), lambda z: (z, 0, 0)),
         compiler_params=params(),
         name="spread",
     )(gathered)
@@ -381,8 +387,6 @@
     blocks_b, pos_b = unpack(lax.ppermute(packed, "core", swap))
     where, blocks = (me, pos_a, pos_b), (blocks_a, blocks_b)
 
-    centre = 0.5 * (filter_high + filter_low)
-    half_width = 0.5 * (filter_high - filter_low)
     at_own = (lax.broadcasted_iota(jnp.int32, (N_ZH, 1, 1), 0) == zh)
     previous = None
     for step in range(DEGREE):
@@ -390,20 +394,17 @@
         out_cols, cols = lax.optimization_barrier((out_cols, cols))
         got_cols = exchange(out_cols, ROW_AX)
         out_rows = product(direct_kernel, "direct", where, cols, blocks, N_ZH)
-        partial = out_rows + jnp.where(at_own, jnp.sum(got_cols, 0)[None], 0.0)
-        if step < DEGREE - 1:
-            image = jnp.sum(gather(partial, "zh", N_ZH).reshape(N_ZH, N_ZH, ORB, LANES), 0)
-        else:
-            image = jnp.sum(exchange(partial, "zh"), 0)
-            current = lax.dynamic_index_in_dim(current, zh, 0, keepdims=False)
-            previous = lax.dynamic_index_in_dim(previous, zh, 0, keepdims=False)
+        own = jnp.sum(got_cols, 0)
+        if step == DEGREE - 1:
+            break
+        partial = out_rows + jnp.where(at_own, own[None], 0.0)
+        image = jnp.sum(gather(partial, "zh", N_ZH).reshape(N_ZH, N_ZH, ORB, LANES), 0)
         shifted = (image - centre * current) / half_width
         following = shifted if previous is None else 2.0 * shifted - previous
         previous, current = current, following
-        if step < DEGREE - 1:
-            cols = gather(lax.dynamic_index_in_dim(current, zh, 0, keepdims=False), ROW_AX, N_R)
-
-    result = jnp.sum(exchange(halve(me, current), "core"), 0)
+        cols = gather(lax.dynamic_index_in_dim(current, zh, 0, keepdims=False), ROW_AX, N_R)
+
+    result = jnp.sum(exchange(finish(me, out_rows, own, current, previous), ("core", "zh")), 0)
     result = gather(result, ("zh", "y"), N_ZH * N_Y).reshape(N_ZH, N_Y, ORB, LANES)
     return spread(result).reshape(vectors.shape)
 

time: 200 us -> 199 us (level)
    all_to_all x4 -> x3, blocking collectives: 60.3 us -> 58.5 us  [exchange(): return lax.all_to_all(x, axes, split_axis=0, concat_axis=0, tiled=True)]
  transfers between devices with their start and end apart: 9 -> 9, of which waited for: 8 -> 8; matrix products, arithmetic and copies ran while one was open for 0% -> 0% of each run, Pallas kernels for 13% -> 14%
where the time goes in v7:
time: 199 us; the launch traced here: 195 us
  blocking collectives  78.9 us (40%)
  starting transfers between devices  52.5 us (26%)
  Pallas kernels  37.7 us (19%)
  waiting for transfers between devices  22.3 us (11%)
  local copies, waits for them, and re-layouts  2.33 us (1%)
    all_to_all x3, blocking collectives, exchange(): return lax.all_to_all(x, axes, split_axis=0, concat_axis=0, tiled=True)  58.5 us
    all_to_all x7, starting transfers between devices, exchange(): return lax.all_to_all(x, axes, split_axis=0, concat_axis=0, tiled=True)  43.6 us
    pallas_call x6, Pallas kernels, product(): pl.pallas_call(kernel, out_shape=jax.ShapeDtypeStruct((chunks, ORB, LANES...  27.5 us
    all_to_all x7, waiting for transfers between devices, exchange(): return lax.all_to_all(x, axes, split_axis=0, concat_axis=0, tiled=True)  20.9 us
    all_gather x1, blocking collectives, body(): lax.all_gather(own, ('x', 'zl', 'core'), axis=0, tiled=False)  20.5 us
    ppermute x1, starting transfers between devices, body(): current = join_cores(me, mine, lax.ppermute(other, 'core', swap))  4.72 us
    ppermute x1, starting transfers between devices, body(): blocks_b, pos_b = unpack(lax.ppermute(packed, 'core', swap))  4.23 us
  transfers between devices with their start and end apart: 9, of which 8 were waited for; matrix products, arithmetic and copies ran while one was open for 0% of the time, Pallas kernels for 14%

profile of v7, /device:TPU:1, one launch (start us, length us, event | category | flops | bytes accessed | tf_op | source)
XLA Modules:
  0.0 195.3 jit_solution(4564938350604952890)
XLA Ops:
  0.0 2.2 %pack.1 = f32[8,56,640]{2,1,0:T(8,128)} custom-call(f32[10,56,56]{2,1,0:T(8,128)} %bitcast.18, f32[56,56]{1,0:T(8,128)} %bitcast.19, s32[2,10]{1,0:T(2,128)} %bitcast.20), custom_call_target="tpu_custom_call" | custom-call | tf_op jit(solution)/shard_map/pack/pallas_call | solution.py:87
  2.2 7.8 %all-to-all-start = ((f32[8,56,640]{2,1,0:T(8,128)}), f32[8,56,640]{2,1,0:T(8,128)S(1)}, u32[]{:S(2)}, u32[]{:S(2)}) async-start(f32[8,56,640]{2,1,0:T(8,128)} %pack.1), calls=%async_computation | async-start | bytes 2293760 | tf_op jit(solution)/shard_map/all_to_all | solution.py:365
  11.3 4.7 %collective-permute-start = (f32[2,56,128]{2,1,0:T(8,128)S(1)}, f32[2,56,128]{2,1,0:T(8,128)S(1)}, u32[]{:S(2)}, u32[]{:S(2)}) collective-permute-start(f32[2,56,128]{2,1,0:T(8,128)S(1)} %get-tuple-element.22), channel_id=1, source_target_pairs={{0,32},{32,0},{1,33},{33,1},{2,34},{34,2},{3,35},{35,3},{4,36},{36... | collective-permute-start | bytes 172040 | tf_op jit(solution)/shard_map/ppermute | solution.py:383
  16.0 20.5 %all-gather = f32[896,128]{1,0:T(8,128)S(1)} all-gather(f32[56,128]{1,0:T(8,128)S(1)} %get-tuple-element.23), channel_id=2, replica_groups=mesh['x'=4,'zl'=2,'core'=2,'zh'=4,'y'=8] {'x','zl','core'}, dimensions={0}, use_global_device_ids=true | all-gather | bytes 487424 | tf_op jit(solution)/shard_map/all_gather | solution.py:382
  37.9 1.6 all-to-all-done.in_ref
  39.5 4.2 %collective-permute-start.1 = (f32[8,56,640]{2,1,0:T(8,128)S(1)}, f32[8,56,640]{2,1,0:T(8,128)S(1)}, u32[]{:S(2)}, u32[]{:S(2)}) collective-permute-start(f32[8,56,640]{2,1,0:T(8,128)S(1)} %all-to-all-done.in_ref), channel_id=1, source_target_pairs={{0,32},{32,0},{1,33},{33,1},{2,34},{34,2},{3,35},{35,3},{4,36},{36... | collective-permute-start | bytes 3440648 | tf_op jit(solution)/shard_map/ppermute | solution.py:387
  47.2 4.7 %mirror.3 = f32[8,56,128]{2,1,0:T(8,128)} custom-call(s32[4]{0:T(128)S(1)} %pad_add_fusion.me_ref, s32[8,128]{1,0:T(8,128)S(1)} %get-tuple-element.25.pos_a_ref, s32[8,128]{1,0:T(8,128)S(1)} %get-tuple-element.26.pos_b_ref, f32[4,56,128]{2,1,0:T(8,128)S(1)} %join_cores.1.rows_ref, bf16[88,56,128]{2,1,0:T(8,128)(2,1)S(1)} %get-tuple-element.28.blocks_a_ref, ...), custom_call_target="tpu_custom_call" | custom-call | flops 200000000 | bytes 4000000 | tf_op jit(solution)/shard_map/mirror/pallas_call | solution.py:293
  51.8 5.8 %all-to-all-start.1 = ((f32[8,56,128]{2,1,0:T(8,128)}), f32[8,56,128]{2,1,0:T(8,128)S(1)}, u32[]{:S(2)}, u32[]{:S(2)}) async-start(f32[8,56,128]{2,1,0:T(8,128)} %mirror.3), calls=%async_computation.1 | async-start | bytes 458752 | tf_op jit(solution)/shard_map/all_to_all | solution.py:365
  57.7 4.5 %direct.3 = f32[4,56,128]{2,1,0:T(8,128)S(1)} custom-call(s32[4]{0:T(128)S(1)} %pad_add_fusion.me_ref, s32[8,128]{1,0:T(8,128)S(1)} %get-tuple-element.25.pos_a_ref, s32[8,128]{1,0:T(8,128)S(1)} %get-tuple-element.26.pos_b_ref, f32[8,56,128]{2,1,0:T(8,128)S(1)} %pick_half.1.cols_ref, bf16[88,56,128]{2,1,0:T(8,128)(2,1)S(1)} %get-tuple-element.28.blocks_a_ref, ...), custom_call_target="tpu_custom_call" | custom-call | flops 200000000 | bytes 4000000 | tf_op jit(solution)/shard_map/direct/pallas_call | solution.py:293
  62.2 1.8 all-to-all-done.1
  64.9 9.1 %all-to-all-start.2 = ((f32[4,4,56,128]{3,2,1,0:T(8,128)}), f32[4,4,56,128]{3,2,1,0:T(8,128)S(1)}, u32[]{:S(2)}, u32[]{:S(2)}) async-start(f32[4,4,56,128]{3,2,1,0:T(8,128)} %broadcast_in_dim.68), calls=%async_computation.2 | async-start | bytes 917504 | tf_op jit(solution)/shard_map/all_to_all | solution.py:365
  74.1 12.0 %all-to-all-done.2 = f32[4,4,56,128]{3,2,1,0:T(8,128)S(1)} async-done(((f32[4,4,56,128]{3,2,1,0:T(8,128)}), f32[4,4,56,128]{3,2,1,0:T(8,128)S(1)}, u32[]{:S(2)}, u32[]{:S(2)}) %all-to-all-start.2) | async-done | bytes 458784 | tf_op jit(solution)/shard_map/all_to_all | solution.py:365
  86.8 5.9 %all-to-all-start.3 = ((f32[8,56,128]{2,1,0:T(8,128)}), f32[8,56,128]{2,1,0:T(8,128)S(1)}, u32[]{:S(2)}, u32[]{:S(2)}) async-start(f32[8,56,128]{2,1,0:T(8,128)} %broadcast_in_dim.70), calls=%async_computation.3 | async-start | bytes 458752 | tf_op jit(solution)/shard_map/all_to_all | solution.py:365
  92.8 4.7 %mirror.4 = f32[8,56,128]{2,1,0:T(8,128)} custom-call(s32[4]{0:T(128)S(1)} %pad_add_fusion.me_ref, s32[8,128]{1,0:T(8,128)S(1)} %get-tuple-element.25.pos_a_ref, s32[8,128]{1,0:T(8,128)S(1)} %get-tuple-element.26.pos_b_ref, f32[4,56,128]{2,1,0:T(8,128)S(1)} %fusion.rows_ref.previous_ref, bf16[88,56,128]{2,1,0:T(8,128)(2,1)S(1)} %get-tuple-element.28.blocks_a_ref, ...), custom_call_target="tpu_custom_call" | custom-call | flops 200000000 | bytes 4000000 | tf_op jit(solution)/shard_map/mirror/pallas_call | solution.py:293
  98.7 4.0 %all-to-all-start.4 = ((f32[8,56,128]{2,1,0:T(8,128)}), f32[8,56,128]{2,1,0:T(8,128)}, u32[]{:S(2)}, u32[]{:S(2)}) async-start(f32[8,56,128]{2,1,0:T(8,128)} %mirror.4), calls=%async_computation.4 | async-start | bytes 458752 | tf_op jit(solution)/shard_map/all_to_all | solution.py:365
  102.8 4.5 %direct.4 = f32[4,56,128]{2,1,0:T(8,128)S(1)} custom-call(s32[4]{0:T(128)S(1)} %pad_add_fusion.me_ref, s32[8,128]{1,0:T(8,128)S(1)} %get-tuple-element.25.pos_a_ref, s32[8,128]{1,0:T(8,128)S(1)} %get-tuple-element.26.pos_b_ref, f32[8,56,128]{2,1,0:T(8,128)S(1)} %all-to-all-done.3.cols_ref, bf16[88,56,128]{2,1,0:T(8,128)(2,1)S(1)} %get-tuple-element.28.blocks_a_ref, ...), custom_call_target="tpu_custom_call" | custom-call | flops 200000000 | bytes 4000000 | tf_op jit(solution)/shard_map/direct/pallas_call | solution.py:293
  109.8 13.2 %all_to_all.50 = f32[4,4,56,128]{3,2,1,0:T(8,128)S(1)} all-to-all(f32[4,4,56,128]{3,2,1,0:T(8,128)S(1)} %broadcast_in_dim.72), channel_id=1, replica_groups=mesh['x'=4,'zl'=2,'core'=2,'zh'=4,'y'=8] {'zh'}, dimensions={0} | all-to-all | bytes 917504 | tf_op jit(solution)/shard_map/all_to_all | solution.py:365
  123.9 7.0 %all-to-all-start.6 = ((f32[8,56,128]{2,1,0:T(8,128)}), f32[8,56,128]{2,1,0:T(8,128)S(1)}, u32[]{:S(2)}, u32[]{:S(2)}) async-start(f32[8,56,128]{2,1,0:T(8,128)} %broadcast_in_dim.74), calls=%async_computation.6 | async-start | bytes 458752 | tf_op jit(solution)/shard_map/all_to_all | solution.py:365
  130.9 4.7 %mirror.5 = f32[8,56,128]{2,1,0:T(8,128)} custom-call(s32[4]{0:T(128)S(1)} %pad_add_fusion.me_ref, s32[8,128]{1,0:T(8,128)S(1)} %get-tuple-element.25.pos_a_ref, s32[8,128]{1,0:T(8,128)S(1)} %get-tuple-element.26.pos_b_ref, f32[4,56,128]{2,1,0:T(8,128)S(1)} %multiply_subtract_fusion.rows_ref.current_ref, ...), custom_call_target="tpu_custom_call" | custom-call | flops 200000000 | bytes 4000000 | tf_op jit(solution)/shard_map/mirror/pallas_call | solution.py:293
  136.8 3.8 %all-to-all-start.7 = ((f32[8,56,128]{2,1,0:T(8,128)}), f32[8,56,128]{2,1,0:T(8,128)S(1)}, u32[]{:S(2)}, u32[]{:S(2)}) async-start(f32[8,56,128]{2,1,0:T(8,128)} %mirror.5), calls=%async_computation.7 | async-start | bytes 458752 | tf_op jit(solution)/shard_map/all_to_all | solution.py:365
  140.7 4.5 %direct.5.rows_ref = f32[4,56,128]{2,1,0:T(8,128)S(1)} custom-call(s32[4]{0:T(128)S(1)} %pad_add_fusion.me_ref, s32[8,128]{1,0:T(8,128)S(1)} %get-tuple-element.25.pos_a_ref, s32[8,128]{1,0:T(8,128)S(1)} %get-tuple-element.26.pos_b_ref, f32[8,56,128]{2,1,0:T(8,128)S(1)} %all-to-all-done.6.cols_ref, bf16[88,56,128]{2,1,0:T(8,128)(2,1)S(1)} %get-tuple-element.28.blocks_a_ref, ...), custom_call_target="tpu_custom_call" | custom-call | flops 200000000 | bytes 4000000 | tf_op jit(solution)/shard_map/direct/pallas_call | solution.py:293
  147.7 16.9 %all_to_all.51 = f32[8,56,128]{2,1,0:T(8,128)S(1)} all-to-all(f32[8,56,128]{2,1,0:T(8,128)S(1)} %finish.1), channel_id=1, replica_groups=mesh['x'=4,'zl'=2,'core'=2,'zh'=4,'y'=8] {'core','zh'}, dimensions={0} | all-to-all | bytes 458752 | tf_op jit(solution)/shard_map/all_to_all | solution.py:365
  164.6 28.4 %all_to_all.52 = f32[32,56,128]{2,1,0:T(8,128)S(1)} all-to-all(f32[32,56,128]{2,1,0:T(8,128)S(1)} %broadcast_in_dim.75), channel_id=1, replica_groups=mesh['x'=4,'zl'=2,'core'=2,'zh'=4,'y'=8] {'zh','y'}, dimensions={0} | all-to-all | bytes 1835008 | tf_op jit(solution)/shard_map/all_to_all | solution.py:365
  193.0 2.3 %spread.1 = f32[32,56,128]{2,1,0:T(8,128)} custom-call(f32[4,8,56,128]{3,2,1,0:T(8,128)S(1)} %bitcast.15), custom_call_target="tpu_custom_call" | custom-call | tf_op jit(solution)/shard_map/spread/pallas_call | solution.py:353
  (33 shorter events, 16.2 us)
Async XLA Ops:
  2.2 7.9 %copy-start = (f32[1792,128]{1,0:T(8,128)S(1)}, f32[1792,128]{1,0:T(8,128)}, u32[]{:S(2)}) copy-start(f32[1792,128]{1,0:T(8,128)} %param.4) | copy-start | bytes 2752516
  2.2 37.3 %all-to-all-start = ((f32[8,56,640]{2,1,0:T(8,128)}), f32[8,56,640]{2,1,0:T(8,128)S(1)}, u32[]{:S(2)}, u32[]{:S(2)}) async-start(f32[8,56,640]{2,1,0:T(8,128)} %pack.1), calls=%async_computation | async-start | bytes 2293760 | tf_op jit(solution)/shard_map/all_to_all | solution.py:365
  11.3 25.9 %collective-permute-start = (f32[2,56,128]{2,1,0:T(8,128)S(1)}, f32[2,56,128]{2,1,0:T(8,128)S(1)}, u32[]{:S(2)}, u32[]{:S(2)}) collective-permute-start(f32[2,56,128]{2,1,0:T(8,128)S(1)} %get-tuple-element.22), channel_id=1, source_target_pairs={{0,32},{32,0},{1,33},{33,1},{2,34},{34,2},{3,35},{35,3},{4,36},{36... | collective-permute-start | bytes 172040 | tf_op jit(solution)/shard_map/ppermute | solution.py:383
  39.5 6.6 %collective-permute-start.1 = (f32[8,56,640]{2,1,0:T(8,128)S(1)}, f32[8,56,640]{2,1,0:T(8,128)S(1)}, u32[]{:S(2)}, u32[]{:S(2)}) collective-permute-start(f32[8,56,640]{2,1,0:T(8,128)S(1)} %all-to-all-done.in_ref), channel_id=1, source_target_pairs={{0,32},{32,0},{1,33},{33,1},{2,34},{34,2},{3,35},{35,3},{4,36},{36... | collective-permute-start | bytes 3440648 | tf_op jit(solution)/shard_map/ppermute | solution.py:387
  51.8 12.2 %all-to-all-start.1 = ((f32[8,56,128]{2,1,0:T(8,128)}), f32[8,56,128]{2,1,0:T(8,128)S(1)}, u32[]{:S(2)}, u32[]{:S(2)}) async-start(f32[8,56,128]{2,1,0:T(8,128)} %mirror.3), calls=%async_computation.1 | async-start | bytes 458752 | tf_op jit(solution)/shard_map/all_to_all | solution.py:365
  64.9 21.1 %all-to-all-start.2 = ((f32[4,4,56,128]{3,2,1,0:T(8,128)}), f32[4,4,56,128]{3,2,1,0:T(8,128)S(1)}, u32[]{:S(2)}, u32[]{:S(2)}) async-start(f32[4,4,56,128]{3,2,1,0:T(8,128)} %broadcast_in_dim.68), calls=%async_computation.2 | async-start | bytes 917504 | tf_op jit(solution)/shard_map/all_to_all | solution.py:365
  86.8 11.9 %all-to-all-start.3 = ((f32[8,56,128]{2,1,0:T(8,128)}), f32[8,56,128]{2,1,0:T(8,128)S(1)}, u32[]{:S(2)}, u32[]{:S(2)}) async-start(f32[8,56,128]{2,1,0:T(8,128)} %broadcast_in_dim.70), calls=%async_computation.3 | async-start | bytes 458752 | tf_op jit(solution)/shard_map/all_to_all | solution.py:365
  98.7 10.0 %all-to-all-start.4 = ((f32[8,56,128]{2,1,0:T(8,128)}), f32[8,56,128]{2,1,0:T(8,128)}, u32[]{:S(2)}, u32[]{:S(2)}) async-start(f32[8,56,128]{2,1,0:T(8,128)} %mirror.4), calls=%async_computation.4 | async-start | bytes 458752 | tf_op jit(solution)/shard_map/all_to_all | solution.py:365
  123.9 13.0 %all-to-all-start.6 = ((f32[8,56,128]{2,1,0:T(8,128)}), f32[8,56,128]{2,1,0:T(8,128)S(1)}, u32[]{:S(2)}, u32[]{:S(2)}) async-start(f32[8,56,128]{2,1,0:T(8,128)} %broadcast_in_dim.74), calls=%async_computation.6 | async-start | bytes 458752 | tf_op jit(solution)/shard_map/all_to_all | solution.py:365
  136.8 9.8 %all-to-all-start.7 = ((f32[8,56,128]{2,1,0:T(8,128)}), f32[8,56,128]{2,1,0:T(8,128)S(1)}, u32[]{:S(2)}, u32[]{:S(2)}) async-start(f32[8,56,128]{2,1,0:T(8,128)} %mirror.5), calls=%async_computation.7 | async-start | bytes 458752 | tf_op jit(solution)/shard_map/all_to_all | solution.py:365

commit v8 on v7

--- a/solution.py
+++ b/solution.py
@@ -334,31 +334,62 @@
     )(me, rows, own, current, previous)
 
 
-def spread_kernel(in_ref, out_ref):
-    lane = lane_iota()
-    x = [in_ref[0, y] for y in range(N_Y)]
-    for d in (4, 2, 1):
-        upper = (lane & (16 * d)) != 0
-        for a in range(N_Y):
-            if a & d:
-                continue
-            low, high = x[a], x[a + d]
-            x[a] = jnp.where(upper, pltpu.roll(high, 16 * d, 1), low)
-            x[a + d] = jnp.where(upper, high, pltpu.roll(low, LANES - 16 * d, 1))
-    for y in range(N_Y):
-        out_ref[y] = x[y]
+def spread_kernel(in_ref, out_hbm, held, sems):
+    lane = lane_iota()
+    copies = []
+    for z in range(N_ZH):
+        x = [in_ref[z, y] for y in range(N_Y)]
+        for d in (4, 2, 1):
+            upper = (lane & (16 * d)) != 0
+            for a in range(N_Y):
+                if a & d:
+                    continue
+                low, high = x[a], x[a + d]
+                x[a] = jnp.where(upper, pltpu.roll(high, 16 * d, 1), low)
+                x[a + d] = jnp.where(upper, high, pltpu.roll(low, LANES - 16 * d, 1))
+        for y in range(N_Y):
+            held[z, y] = x[y]
+        copy = pltpu.make_async_copy(held.at[z], out_hbm.at[pl.ds(z * N_Y, N_Y)], sems.at[z])
+        copy.start()
+        copies.append(copy)
+    for copy in copies:
+        copy.wait()
 
 
 def spread(gathered):
     return pl.pallas_call(
         spread_kernel,
         out_shape=jax.ShapeDtypeStruct((N_ZH * N_Y, ORB, LANES), f32),
-        grid=(N_ZH,),
-        in_specs=[pl.BlockSpec((1, N_Y, ORB, LANES), lambda z: (z, 0, 0, 0))],
-        out_specs=pl.BlockSpec((N_Y, ORB, LANES), lambda z: (z, 0, 0)),
+        in_specs=vmem(1),
+        out_specs=pl.BlockSpec(memory_space=pl.ANY),
+        scratch_shapes=[
+            pltpu.VMEM((N_ZH, N_Y, ORB, LANES), f32),
+            pltpu.SemaphoreType.DMA((N_ZH,)),
+        ],
         compiler_params=params(),
         name="spread",
     )(gathered)
+
+
+def merge_kernel(me_ref, rows_ref, cols_ref, out_ref):
+    own = cols_ref[0]
+    for r in range(1, N_R):
+        own = own + cols_ref[r]
+    for z in range(N_ZH):
+        total = rows_ref[z] + jnp.where(me_ref[1] == z, own, 0.0)
+        for copy in range(N_ZH):
+            out_ref[copy, z] = total
+
+
+def merge(me, rows, cols):
+    return pl.pallas_call(
+        merge_kernel,
+        out_shape=jax.ShapeDtypeStruct((N_ZH, N_ZH, ORB, LANES), f32),
+        in_specs=[pl.BlockSpec(memory_space=pltpu.SMEM)] + vmem(2),
+        out_specs=vmem(1)[0],
+        compiler_params=params(),
+        name="merge",
+    )(me, rows, cols)
 
 
 def exchange(x, axes):
@@ -387,24 +418,21 @@
     blocks_b, pos_b = unpack(lax.ppermute(packed, "core", swap))
     where, blocks = (me, pos_a, pos_b), (blocks_a, blocks_b)
 
-    at_own = (lax.broadcasted_iota(jnp.int32, (N_ZH, 1, 1), 0) == zh)
     previous = None
     for step in range(DEGREE):
         out_cols = product(mirror_kernel, "mirror", where, current, blocks, N_R)
         out_cols, cols = lax.optimization_barrier((out_cols, cols))
         got_cols = exchange(out_cols, ROW_AX)
         out_rows = product(direct_kernel, "direct", where, cols, blocks, N_ZH)
-        own = jnp.sum(got_cols, 0)
         if step == DEGREE - 1:
             break
-        partial = out_rows + jnp.where(at_own, own[None], 0.0)
-        image = jnp.sum(gather(partial, "zh", N_ZH).reshape(N_ZH, N_ZH, ORB, LANES), 0)
+        image = jnp.sum(exchange(merge(me, out_rows, got_cols), "zh"), 0)
         shifted = (image - centre * current) / half_width
         following = shifted if previous is None else 2.0 * shifted - previous
         previous, current = current, following
         cols = gather(lax.dynamic_index_in_dim(current, zh, 0, keepdims=False), ROW_AX, N_R)
 
-    result = jnp.sum(exchange(finish(me, out_rows, own, current, previous), ("core", "zh")), 0)
+    result = jnp.sum(exchange(finish(me, out_rows, jnp.sum(got_cols, 0), current, previous), ("core", "zh")), 0)
     result = gather(result, ("zh", "y"), N_ZH * N_Y).reshape(N_ZH, N_Y, ORB, LANES)
     return spread(result).reshape(vectors.shape)
 

time: 199 us -> 198 us (level)
  no operation moved by 1% of the time
where the time goes in v8:
time: 198 us; the launch traced here: 195 us
  blocking collectives  78.8 us (40%)
  starting transfers between devices  52.6 us (27%)
  Pallas kernels  39.1 us (20%)
  waiting for transfers between devices  22.3 us (11%)
    all_to_all x3, blocking collectives, exchange(): return lax.all_to_all(x, axes, split_axis=0, concat_axis=0, tiled=True)  58.4 us
    all_to_all x7, starting transfers between devices, exchange(): return lax.all_to_all(x, axes, split_axis=0, concat_axis=0, tiled=True)  43.6 us
    pallas_call x6, Pallas kernels, product(): pl.pallas_call(kernel, out_shape=jax.ShapeDtypeStruct((chunks, ORB, LANES...  27.5 us
    all_to_all x7, waiting for transfers between devices, exchange(): return lax.all_to_all(x, axes, split_axis=0, concat_axis=0, tiled=True)  20.9 us
    all_gather x1, blocking collectives, body(): lax.all_gather(own, ('x', 'zl', 'core'), axis=0, tiled=False)  20.5 us
    ppermute x1, starting transfers between devices, body(): current = join_cores(me, mine, lax.ppermute(other, 'core', swap))  4.72 us
    ppermute x1, starting transfers between devices, body(): blocks_b, pos_b = unpack(lax.ppermute(packed, 'core', swap))  4.23 us
  transfers between devices with their start and end apart: 9, of which 8 were waited for; matrix products, arithmetic and copies ran while one was open for 0% of the time, Pallas kernels for 14%

profile of v8, /device:TPU:1, one launch (start us, length us, event | category | flops | bytes accessed | tf_op | source)
XLA Modules:
  0.0 194.6 jit_solution(15652008880116881634)
XLA Ops:
  0.0 2.2 %pack.1 = f32[8,56,640]{2,1,0:T(8,128)} custom-call(f32[10,56,56]{2,1,0:T(8,128)} %bitcast.18, f32[56,56]{1,0:T(8,128)} %bitcast.19, s32[2,10]{1,0:T(2,128)} %bitcast.20), custom_call_target="tpu_custom_call" | custom-call | tf_op jit(solution)/shard_map/pack/pallas_call | solution.py:87
  2.2 7.8 %all-to-all-start = ((f32[8,56,640]{2,1,0:T(8,128)}), f32[8,56,640]{2,1,0:T(8,128)S(1)}, u32[]{:S(2)}, u32[]{:S(2)}) async-start(f32[8,56,640]{2,1,0:T(8,128)} %pack.1), calls=%async_computation | async-start | bytes 2293760 | tf_op jit(solution)/shard_map/all_to_all | solution.py:396
  11.3 4.7 %collective-permute-start = (f32[2,56,128]{2,1,0:T(8,128)S(1)}, f32[2,56,128]{2,1,0:T(8,128)S(1)}, u32[]{:S(2)}, u32[]{:S(2)}) collective-permute-start(f32[2,56,128]{2,1,0:T(8,128)S(1)} %get-tuple-element.22), channel_id=1, source_target_pairs={{0,32},{32,0},{1,33},{33,1},{2,34},{34,2},{3,35},{35,3},{4,36},{36... | collective-permute-start | bytes 172040 | tf_op jit(solution)/shard_map/ppermute | solution.py:414
  16.1 20.5 %all-gather = f32[896,128]{1,0:T(8,128)S(1)} all-gather(f32[56,128]{1,0:T(8,128)S(1)} %get-tuple-element.23), channel_id=2, replica_groups=mesh['x'=4,'zl'=2,'core'=2,'zh'=4,'y'=8] {'x','zl','core'}, dimensions={0}, use_global_device_ids=true | all-gather | bytes 487424 | tf_op jit(solution)/shard_map/all_gather | solution.py:413
  37.9 1.6 all-to-all-done.in_ref
  39.5 4.2 %collective-permute-start.1 = (f32[8,56,640]{2,1,0:T(8,128)S(1)}, f32[8,56,640]{2,1,0:T(8,128)S(1)}, u32[]{:S(2)}, u32[]{:S(2)}) collective-permute-start(f32[8,56,640]{2,1,0:T(8,128)S(1)} %all-to-all-done.in_ref), channel_id=1, source_target_pairs={{0,32},{32,0},{1,33},{33,1},{2,34},{34,2},{3,35},{35,3},{4,36},{36... | collective-permute-start | bytes 3440648 | tf_op jit(solution)/shard_map/ppermute | solution.py:418
  47.2 4.7 %mirror.3 = f32[8,56,128]{2,1,0:T(8,128)} custom-call(s32[4]{0:T(128)S(1)} %pad_add_fusion.me_ref, s32[8,128]{1,0:T(8,128)S(1)} %get-tuple-element.25.pos_a_ref, s32[8,128]{1,0:T(8,128)S(1)} %get-tuple-element.26.pos_b_ref, f32[4,56,128]{2,1,0:T(8,128)S(1)} %join_cores.1.rows_ref, bf16[88,56,128]{2,1,0:T(8,128)(2,1)S(1)} %get-tuple-element.28.blocks_a_ref, ...), custom_call_target="tpu_custom_call" | custom-call | flops 200000000 | bytes 4000000 | tf_op jit(solution)/shard_map/mirror/pallas_call | solution.py:293
  51.9 5.9 %all-to-all-start.1 = ((f32[8,56,128]{2,1,0:T(8,128)}), f32[8,56,128]{2,1,0:T(8,128)S(1)}, u32[]{:S(2)}, u32[]{:S(2)}) async-start(f32[8,56,128]{2,1,0:T(8,128)} %mirror.3), calls=%async_computation.1 | async-start | bytes 458752 | tf_op jit(solution)/shard_map/all_to_all | solution.py:396
  57.7 4.5 %direct.3.rows_ref = f32[4,56,128]{2,1,0:T(8,128)S(1)} custom-call(s32[4]{0:T(128)S(1)} %pad_add_fusion.me_ref, s32[8,128]{1,0:T(8,128)S(1)} %get-tuple-element.25.pos_a_ref, s32[8,128]{1,0:T(8,128)S(1)} %get-tuple-element.26.pos_b_ref, f32[8,56,128]{2,1,0:T(8,128)S(1)} %pick_half.1.cols_ref, bf16[88,56,128]{2,1,0:T(8,128)(2,1)S(1)} %get-tuple-element.28.blocks_a_ref, ...), custom_call_target="tpu_custom_call" | custom-call | flops 200000000 | bytes 4000000 | tf_op jit(solution)/shard_map/direct/pallas_call | solution.py:293
  62.2 1.8 all-to-all-done.1.cols_ref
  65.4 9.1 %all-to-all-start.2 = ((f32[4,4,56,128]{3,2,1,0:T(8,128)}), f32[4,4,56,128]{3,2,1,0:T(8,128)S(1)}, u32[]{:S(2)}, u32[]{:S(2)}) async-start(f32[4,4,56,128]{3,2,1,0:T(8,128)} %merge.2), calls=%async_computation.2 | async-start | bytes 917504 | tf_op jit(solution)/shard_map/all_to_all | solution.py:396
  74.5 12.0 %all-to-all-done.2 = f32[4,4,56,128]{3,2,1,0:T(8,128)S(1)} async-done(((f32[4,4,56,128]{3,2,1,0:T(8,128)}), f32[4,4,56,128]{3,2,1,0:T(8,128)S(1)}, u32[]{:S(2)}, u32[]{:S(2)}) %all-to-all-start.2) | async-done | bytes 458784 | tf_op jit(solution)/shard_map/all_to_all | solution.py:396
  87.3 5.9 %all-to-all-start.3 = ((f32[8,56,128]{2,1,0:T(8,128)}), f32[8,56,128]{2,1,0:T(8,128)S(1)}, u32[]{:S(2)}, u32[]{:S(2)}) async-start(f32[8,56,128]{2,1,0:T(8,128)} %broadcast_in_dim.11), calls=%async_computation.3 | async-start | bytes 458752 | tf_op jit(solution)/shard_map/all_to_all | solution.py:396
  93.2 4.7 %mirror.4 = f32[8,56,128]{2,1,0:T(8,128)} custom-call(s32[4]{0:T(128)S(1)} %pad_add_fusion.me_ref, s32[8,128]{1,0:T(8,128)S(1)} %get-tuple-element.25.pos_a_ref, s32[8,128]{1,0:T(8,128)S(1)} %get-tuple-element.26.pos_b_ref, f32[4,56,128]{2,1,0:T(8,128)S(1)} %fusion.rows_ref.previous_ref, bf16[88,56,128]{2,1,0:T(8,128)(2,1)S(1)} %get-tuple-element.28.blocks_a_ref, ...), custom_call_target="tpu_custom_call" | custom-call | flops 200000000 | bytes 4000000 | tf_op jit(solution)/shard_map/mirror/pallas_call | solution.py:293
  99.2 3.8 %all-to-all-start.4 = ((f32[8,56,128]{2,1,0:T(8,128)}), f32[8,56,128]{2,1,0:T(8,128)S(1)}, u32[]{:S(2)}, u32[]{:S(2)}) async-start(f32[8,56,128]{2,1,0:T(8,128)} %mirror.4), calls=%async_computation.4 | async-start | bytes 458752 | tf_op jit(solution)/shard_map/all_to_all | solution.py:396
  103.0 4.5 %direct.4.rows_ref = f32[4,56,128]{2,1,0:T(8,128)S(1)} custom-call(s32[4]{0:T(128)S(1)} %pad_add_fusion.me_ref, s32[8,128]{1,0:T(8,128)S(1)} %get-tuple-element.25.pos_a_ref, s32[8,128]{1,0:T(8,128)S(1)} %get-tuple-element.26.pos_b_ref, f32[8,56,128]{2,1,0:T(8,128)S(1)} %all-to-all-done.3.cols_ref, bf16[88,56,128]{2,1,0:T(8,128)(2,1)S(1)} %get-tuple-element.28.blocks_a_ref, ...), custom_call_target="tpu_custom_call" | custom-call | flops 200000000 | bytes 4000000 | tf_op jit(solution)/shard_map/direct/pallas_call | solution.py:293
  109.6 13.7 %all_to_all.50 = f32[4,4,56,128]{3,2,1,0:T(8,128)S(1)} all-to-all(f32[4,4,56,128]{3,2,1,0:T(8,128)S(1)} %merge.3), channel_id=1, replica_groups=mesh['x'=4,'zl'=2,'core'=2,'zh'=4,'y'=8] {'zh'}, dimensions={0} | all-to-all | bytes 917504 | tf_op jit(solution)/shard_map/all_to_all | solution.py:396
  124.1 7.3 %all-to-all-start.6 = ((f32[8,56,128]{2,1,0:T(8,128)}), f32[8,56,128]{2,1,0:T(8,128)S(1)}, u32[]{:S(2)}, u32[]{:S(2)}) async-start(f32[8,56,128]{2,1,0:T(8,128)} %broadcast_in_dim.25), calls=%async_computation.6 | async-start | bytes 458752 | tf_op jit(solution)/shard_map/all_to_all | solution.py:396
  131.4 4.7 %mirror.5 = f32[8,56,128]{2,1,0:T(8,128)} custom-call(s32[4]{0:T(128)S(1)} %pad_add_fusion.me_ref, s32[8,128]{1,0:T(8,128)S(1)} %get-tuple-element.25.pos_a_ref, s32[8,128]{1,0:T(8,128)S(1)} %get-tuple-element.26.pos_b_ref, f32[4,56,128]{2,1,0:T(8,128)S(1)} %multiply_subtract_fusion.rows_ref.current_ref, ...), custom_call_target="tpu_custom_call" | custom-call | flops 200000000 | bytes 4000000 | tf_op jit(solution)/shard_map/mirror/pallas_call | solution.py:293
  137.4 3.8 %all-to-all-start.7 = ((f32[8,56,128]{2,1,0:T(8,128)}), f32[8,56,128]{2,1,0:T(8,128)S(1)}, u32[]{:S(2)}, u32[]{:S(2)}) async-start(f32[8,56,128]{2,1,0:T(8,128)} %mirror.5), calls=%async_computation.7 | async-start | bytes 458752 | tf_op jit(solution)/shard_map/all_to_all | solution.py:396
  141.2 4.5 %direct.5.rows_ref = f32[4,56,128]{2,1,0:T(8,128)S(1)} custom-call(s32[4]{0:T(128)S(1)} %pad_add_fusion.me_ref, s32[8,128]{1,0:T(8,128)S(1)} %get-tuple-element.25.pos_a_ref, s32[8,128]{1,0:T(8,128)S(1)} %get-tuple-element.26.pos_b_ref, f32[8,56,128]{2,1,0:T(8,128)S(1)} %all-to-all-done.6.cols_ref, bf16[88,56,128]{2,1,0:T(8,128)(2,1)S(1)} %get-tuple-element.28.blocks_a_ref, ...), custom_call_target="tpu_custom_call" | custom-call | flops 200000000 | bytes 4000000 | tf_op jit(solution)/shard_map/direct/pallas_call | solution.py:293
  148.2 16.2 %all_to_all.51 = f32[8,56,128]{2,1,0:T(8,128)S(1)} all-to-all(f32[8,56,128]{2,1,0:T(8,128)S(1)} %finish.1), channel_id=1, replica_groups=mesh['x'=4,'zl'=2,'core'=2,'zh'=4,'y'=8] {'core','zh'}, dimensions={0} | all-to-all | bytes 458752 | tf_op jit(solution)/shard_map/all_to_all | solution.py:396
  164.5 28.4 %all_to_all.52 = f32[32,56,128]{2,1,0:T(8,128)S(1)} all-to-all(f32[32,56,128]{2,1,0:T(8,128)S(1)} %broadcast_in_dim.26), channel_id=1, replica_groups=mesh['x'=4,'zl'=2,'core'=2,'zh'=4,'y'=8] {'zh','y'}, dimensions={0} | all-to-all | bytes 1835008 | tf_op jit(solution)/shard_map/all_to_all | solution.py:396
  192.9 1.7 spread.1
  (28 shorter events, 16.2 us)
Async XLA Ops:
  2.2 7.9 %copy-start = (f32[1792,128]{1,0:T(8,128)S(1)}, f32[1792,128]{1,0:T(8,128)}, u32[]{:S(2)}) copy-start(f32[1792,128]{1,0:T(8,128)} %param.4) | copy-start | bytes 2752516
  2.2 37.3 %all-to-all-start = ((f32[8,56,640]{2,1,0:T(8,128)}), f32[8,56,640]{2,1,0:T(8,128)S(1)}, u32[]{:S(2)}, u32[]{:S(2)}) async-start(f32[8,56,640]{2,1,0:T(8,128)} %pack.1), calls=%async_computation | async-start | bytes 2293760 | tf_op jit(solution)/shard_map/all_to_all | solution.py:396
  11.3 25.9 %collective-permute-start = (f32[2,56,128]{2,1,0:T(8,128)S(1)}, f32[2,56,128]{2,1,0:T(8,128)S(1)}, u32[]{:S(2)}, u32[]{:S(2)}) collective-permute-start(f32[2,56,128]{2,1,0:T(8,128)S(1)} %get-tuple-element.22), channel_id=1, source_target_pairs={{0,32},{32,0},{1,33},{33,1},{2,34},{34,2},{3,35},{35,3},{4,36},{36... | collective-permute-start | bytes 172040 | tf_op jit(solution)/shard_map/ppermute | solution.py:414
  39.5 6.6 %collective-permute-start.1 = (f32[8,56,640]{2,1,0:T(8,128)S(1)}, f32[8,56,640]{2,1,0:T(8,128)S(1)}, u32[]{:S(2)}, u32[]{:S(2)}) collective-permute-start(f32[8,56,640]{2,1,0:T(8,128)S(1)} %all-to-all-done.in_ref), channel_id=1, source_target_pairs={{0,32},{32,0},{1,33},{33,1},{2,34},{34,2},{3,35},{35,3},{4,36},{36... | collective-permute-start | bytes 3440648 | tf_op jit(solution)/shard_map/ppermute | solution.py:418
  51.9 12.2 %all-to-all-start.1 = ((f32[8,56,128]{2,1,0:T(8,128)}), f32[8,56,128]{2,1,0:T(8,128)S(1)}, u32[]{:S(2)}, u32[]{:S(2)}) async-start(f32[8,56,128]{2,1,0:T(8,128)} %mirror.3), calls=%async_computation.1 | async-start | bytes 458752 | tf_op jit(solution)/shard_map/all_to_all | solution.py:396
  65.4 21.1 %all-to-all-start.2 = ((f32[4,4,56,128]{3,2,1,0:T(8,128)}), f32[4,4,56,128]{3,2,1,0:T(8,128)S(1)}, u32[]{:S(2)}, u32[]{:S(2)}) async-start(f32[4,4,56,128]{3,2,1,0:T(8,128)} %merge.2), calls=%async_computation.2 | async-start | bytes 917504 | tf_op jit(solution)/shard_map/all_to_all | solution.py:396
  87.3 11.9 %all-to-all-start.3 = ((f32[8,56,128]{2,1,0:T(8,128)}), f32[8,56,128]{2,1,0:T(8,128)S(1)}, u32[]{:S(2)}, u32[]{:S(2)}) async-start(f32[8,56,128]{2,1,0:T(8,128)} %broadcast_in_dim.11), calls=%async_computation.3 | async-start | bytes 458752 | tf_op jit(solution)/shard_map/all_to_all | solution.py:396
  99.2 9.8 %all-to-all-start.4 = ((f32[8,56,128]{2,1,0:T(8,128)}), f32[8,56,128]{2,1,0:T(8,128)S(1)}, u32[]{:S(2)}, u32[]{:S(2)}) async-start(f32[8,56,128]{2,1,0:T(8,128)} %mirror.4), calls=%async_computation.4 | async-start | bytes 458752 | tf_op jit(solution)/shard_map/all_to_all | solution.py:396
  124.1 13.3 %all-to-all-start.6 = ((f32[8,56,128]{2,1,0:T(8,128)}), f32[8,56,128]{2,1,0:T(8,128)S(1)}, u32[]{:S(2)}, u32[]{:S(2)}) async-start(f32[8,56,128]{2,1,0:T(8,128)} %broadcast_in_dim.25), calls=%async_computation.6 | async-start | bytes 458752 | tf_op jit(solution)/shard_map/all_to_all | solution.py:396
  137.4 9.8 %all-to-all-start.7 = ((f32[8,56,128]{2,1,0:T(8,128)}), f32[8,56,128]{2,1,0:T(8,128)S(1)}, u32[]{:S(2)}, u32[]{:S(2)}) async-start(f32[8,56,128]{2,1,0:T(8,128)} %mirror.5), calls=%async_computation.7 | async-start | bytes 458752 | tf_op jit(solution)/shard_map/all_to_all | solution.py:396

commit v9 on v8

--- a/solution.py
+++ b/solution.py
@@ -246,16 +246,17 @@
     split_terms(rows_ref, v_ref)
     acc_ref[...] = jnp.zeros_like(acc_ref)
     core = me_ref[2]
-    for pos_ref, blocks_ref, core_s in ((pos_a_ref, blocks_a_ref, core), (pos_b_ref, blocks_b_ref, 1 - core)):
-
-        def one_source(s, carry, pos_ref=pos_ref, blocks_ref=blocks_ref, core_s=core_s):
-            for t in range(TILES):
+    parts = ((pos_a_ref, blocks_a_ref, core), (pos_b_ref, blocks_b_ref, 1 - core))
+
+    def one_source(s, carry):
+        for t in range(TILES):
+            for pos_ref, blocks_ref, core_s in parts:
                 row, col = row_col(pos_ref, core_s, s, t)
                 both = jnp.dot(v_ref[row][:, :ORB], blocks_ref[s * SLOTS + t], preferred_element_type=f32)
                 acc_ref[col] += both[:VS] + both[VS:]
-            return carry
-
-        lax.fori_loop(0, N_Y, one_source, 0)
+        return carry
+
+    lax.fori_loop(0, N_Y, one_source, 0)
     for chunk in range(out_ref.shape[0]):
         x = acc_ref[chunk * GROUPS : (chunk + 1) * GROUPS].reshape(LANES, LANES)
         x = x + pltpu.roll(x, 64, 1)
@@ -266,10 +267,11 @@
     split_terms(cols_ref, v_ref)
     acc_ref[...] = jnp.zeros_like(acc_ref)
     my_r, my_zh, core = me_ref[0], me_ref[1], me_ref[2]
-    for pos_ref, blocks_ref, core_s in ((pos_a_ref, blocks_a_ref, core), (pos_b_ref, blocks_b_ref, 1 - core)):
-
-        def one_source(s, carry, pos_ref=pos_ref, blocks_ref=blocks_ref, core_s=core_s):
-            for t in range(SLOTS):
+    parts = ((pos_a_ref, blocks_a_ref, core), (pos_b_ref, blocks_b_ref, 1 - core))
+
+    def one_source(s, carry):
+        for t in range(SLOTS):
+            for pos_ref, blocks_ref, core_s in parts:
                 if t < TILES:
                     row, col = row_col(pos_ref, core_s, s, t)
                 else:
@@ -280,9 +282,9 @@
                     preferred_element_type=f32,
                 )
                 acc_ref[row, :, 0:ORB] += both[:VS] + both[VS:]
-            return carry
-
-        lax.fori_loop(0, N_Y, one_source, 0)
+        return carry
+
+    lax.fori_loop(0, N_Y, one_source, 0)
     for chunk in range(out_ref.shape[0]):
         x = acc_ref[chunk * GROUPS : (chunk + 1) * GROUPS].reshape(LANES, LANES)
         out_ref[chunk] = x.T[:ORB]
@@ -392,6 +394,31 @@
     )(me, rows, cols)
 
 
+def advance_kernel(me_ref, got_ref, *refs):
+    *fields, out_ref, own_ref = refs
+    for z in range(N_ZH):
+        image = got_ref[0, z]
+        for source in range(1, N_ZH):
+            image = image + got_ref[source, z]
+        shifted = (image - centre * fields[0][z]) / half_width
+        out_ref[z] = shifted if len(fields) == 1 else 2.0 * shifted - fields[1][z]
+    own_ref[...] = out_ref[me_ref[1]]
+
+
+def advance(me, got, fields):
+    return pl.pallas_call(
+        advance_kernel,
+        out_shape=(
+            jax.ShapeDtypeStruct((N_ZH, ORB, LANES), f32),
+            jax.ShapeDtypeStruct((ORB, LANES), f32),
+        ),
+        in_specs=[pl.BlockSpec(memory_space=pltpu.SMEM)] + vmem(1 + len(fields)),
+        out_specs=tuple(vmem(2)),
+        compiler_params=params(),
+        name="advance",
+    )(me, got, *fields)
+
+
 def exchange(x, axes):
     return lax.all_to_all(x, axes, split_axis=0, concat_axis=0, tiled=True)
 
@@ -426,11 +453,10 @@
         out_rows = product(direct_kernel, "direct", where, cols, blocks, N_ZH)
         if step == DEGREE - 1:
             break
-        image = jnp.sum(exchange(merge(me, out_rows, got_cols), "zh"), 0)
-        shifted = (image - centre * current) / half_width
-        following = shifted if previous is None else 2.0 * shifted - previous
+        got = exchange(merge(me, out_rows, got_cols), "zh")
+        following, own = advance(me, got, (current,) if previous is None else (current, previous))
         previous, current = current, following
-        cols = gather(lax.dynamic_index_in_dim(current, zh, 0, keepdims=False), ROW_AX, N_R)
+        cols = gather(own, ROW_AX, N_R)
 
     result = jnp.sum(exchange(finish(me, out_rows, jnp.sum(got_cols, 0), current, previous), ("core", "zh")), 0)
     result = gather(result, ("zh", "y"), N_ZH * N_Y).reshape(N_ZH, N_Y, ORB, LANES)

time: 198 us -> 195 us (0.985)
  blocking collectives: 78.8 us -> 104 us
  starting transfers between devices: 52.6 us -> 38.1 us
  waiting for transfers between devices: 22.3 us -> 15.2 us
  Pallas kernels: 39.1 us -> 33.4 us
    all_to_all x3 -> x4, blocking collectives: 58.4 us -> 83.2 us  [exchange(): return lax.all_to_all(x, axes, split_axis=0, concat_axis=0, tiled=True)]
    all_to_all x7 -> x6, starting transfers between devices: 43.6 us -> 29.1 us  [exchange(): return lax.all_to_all(x, axes, split_axis=0, concat_axis=0, tiled=True)]
    all_to_all x7 -> x6, waiting for transfers between devices: 20.9 us -> 13.8 us  [exchange(): return lax.all_to_all(x, axes, split_axis=0, concat_axis=0, tiled=True)]
    pallas_call x6, Pallas kernels: 27.5 us -> 21.4 us  [product(): pl.pallas_call(kernel, out_shape=jax.ShapeDtypeStruct((chunks, ORB, LANES...]
  transfers between devices with their start and end apart: 9 -> 8, of which waited for: 8 -> 7; matrix products, arithmetic and copies ran while one was open for 0% -> 0% of each run, Pallas kernels for 14% -> 11%
where the time goes in v9:
time: 195 us; the launch traced here: 192 us
  blocking collectives  104 us (53%)
  starting transfers between devices  38.1 us (20%)
  Pallas kernels  33.4 us (17%)
  waiting for transfers between devices  15.2 us (8%)
    all_to_all x4, blocking collectives, exchange(): return lax.all_to_all(x, axes, split_axis=0, concat_axis=0, tiled=True)  83.2 us
    all_to_all x6, starting transfers between devices, exchange(): return lax.all_to_all(x, axes, split_axis=0, concat_axis=0, tiled=True)  29.1 us
    pallas_call x6, Pallas kernels, product(): pl.pallas_call(kernel, out_shape=jax.ShapeDtypeStruct((chunks, ORB, LANES...  21.4 us
    all_gather x1, blocking collectives, body(): lax.all_gather(own, ('x', 'zl', 'core'), axis=0, tiled=False)  20.5 us
    all_to_all x6, waiting for transfers between devices, exchange(): return lax.all_to_all(x, axes, split_axis=0, concat_axis=0, tiled=True)  13.8 us
    ppermute x1, starting transfers between devices, body(): current = join_cores(me, mine, lax.ppermute(other, 'core', swap))  4.72 us
    ppermute x1, starting transfers between devices, body(): blocks_b, pos_b = unpack(lax.ppermute(packed, 'core', swap))  4.23 us
  transfers between devices with their start and end apart: 8, of which 7 were waited for; matrix products, arithmetic and copies ran while one was open for 0% of the time, Pallas kernels for 11%

profile of v9, /device:TPU:1, one launch (start us, length us, event | category | flops | bytes accessed | tf_op | source)
XLA Modules:
  0.0 192.1 jit_solution(18442389124710396089)
XLA Ops:
  2.2 7.8 %all-to-all-start = ((f32[8,56,640]{2,1,0:T(8,128)}), f32[8,56,640]{2,1,0:T(8,128)S(1)}, u32[]{:S(2)}, u32[]{:S(2)}) async-start(f32[8,56,640]{2,1,0:T(8,128)} %pack.1), calls=%async_computation | async-start | bytes 2293760 | tf_op jit(solution)/shard_map/all_to_all | solution.py:423
  11.3 4.7 %collective-permute-start = (f32[2,56,128]{2,1,0:T(8,128)S(1)}, f32[2,56,128]{2,1,0:T(8,128)S(1)}, u32[]{:S(2)}, u32[]{:S(2)}) collective-permute-start(f32[2,56,128]{2,1,0:T(8,128)S(1)} %get-tuple-element.26), channel_id=1, source_target_pairs={{0,32},{32,0},{1,33},{33,1},{2,34},{34,2},{3,35},{35,3},{4,36},{36... | collective-permute-start | bytes 172040 | tf_op jit(solution)/shard_map/ppermute | solution.py:441
  16.1 20.5 %all-gather = f32[896,128]{1,0:T(8,128)S(1)} all-gather(f32[56,128]{1,0:T(8,128)S(1)} %get-tuple-element.27), channel_id=2, replica_groups=mesh['x'=4,'zl'=2,'core'=2,'zh'=4,'y'=8] {'x','zl','core'}, dimensions={0}, use_global_device_ids=true | all-gather | bytes 487424 | tf_op jit(solution)/shard_map/all_gather | solution.py:440
  39.5 4.2 %collective-permute-start.1 = (f32[8,56,640]{2,1,0:T(8,128)S(1)}, f32[8,56,640]{2,1,0:T(8,128)S(1)}, u32[]{:S(2)}, u32[]{:S(2)}) collective-permute-start(f32[8,56,640]{2,1,0:T(8,128)S(1)} %all-to-all-done.in_ref), channel_id=1, source_target_pairs={{0,32},{32,0},{1,33},{33,1},{2,34},{34,2},{3,35},{35,3},{4,36},{36... | collective-permute-start | bytes 3440648 | tf_op jit(solution)/shard_map/ppermute | solution.py:445
  47.2 3.7 %mirror.3 = f32[8,56,128]{2,1,0:T(8,128)} custom-call(s32[4]{0:T(128)S(1)} %pad_add_fusion.me_ref, s32[8,128]{1,0:T(8,128)S(1)} %get-tuple-element.29.pos_a_ref, s32[8,128]{1,0:T(8,128)S(1)} %get-tuple-element.30.pos_b_ref, f32[4,56,128]{2,1,0:T(8,128)S(1)} %join_cores.1.rows_ref.refs_0_.refs_1_, bf16[88,56,128]{2,1,0:T(8,128)(2,1)S(1)} %get-tuple-element.32.blocks_a_ref, ...), custom_call_target="tpu_custom_call" | custom-call | flops 200000000 | bytes 4000000 | tf_op jit(solution)/shard_map/mirror/pallas_call | solution.py:295
  50.9 5.8 %all-to-all-start.1 = ((f32[8,56,128]{2,1,0:T(8,128)}), f32[8,56,128]{2,1,0:T(8,128)S(1)}, u32[]{:S(2)}, u32[]{:S(2)}) async-start(f32[8,56,128]{2,1,0:T(8,128)} %mirror.3), calls=%async_computation.1 | async-start | bytes 458752 | tf_op jit(solution)/shard_map/all_to_all | solution.py:423
  56.7 3.5 %direct.3.rows_ref = f32[4,56,128]{2,1,0:T(8,128)S(1)} custom-call(s32[4]{0:T(128)S(1)} %pad_add_fusion.me_ref, s32[8,128]{1,0:T(8,128)S(1)} %get-tuple-element.29.pos_a_ref, s32[8,128]{1,0:T(8,128)S(1)} %get-tuple-element.30.pos_b_ref, f32[8,56,128]{2,1,0:T(8,128)S(1)} %pick_half.1.cols_ref, bf16[88,56,128]{2,1,0:T(8,128)(2,1)S(1)} %get-tuple-element.32.blocks_a_ref, ...), custom_call_target="tpu_custom_call" | custom-call | flops 200000000 | bytes 4000000 | tf_op jit(solution)/shard_map/direct/pallas_call | solution.py:295
  60.2 2.9 %all-to-all-done.1.cols_ref = f32[8,56,128]{2,1,0:T(8,128)S(1)} async-done(((f32[8,56,128]{2,1,0:T(8,128)}), f32[8,56,128]{2,1,0:T(8,128)S(1)}, u32[]{:S(2)}, u32[]{:S(2)}) %all-to-all-start.1) | async-done | bytes 229408 | tf_op jit(solution)/shard_map/all_to_all | solution.py:423
  63.7 21.3 %all_to_all.50.got_ref = f32[4,4,56,128]{3,2,1,0:T(8,128)S(1)} all-to-all(f32[4,4,56,128]{3,2,1,0:T(8,128)S(1)} %merge.2), channel_id=1, replica_groups=mesh['x'=4,'zl'=2,'core'=2,'zh'=4,'y'=8] {'zh'}, dimensions={0} | all-to-all | bytes 917504 | tf_op jit(solution)/shard_map/all_to_all | solution.py:423
  86.2 4.2 %all-to-all-start.3 = ((f32[8,56,128]{2,1,0:T(8,128)}), f32[8,56,128]{2,1,0:T(8,128)S(1)}, u32[]{:S(2)}, u32[]{:S(2)}) async-start(f32[8,56,128]{2,1,0:T(8,128)} %broadcast_in_dim.6), calls=%async_computation.3 | async-start | bytes 458752 | tf_op jit(solution)/shard_map/all_to_all | solution.py:423
  90.5 3.7 %mirror.4 = f32[8,56,128]{2,1,0:T(8,128)} custom-call(s32[4]{0:T(128)S(1)} %pad_add_fusion.me_ref, s32[8,128]{1,0:T(8,128)S(1)} %get-tuple-element.29.pos_a_ref, s32[8,128]{1,0:T(8,128)S(1)} %get-tuple-element.30.pos_b_ref, f32[4,56,128]{2,1,0:T(8,128)S(1)} %get-tuple-element.37.rows_ref.refs_0_.previous_ref, ...), custom_call_target="tpu_custom_call" | custom-call | flops 200000000 | bytes 4000000 | tf_op jit(solution)/shard_map/mirror/pallas_call | solution.py:295
  94.2 2.3 %all-to-all-done.3.cols_ref = f32[8,56,128]{2,1,0:T(8,128)S(1)} async-done(((f32[8,56,128]{2,1,0:T(8,128)}), f32[8,56,128]{2,1,0:T(8,128)S(1)}, u32[]{:S(2)}, u32[]{:S(2)}) %all-to-all-start.3) | async-done | bytes 229408 | tf_op jit(solution)/shard_map/all_to_all | solution.py:423
  96.4 3.4 %all-to-all-start.4 = ((f32[8,56,128]{2,1,0:T(8,128)}), f32[8,56,128]{2,1,0:T(8,128)S(1)}, u32[]{:S(2)}, u32[]{:S(2)}) async-start(f32[8,56,128]{2,1,0:T(8,128)} %mirror.4), calls=%async_computation.4 | async-start | bytes 458752 | tf_op jit(solution)/shard_map/all_to_all | solution.py:423
  99.8 3.5 %direct.4.rows_ref = f32[4,56,128]{2,1,0:T(8,128)S(1)} custom-call(s32[4]{0:T(128)S(1)} %pad_add_fusion.me_ref, s32[8,128]{1,0:T(8,128)S(1)} %get-tuple-element.29.pos_a_ref, s32[8,128]{1,0:T(8,128)S(1)} %get-tuple-element.30.pos_b_ref, f32[8,56,128]{2,1,0:T(8,128)S(1)} %all-to-all-done.3.cols_ref, bf16[88,56,128]{2,1,0:T(8,128)(2,1)S(1)} %get-tuple-element.32.blocks_a_ref, ...), custom_call_target="tpu_custom_call" | custom-call | flops 200000000 | bytes 4000000 | tf_op jit(solution)/shard_map/direct/pallas_call | solution.py:295
  103.3 2.4 %all-to-all-done.4.cols_ref = f32[8,56,128]{2,1,0:T(8,128)S(1)} async-done(((f32[8,56,128]{2,1,0:T(8,128)}), f32[8,56,128]{2,1,0:T(8,128)S(1)}, u32[]{:S(2)}, u32[]{:S(2)}) %all-to-all-start.4) | async-done | bytes 229408 | tf_op jit(solution)/shard_map/all_to_all | solution.py:423
  106.3 14.1 %all_to_all.51.got_ref = f32[4,4,56,128]{3,2,1,0:T(8,128)S(1)} all-to-all(f32[4,4,56,128]{3,2,1,0:T(8,128)S(1)} %merge.3), channel_id=1, replica_groups=mesh['x'=4,'zl'=2,'core'=2,'zh'=4,'y'=8] {'zh'}, dimensions={0} | all-to-all | bytes 917504 | tf_op jit(solution)/shard_map/all_to_all | solution.py:423
  121.8 4.5 %all-to-all-start.6 = ((f32[8,56,128]{2,1,0:T(8,128)}), f32[8,56,128]{2,1,0:T(8,128)S(1)}, u32[]{:S(2)}, u32[]{:S(2)}) async-start(f32[8,56,128]{2,1,0:T(8,128)} %broadcast_in_dim.7), calls=%async_computation.6 | async-start | bytes 458752 | tf_op jit(solution)/shard_map/all_to_all | solution.py:423
  126.2 3.7 %mirror.5 = f32[8,56,128]{2,1,0:T(8,128)} custom-call(s32[4]{0:T(128)S(1)} %pad_add_fusion.me_ref, s32[8,128]{1,0:T(8,128)S(1)} %get-tuple-element.29.pos_a_ref, s32[8,128]{1,0:T(8,128)S(1)} %get-tuple-element.30.pos_b_ref, f32[4,56,128]{2,1,0:T(8,128)S(1)} %get-tuple-element.41.rows_ref.current_ref, ...), custom_call_target="tpu_custom_call" | custom-call | flops 200000000 | bytes 4000000 | tf_op jit(solution)/shard_map/mirror/pallas_call | solution.py:295
  129.9 2.3 %all-to-all-done.6.cols_ref = f32[8,56,128]{2,1,0:T(8,128)S(1)} async-done(((f32[8,56,128]{2,1,0:T(8,128)}), f32[8,56,128]{2,1,0:T(8,128)S(1)}, u32[]{:S(2)}, u32[]{:S(2)}) %all-to-all-start.6) | async-done | bytes 229408 | tf_op jit(solution)/shard_map/all_to_all | solution.py:423
  132.2 3.4 %all-to-all-start.7 = ((f32[8,56,128]{2,1,0:T(8,128)}), f32[8,56,128]{2,1,0:T(8,128)S(1)}, u32[]{:S(2)}, u32[]{:S(2)}) async-start(f32[8,56,128]{2,1,0:T(8,128)} %mirror.5), calls=%async_computation.7 | async-start | bytes 458752 | tf_op jit(solution)/shard_map/all_to_all | solution.py:423
  135.6 3.5 %direct.5.rows_ref = f32[4,56,128]{2,1,0:T(8,128)S(1)} custom-call(s32[4]{0:T(128)S(1)} %pad_add_fusion.me_ref, s32[8,128]{1,0:T(8,128)S(1)} %get-tuple-element.29.pos_a_ref, s32[8,128]{1,0:T(8,128)S(1)} %get-tuple-element.30.pos_b_ref, f32[8,56,128]{2,1,0:T(8,128)S(1)} %all-to-all-done.6.cols_ref, bf16[88,56,128]{2,1,0:T(8,128)(2,1)S(1)} %get-tuple-element.32.blocks_a_ref, ...), custom_call_target="tpu_custom_call" | custom-call | flops 200000000 | bytes 4000000 | tf_op jit(solution)/shard_map/direct/pallas_call | solution.py:295
  139.1 2.4 %all-to-all-done.7 = f32[8,56,128]{2,1,0:T(8,128)S(1)} async-done(((f32[8,56,128]{2,1,0:T(8,128)}), f32[8,56,128]{2,1,0:T(8,128)S(1)}, u32[]{:S(2)}, u32[]{:S(2)}) %all-to-all-start.7) | async-done | bytes 229408 | tf_op jit(solution)/shard_map/all_to_all | solution.py:423
  142.5 19.4 %all_to_all.52 = f32[8,56,128]{2,1,0:T(8,128)S(1)} all-to-all(f32[8,56,128]{2,1,0:T(8,128)S(1)} %finish.1), channel_id=1, replica_groups=mesh['x'=4,'zl'=2,'core'=2,'zh'=4,'y'=8] {'core','zh'}, dimensions={0} | all-to-all | bytes 458752 | tf_op jit(solution)/shard_map/all_to_all | solution.py:423
  162.0 28.4 %all_to_all.53 = f32[32,56,128]{2,1,0:T(8,128)S(1)} all-to-all(f32[32,56,128]{2,1,0:T(8,128)S(1)} %broadcast_in_dim.8), channel_id=1, replica_groups=mesh['x'=4,'zl'=2,'core'=2,'zh'=4,'y'=8] {'zh','y'}, dimensions={0} | all-to-all | bytes 1835008 | tf_op jit(solution)/shard_map/all_to_all | solution.py:423
  (23 shorter events, 16.5 us)
Async XLA Ops:
  2.2 7.9 %copy-start = (f32[1792,128]{1,0:T(8,128)S(1)}, f32[1792,128]{1,0:T(8,128)}, u32[]{:S(2)}) copy-start(f32[1792,128]{1,0:T(8,128)} %param.4) | copy-start | bytes 2752516
  2.2 37.3 %all-to-all-start = ((f32[8,56,640]{2,1,0:T(8,128)}), f32[8,56,640]{2,1,0:T(8,128)S(1)}, u32[]{:S(2)}, u32[]{:S(2)}) async-start(f32[8,56,640]{2,1,0:T(8,128)} %pack.1), calls=%async_computation | async-start | bytes 2293760 | tf_op jit(solution)/shard_map/all_to_all | solution.py:423
  11.3 25.9 %collective-permute-start = (f32[2,56,128]{2,1,0:T(8,128)S(1)}, f32[2,56,128]{2,1,0:T(8,128)S(1)}, u32[]{:S(2)}, u32[]{:S(2)}) collective-permute-start(f32[2,56,128]{2,1,0:T(8,128)S(1)} %get-tuple-element.26), channel_id=1, source_target_pairs={{0,32},{32,0},{1,33},{33,1},{2,34},{34,2},{3,35},{35,3},{4,36},{36... | collective-permute-start | bytes 172040 | tf_op jit(solution)/shard_map/ppermute | solution.py:441
  39.5 6.6 %collective-permute-start.1 = (f32[8,56,640]{2,1,0:T(8,128)S(1)}, f32[8,56,640]{2,1,0:T(8,128)S(1)}, u32[]{:S(2)}, u32[]{:S(2)}) collective-permute-start(f32[8,56,640]{2,1,0:T(8,128)S(1)} %all-to-all-done.in_ref), channel_id=1, source_target_pairs={{0,32},{32,0},{1,33},{33,1},{2,34},{34,2},{3,35},{35,3},{4,36},{36... | collective-permute-start | bytes 3440648 | tf_op jit(solution)/shard_map/ppermute | solution.py:445
  50.9 12.2 %all-to-all-start.1 = ((f32[8,56,128]{2,1,0:T(8,128)}), f32[8,56,128]{2,1,0:T(8,128)S(1)}, u32[]{:S(2)}, u32[]{:S(2)}) async-start(f32[8,56,128]{2,1,0:T(8,128)} %mirror.3), calls=%async_computation.1 | async-start | bytes 458752 | tf_op jit(solution)/shard_map/all_to_all | solution.py:423
  86.2 10.2 %all-to-all-start.3 = ((f32[8,56,128]{2,1,0:T(8,128)}), f32[8,56,128]{2,1,0:T(8,128)S(1)}, u32[]{:S(2)}, u32[]{:S(2)}) async-start(f32[8,56,128]{2,1,0:T(8,128)} %broadcast_in_dim.6), calls=%async_computation.3 | async-start | bytes 458752 | tf_op jit(solution)/shard_map/all_to_all | solution.py:423
  96.4 9.3 %all-to-all-start.4 = ((f32[8,56,128]{2,1,0:T(8,128)}), f32[8,56,128]{2,1,0:T(8,128)S(1)}, u32[]{:S(2)}, u32[]{:S(2)}) async-start(f32[8,56,128]{2,1,0:T(8,128)} %mirror.4), calls=%async_computation.4 | async-start | bytes 458752 | tf_op jit(solution)/shard_map/all_to_all | solution.py:423
  121.8 10.4 %all-to-all-start.6 = ((f32[8,56,128]{2,1,0:T(8,128)}), f32[8,56,128]{2,1,0:T(8,128)S(1)}, u32[]{:S(2)}, u32[]{:S(2)}) async-start(f32[8,56,128]{2,1,0:T(8,128)} %broadcast_in_dim.7), calls=%async_computation.6 | async-start | bytes 458752 | tf_op jit(solution)/shard_map/all_to_all | solution.py:423
  132.2 9.3 %all-to-all-start.7 = ((f32[8,56,128]{2,1,0:T(8,128)}), f32[8,56,128]{2,1,0:T(8,128)S(1)}, u32[]{:S(2)}, u32[]{:S(2)}) async-start(f32[8,56,128]{2,1,0:T(8,128)} %mirror.5), calls=%async_computation.7 | async-start | bytes 458752 | tf_op jit(solution)/shard_map/all_to_all | solution.py:423

commit v10 on v9

--- a/solution.py
+++ b/solution.py
@@ -248,15 +248,16 @@
     core = me_ref[2]
     parts = ((pos_a_ref, blocks_a_ref, core), (pos_b_ref, blocks_b_ref, 1 - core))
 
-    def one_source(s, carry):
-        for t in range(TILES):
-            for pos_ref, blocks_ref, core_s in parts:
-                row, col = row_col(pos_ref, core_s, s, t)
-                both = jnp.dot(v_ref[row][:, :ORB], blocks_ref[s * SLOTS + t], preferred_element_type=f32)
-                acc_ref[col] += both[:VS] + both[VS:]
+    def two_sources(pair, carry):
+        for s in (2 * pair, 2 * pair + 1):
+            for t in range(TILES):
+                for pos_ref, blocks_ref, core_s in parts:
+                    row, col = row_col(pos_ref, core_s, s, t)
+                    both = jnp.dot(v_ref[row][:, :ORB], blocks_ref[s * SLOTS + t], preferred_element_type=f32)
+                    acc_ref[col] += both[:VS] + both[VS:]
         return carry
 
-    lax.fori_loop(0, N_Y, one_source, 0)
+    lax.fori_loop(0, N_Y // 2, two_sources, 0)
     for chunk in range(out_ref.shape[0]):
         x = acc_ref[chunk * GROUPS : (chunk + 1) * GROUPS].reshape(LANES, LANES)
         x = x + pltpu.roll(x, 64, 1)
@@ -340,7 +341,7 @@
     lane = lane_iota()
     copies = []
     for z in range(N_ZH):
-        x = [in_ref[z, y] for y in range(N_Y)]
+        x = [in_ref[y, z] for y in range(N_Y)]
         for d in (4, 2, 1):
             upper = (lane & (16 * d)) != 0
             for a in range(N_Y):
@@ -402,7 +403,9 @@
             image = image + got_ref[source, z]
         shifted = (image - centre * fields[0][z]) / half_width
         out_ref[z] = shifted if len(fields) == 1 else 2.0 * shifted - fields[1][z]
-    own_ref[...] = out_ref[me_ref[1]]
+    own = out_ref[me_ref[1]]
+    for r in range(N_R):
+        own_ref[r] = own
 
 
 def advance(me, got, fields):
@@ -410,7 +413,7 @@
         advance_kernel,
         out_shape=(
             jax.ShapeDtypeStruct((N_ZH, ORB, LANES), f32),
-            jax.ShapeDtypeStruct((ORB, LANES), f32),
+            jax.ShapeDtypeStruct((N_R, ORB, LANES), f32),
         ),
         in_specs=[pl.BlockSpec(memory_space=pltpu.SMEM)] + vmem(1 + len(fields)),
         out_specs=tuple(vmem(2)),
@@ -456,10 +459,10 @@
         got = exchange(merge(me, out_rows, got_cols), "zh")
         following, own = advance(me, got, (current,) if previous is None else (current, previous))
         previous, current = current, following
-        cols = gather(own, ROW_AX, N_R)
+        cols = exchange(own, ROW_AX)
 
     result = jnp.sum(exchange(finish(me, out_rows, jnp.sum(got_cols, 0), current, previous), ("core", "zh")), 0)
-    result = gather(result, ("zh", "y"), N_ZH * N_Y).reshape(N_ZH, N_Y, ORB, LANES)
+    result = gather(result, ("y", "zh"), N_ZH * N_Y).reshape(N_Y, N_ZH, ORB, LANES)
     return spread(result).reshape(vectors.shape)
 
 

time: 195 us -> 194 us (level)
  no operation moved by 1% of the time
where the time goes in v10:
time: 194 us; the launch traced here: 193 us
  blocking collectives  105 us (54%)
  starting transfers between devices  38.1 us (20%)
  Pallas kernels  33.3 us (17%)
  waiting for transfers between devices  16.2 us (8%)
    all_to_all x4, blocking collectives, exchange(): return lax.all_to_all(x, axes, split_axis=0, concat_axis=0, tiled=True)  84.2 us
    all_to_all x6, starting transfers between devices, exchange(): return lax.all_to_all(x, axes, split_axis=0, concat_axis=0, tiled=True)  29.1 us
    all_gather x1, blocking collectives, body(): lax.all_gather(own, ('x', 'zl', 'core'), axis=0, tiled=False)  20.5 us
    pallas_call x6, Pallas kernels, product(): pl.pallas_call(kernel, out_shape=jax.ShapeDtypeStruct((chunks, ORB, LANES...  19.9 us
    all_to_all x6, waiting for transfers between devices, exchange(): return lax.all_to_all(x, axes, split_axis=0, concat_axis=0, tiled=True)  14.9 us
    ppermute x1, starting transfers between devices, body(): current = join_cores(me, mine, lax.ppermute(other, 'core', swap))  4.72 us
    ppermute x1, starting transfers between devices, body(): blocks_b, pos_b = unpack(lax.ppermute(packed, 'core', swap))  4.23 us
  transfers between devices with their start and end apart: 8, of which 7 were waited for; matrix products, arithmetic and copies ran while one was open for 0% of the time, Pallas kernels for 11%

profile of v10, /device:TPU:1, one launch (start us, length us, event | category | flops | bytes accessed | tf_op | source)
XLA Modules:
  0.0 192.5 jit_solution(11500863795920900628)
XLA Ops:
  2.2 7.8 %all-to-all-start = ((f32[8,56,640]{2,1,0:T(8,128)}), f32[8,56,640]{2,1,0:T(8,128)S(1)}, u32[]{:S(2)}, u32[]{:S(2)}) async-start(f32[8,56,640]{2,1,0:T(8,128)} %pack.1), calls=%async_computation | async-start | bytes 2293760 | tf_op jit(solution)/shard_map/all_to_all | solution.py:426
  11.3 4.7 %collective-permute-start = (f32[2,56,128]{2,1,0:T(8,128)S(1)}, f32[2,56,128]{2,1,0:T(8,128)S(1)}, u32[]{:S(2)}, u32[]{:S(2)}) collective-permute-start(f32[2,56,128]{2,1,0:T(8,128)S(1)} %get-tuple-element.26), channel_id=1, source_target_pairs={{0,32},{32,0},{1,33},{33,1},{2,34},{34,2},{3,35},{35,3},{4,36},{36... | collective-permute-start | bytes 172040 | tf_op jit(solution)/shard_map/ppermute | solution.py:444
  16.1 20.5 %all-gather = f32[896,128]{1,0:T(8,128)S(1)} all-gather(f32[56,128]{1,0:T(8,128)S(1)} %get-tuple-element.27), channel_id=2, replica_groups=mesh['x'=4,'zl'=2,'core'=2,'zh'=4,'y'=8] {'x','zl','core'}, dimensions={0}, use_global_device_ids=true | all-gather | bytes 487424 | tf_op jit(solution)/shard_map/all_gather | solution.py:443
  39.5 4.2 %collective-permute-start.1 = (f32[8,56,640]{2,1,0:T(8,128)S(1)}, f32[8,56,640]{2,1,0:T(8,128)S(1)}, u32[]{:S(2)}, u32[]{:S(2)}) collective-permute-start(f32[8,56,640]{2,1,0:T(8,128)S(1)} %all-to-all-done.in_ref), channel_id=1, source_target_pairs={{0,32},{32,0},{1,33},{33,1},{2,34},{34,2},{3,35},{35,3},{4,36},{36... | collective-permute-start | bytes 3440648 | tf_op jit(solution)/shard_map/ppermute | solution.py:448
  47.2 3.2 %mirror.3 = f32[8,56,128]{2,1,0:T(8,128)} custom-call(s32[4]{0:T(128)S(1)} %pad_add_fusion.me_ref, s32[8,128]{1,0:T(8,128)S(1)} %get-tuple-element.29.pos_a_ref, s32[8,128]{1,0:T(8,128)S(1)} %get-tuple-element.30.pos_b_ref, f32[4,56,128]{2,1,0:T(8,128)S(1)} %join_cores.1.rows_ref.refs_0_.refs_1_, bf16[88,56,128]{2,1,0:T(8,128)(2,1)S(1)} %get-tuple-element.32.blocks_a_ref, ...), custom_call_target="tpu_custom_call" | custom-call | flops 200000000 | bytes 4000000 | tf_op jit(solution)/shard_map/mirror/pallas_call | solution.py:296
  50.4 5.9 %all-to-all-start.1 = ((f32[8,56,128]{2,1,0:T(8,128)}), f32[8,56,128]{2,1,0:T(8,128)S(1)}, u32[]{:S(2)}, u32[]{:S(2)}) async-start(f32[8,56,128]{2,1,0:T(8,128)} %mirror.3), calls=%async_computation.1 | async-start | bytes 458752 | tf_op jit(solution)/shard_map/all_to_all | solution.py:426
  56.2 3.5 %direct.3.rows_ref = f32[4,56,128]{2,1,0:T(8,128)S(1)} custom-call(s32[4]{0:T(128)S(1)} %pad_add_fusion.me_ref, s32[8,128]{1,0:T(8,128)S(1)} %get-tuple-element.29.pos_a_ref, s32[8,128]{1,0:T(8,128)S(1)} %get-tuple-element.30.pos_b_ref, f32[8,56,128]{2,1,0:T(8,128)S(1)} %pick_half.1.cols_ref, bf16[88,56,128]{2,1,0:T(8,128)(2,1)S(1)} %get-tuple-element.32.blocks_a_ref, ...), custom_call_target="tpu_custom_call" | custom-call | flops 200000000 | bytes 4000000 | tf_op jit(solution)/shard_map/direct/pallas_call | solution.py:296
  59.7 2.9 %all-to-all-done.1.cols_ref = f32[8,56,128]{2,1,0:T(8,128)S(1)} async-done(((f32[8,56,128]{2,1,0:T(8,128)}), f32[8,56,128]{2,1,0:T(8,128)S(1)}, u32[]{:S(2)}, u32[]{:S(2)}) %all-to-all-start.1) | async-done | bytes 229408 | tf_op jit(solution)/shard_map/all_to_all | solution.py:426
  63.2 21.3 %all_to_all.50.got_ref = f32[4,4,56,128]{3,2,1,0:T(8,128)S(1)} all-to-all(f32[4,4,56,128]{3,2,1,0:T(8,128)S(1)} %merge.2), channel_id=1, replica_groups=mesh['x'=4,'zl'=2,'core'=2,'zh'=4,'y'=8] {'zh'}, dimensions={0} | all-to-all | bytes 917504 | tf_op jit(solution)/shard_map/all_to_all | solution.py:426
  85.7 4.2 %all-to-all-start.3 = ((f32[8,56,128]{2,1,0:T(8,128)}), f32[8,56,128]{2,1,0:T(8,128)S(1)}, u32[]{:S(2)}, u32[]{:S(2)}) async-start(f32[8,56,128]{2,1,0:T(8,128)} %get-tuple-element.38), calls=%async_computation.3 | async-start | bytes 458752 | tf_op jit(solution)/shard_map/all_to_all | solution.py:426
  89.9 3.2 %mirror.4 = f32[8,56,128]{2,1,0:T(8,128)} custom-call(s32[4]{0:T(128)S(1)} %pad_add_fusion.me_ref, s32[8,128]{1,0:T(8,128)S(1)} %get-tuple-element.29.pos_a_ref, s32[8,128]{1,0:T(8,128)S(1)} %get-tuple-element.30.pos_b_ref, f32[4,56,128]{2,1,0:T(8,128)S(1)} %get-tuple-element.37.rows_ref.refs_0_.previous_ref, ...), custom_call_target="tpu_custom_call" | custom-call | flops 200000000 | bytes 4000000 | tf_op jit(solution)/shard_map/mirror/pallas_call | solution.py:296
  93.1 2.8 %all-to-all-done.3.cols_ref = f32[8,56,128]{2,1,0:T(8,128)S(1)} async-done(((f32[8,56,128]{2,1,0:T(8,128)}), f32[8,56,128]{2,1,0:T(8,128)S(1)}, u32[]{:S(2)}, u32[]{:S(2)}) %all-to-all-start.3) | async-done | bytes 229408 | tf_op jit(solution)/shard_map/all_to_all | solution.py:426
  95.9 3.4 %all-to-all-start.4 = ((f32[8,56,128]{2,1,0:T(8,128)}), f32[8,56,128]{2,1,0:T(8,128)S(1)}, u32[]{:S(2)}, u32[]{:S(2)}) async-start(f32[8,56,128]{2,1,0:T(8,128)} %mirror.4), calls=%async_computation.4 | async-start | bytes 458752 | tf_op jit(solution)/shard_map/all_to_all | solution.py:426
  99.3 3.5 %direct.4.rows_ref = f32[4,56,128]{2,1,0:T(8,128)S(1)} custom-call(s32[4]{0:T(128)S(1)} %pad_add_fusion.me_ref, s32[8,128]{1,0:T(8,128)S(1)} %get-tuple-element.29.pos_a_ref, s32[8,128]{1,0:T(8,128)S(1)} %get-tuple-element.30.pos_b_ref, f32[8,56,128]{2,1,0:T(8,128)S(1)} %all-to-all-done.3.cols_ref, bf16[88,56,128]{2,1,0:T(8,128)(2,1)S(1)} %get-tuple-element.32.blocks_a_ref, ...), custom_call_target="tpu_custom_call" | custom-call | flops 200000000 | bytes 4000000 | tf_op jit(solution)/shard_map/direct/pallas_call | solution.py:296
  102.8 2.4 %all-to-all-done.4.cols_ref = f32[8,56,128]{2,1,0:T(8,128)S(1)} async-done(((f32[8,56,128]{2,1,0:T(8,128)}), f32[8,56,128]{2,1,0:T(8,128)S(1)}, u32[]{:S(2)}, u32[]{:S(2)}) %all-to-all-start.4) | async-done | bytes 229408 | tf_op jit(solution)/shard_map/all_to_all | solution.py:426
  105.8 14.2 %all_to_all.51.got_ref = f32[4,4,56,128]{3,2,1,0:T(8,128)S(1)} all-to-all(f32[4,4,56,128]{3,2,1,0:T(8,128)S(1)} %merge.3), channel_id=1, replica_groups=mesh['x'=4,'zl'=2,'core'=2,'zh'=4,'y'=8] {'zh'}, dimensions={0} | all-to-all | bytes 917504 | tf_op jit(solution)/shard_map/all_to_all | solution.py:426
  121.2 4.5 %all-to-all-start.6 = ((f32[8,56,128]{2,1,0:T(8,128)}), f32[8,56,128]{2,1,0:T(8,128)S(1)}, u32[]{:S(2)}, u32[]{:S(2)}) async-start(f32[8,56,128]{2,1,0:T(8,128)} %get-tuple-element.42), calls=%async_computation.6 | async-start | bytes 458752 | tf_op jit(solution)/shard_map/all_to_all | solution.py:426
  125.7 3.2 %mirror.5 = f32[8,56,128]{2,1,0:T(8,128)} custom-call(s32[4]{0:T(128)S(1)} %pad_add_fusion.me_ref, s32[8,128]{1,0:T(8,128)S(1)} %get-tuple-element.29.pos_a_ref, s32[8,128]{1,0:T(8,128)S(1)} %get-tuple-element.30.pos_b_ref, f32[4,56,128]{2,1,0:T(8,128)S(1)} %get-tuple-element.41.rows_ref.current_ref, ...), custom_call_target="tpu_custom_call" | custom-call | flops 200000000 | bytes 4000000 | tf_op jit(solution)/shard_map/mirror/pallas_call | solution.py:296
  128.9 2.8 %all-to-all-done.6.cols_ref = f32[8,56,128]{2,1,0:T(8,128)S(1)} async-done(((f32[8,56,128]{2,1,0:T(8,128)}), f32[8,56,128]{2,1,0:T(8,128)S(1)}, u32[]{:S(2)}, u32[]{:S(2)}) %all-to-all-start.6) | async-done | bytes 229408 | tf_op jit(solution)/shard_map/all_to_all | solution.py:426
  131.6 3.4 %all-to-all-start.7 = ((f32[8,56,128]{2,1,0:T(8,128)}), f32[8,56,128]{2,1,0:T(8,128)S(1)}, u32[]{:S(2)}, u32[]{:S(2)}) async-start(f32[8,56,128]{2,1,0:T(8,128)} %mirror.5), calls=%async_computation.7 | async-start | bytes 458752 | tf_op jit(solution)/shard_map/all_to_all | solution.py:426
  135.1 3.5 %direct.5.rows_ref = f32[4,56,128]{2,1,0:T(8,128)S(1)} custom-call(s32[4]{0:T(128)S(1)} %pad_add_fusion.me_ref, s32[8,128]{1,0:T(8,128)S(1)} %get-tuple-element.29.pos_a_ref, s32[8,128]{1,0:T(8,128)S(1)} %get-tuple-element.30.pos_b_ref, f32[8,56,128]{2,1,0:T(8,128)S(1)} %all-to-all-done.6.cols_ref, bf16[88,56,128]{2,1,0:T(8,128)(2,1)S(1)} %get-tuple-element.32.blocks_a_ref, ...), custom_call_target="tpu_custom_call" | custom-call | flops 200000000 | bytes 4000000 | tf_op jit(solution)/shard_map/direct/pallas_call | solution.py:296
  138.5 2.4 %all-to-all-done.7 = f32[8,56,128]{2,1,0:T(8,128)S(1)} async-done(((f32[8,56,128]{2,1,0:T(8,128)}), f32[8,56,128]{2,1,0:T(8,128)S(1)}, u32[]{:S(2)}, u32[]{:S(2)}) %all-to-all-start.7) | async-done | bytes 229408 | tf_op jit(solution)/shard_map/all_to_all | solution.py:426
  142.0 19.4 %all_to_all.52 = f32[8,56,128]{2,1,0:T(8,128)S(1)} all-to-all(f32[8,56,128]{2,1,0:T(8,128)S(1)} %finish.1), channel_id=1, replica_groups=mesh['x'=4,'zl'=2,'core'=2,'zh'=4,'y'=8] {'core','zh'}, dimensions={0} | all-to-all | bytes 458752 | tf_op jit(solution)/shard_map/all_to_all | solution.py:426
  161.5 29.3 %all_to_all.53 = f32[32,56,128]{2,1,0:T(8,128)S(1)} all-to-all(f32[32,56,128]{2,1,0:T(8,128)S(1)} %broadcast_in_dim.2), channel_id=1, replica_groups=mesh['x'=4,'zl'=2,'core'=2,'zh'=4,'y'=8] {'y','zh'}, dimensions={0} | all-to-all | bytes 1835008 | tf_op jit(solution)/shard_map/all_to_all | solution.py:426
  (21 shorter events, 16.5 us)
Async XLA Ops:
  2.2 7.9 %copy-start = (f32[1792,128]{1,0:T(8,128)S(1)}, f32[1792,128]{1,0:T(8,128)}, u32[]{:S(2)}) copy-start(f32[1792,128]{1,0:T(8,128)} %param.4) | copy-start | bytes 2752516
  2.2 37.3 %all-to-all-start = ((f32[8,56,640]{2,1,0:T(8,128)}), f32[8,56,640]{2,1,0:T(8,128)S(1)}, u32[]{:S(2)}, u32[]{:S(2)}) async-start(f32[8,56,640]{2,1,0:T(8,128)} %pack.1), calls=%async_computation | async-start | bytes 2293760 | tf_op jit(solution)/shard_map/all_to_all | solution.py:426
  11.3 25.9 %collective-permute-start = (f32[2,56,128]{2,1,0:T(8,128)S(1)}, f32[2,56,128]{2,1,0:T(8,128)S(1)}, u32[]{:S(2)}, u32[]{:S(2)}) collective-permute-start(f32[2,56,128]{2,1,0:T(8,128)S(1)} %get-tuple-element.26), channel_id=1, source_target_pairs={{0,32},{32,0},{1,33},{33,1},{2,34},{34,2},{3,35},{35,3},{4,36},{36... | collective-permute-start | bytes 172040 | tf_op jit(solution)/shard_map/ppermute | solution.py:444
  39.5 6.6 %collective-permute-start.1 = (f32[8,56,640]{2,1,0:T(8,128)S(1)}, f32[8,56,640]{2,1,0:T(8,128)S(1)}, u32[]{:S(2)}, u32[]{:S(2)}) collective-permute-start(f32[8,56,640]{2,1,0:T(8,128)S(1)} %all-to-all-done.in_ref), channel_id=1, source_target_pairs={{0,32},{32,0},{1,33},{33,1},{2,34},{34,2},{3,35},{35,3},{4,36},{36... | collective-permute-start | bytes 3440648 | tf_op jit(solution)/shard_map/ppermute | solution.py:448
  50.4 12.2 %all-to-all-start.1 = ((f32[8,56,128]{2,1,0:T(8,128)}), f32[8,56,128]{2,1,0:T(8,128)S(1)}, u32[]{:S(2)}, u32[]{:S(2)}) async-start(f32[8,56,128]{2,1,0:T(8,128)} %mirror.3), calls=%async_computation.1 | async-start | bytes 458752 | tf_op jit(solution)/shard_map/all_to_all | solution.py:426
  85.7 10.2 %all-to-all-start.3 = ((f32[8,56,128]{2,1,0:T(8,128)}), f32[8,56,128]{2,1,0:T(8,128)S(1)}, u32[]{:S(2)}, u32[]{:S(2)}) async-start(f32[8,56,128]{2,1,0:T(8,128)} %get-tuple-element.38), calls=%async_computation.3 | async-start | bytes 458752 | tf_op jit(solution)/shard_map/all_to_all | solution.py:426
  95.9 9.3 %all-to-all-start.4 = ((f32[8,56,128]{2,1,0:T(8,128)}), f32[8,56,128]{2,1,0:T(8,128)S(1)}, u32[]{:S(2)}, u32[]{:S(2)}) async-start(f32[8,56,128]{2,1,0:T(8,128)} %mirror.4), calls=%async_computation.4 | async-start | bytes 458752 | tf_op jit(solution)/shard_map/all_to_all | solution.py:426
  121.2 10.4 %all-to-all-start.6 = ((f32[8,56,128]{2,1,0:T(8,128)}), f32[8,56,128]{2,1,0:T(8,128)S(1)}, u32[]{:S(2)}, u32[]{:S(2)}) async-start(f32[8,56,128]{2,1,0:T(8,128)} %get-tuple-element.42), calls=%async_computation.6 | async-start | bytes 458752 | tf_op jit(solution)/shard_map/all_to_all | solution.py:426
  131.6 9.3 %all-to-all-start.7 = ((f32[8,56,128]{2,1,0:T(8,128)}), f32[8,56,128]{2,1,0:T(8,128)S(1)}, u32[]{:S(2)}, u32[]{:S(2)}) async-start(f32[8,56,128]{2,1,0:T(8,128)} %mirror.5), calls=%async_computation.7 | async-start | bytes 458752 | tf_op jit(solution)/shard_map/all_to_all | solution.py:426

commit v11 on v10

--- a/solution.py
+++ b/solution.py
@@ -311,7 +311,6 @@
 def finish_kernel(me_ref, rows_ref, own_ref, current_ref, previous_ref, out_ref):
     lane = lane_iota()
     zh, core = me_ref[1], me_ref[2]
-    mine = ((lane >> 3) & 1) == core
     scale = 2.0 / half_width
     own = scale * own_ref[...] - (scale * centre) * current_ref[zh] - previous_ref[zh]
     for z in range(N_ZH):
@@ -323,7 +322,7 @@
                 block = lane & (4 * step - 1)
                 moved = pltpu.roll(x, step, 1)
                 x = jnp.where(block < step, x, jnp.where((block >= 2 * step) & (block < 3 * step), moved, 0.0))
-            out_ref[k * N_ZH + z] = jnp.where(mine, pltpu.roll(x, core * VS, 1), 0.0)
+            out_ref[k * N_ZH + z] = pltpu.roll(x, core * VS, 1)
 
 
 def finish(me, rows, own, current, previous):
@@ -395,33 +394,6 @@
     )(me, rows, cols)
 
 
-def advance_kernel(me_ref, got_ref, *refs):
-    *fields, out_ref, own_ref = refs
-    for z in range(N_ZH):
-        image = got_ref[0, z]
-        for source in range(1, N_ZH):
-            image = image + got_ref[source, z]
-        shifted = (image - centre * fields[0][z]) / half_width
-        out_ref[z] = shifted if len(fields) == 1 else 2.0 * shifted - fields[1][z]
-    own = out_ref[me_ref[1]]
-    for r in range(N_R):
-        own_ref[r] = own
-
-
-def advance(me, got, fields):
-    return pl.pallas_call(
-        advance_kernel,
-        out_shape=(
-            jax.ShapeDtypeStruct((N_ZH, ORB, LANES), f32),
-            jax.ShapeDtypeStruct((N_R, ORB, LANES), f32),
-        ),
-        in_specs=[pl.BlockSpec(memory_space=pltpu.SMEM)] + vmem(1 + len(fields)),
-        out_specs=tuple(vmem(2)),
-        compiler_params=params(),
-        name="advance",
-    )(me, got, *fields)
-
-
 def exchange(x, axes):
     return lax.all_to_all(x, axes, split_axis=0, concat_axis=0, tiled=True)
 
@@ -457,9 +429,11 @@
         if step == DEGREE - 1:
             break
         got = exchange(merge(me, out_rows, got_cols), "zh")
-        following, own = advance(me, got, (current,) if previous is None else (current, previous))
+        got, current, own_at = lax.optimization_barrier((got, current, zh))
+        shifted = (jnp.sum(got, 0) - centre * current) / half_width
+        following = shifted if previous is None else 2.0 * shifted - previous
         previous, current = current, following
-        cols = exchange(own, ROW_AX)
+        cols = gather(lax.dynamic_index_in_dim(current, own_at, 0, keepdims=False), ROW_AX, N_R)
 
     result = jnp.sum(exchange(finish(me, out_rows, jnp.sum(got_cols, 0), current, previous), ("core", "zh")), 0)
     result = gather(result, ("y", "zh"), N_ZH * N_Y).reshape(N_Y, N_ZH, ORB, LANES)

time: 194 us -> 193 us (level)
  Pallas kernels: 33.3 us -> 30.7 us
    pallas_call x2 -> x0, Pallas kernels: 2.56 us -> none  [advance(): pl.pallas_call(advance_kernel, out_shape=(jax.ShapeDtypeStruct((N_ZH, ORB...]
where the time goes in v11:
time: 193 us; the launch traced here: 192 us
  blocking collectives  105 us (54%)
  starting transfers between devices  38.1 us (20%)
  Pallas kernels  30.7 us (16%)
  waiting for transfers between devices  16.2 us (8%)
    all_to_all x4, blocking collectives, exchange(): return lax.all_to_all(x, axes, split_axis=0, concat_axis=0, tiled=True)  84.1 us
    all_to_all x6, starting transfers between devices, exchange(): return lax.all_to_all(x, axes, split_axis=0, concat_axis=0, tiled=True)  29.2 us
    all_gather x1, blocking collectives, body(): lax.all_gather(own, ('x', 'zl', 'core'), axis=0, tiled=False)  20.5 us
    pallas_call x6, Pallas kernels, product(): pl.pallas_call(kernel, out_shape=jax.ShapeDtypeStruct((chunks, ORB, LANES...  19.9 us
    all_to_all x6, waiting for transfers between devices, exchange(): return lax.all_to_all(x, axes, split_axis=0, concat_axis=0, tiled=True)  14.9 us
    ppermute x1, starting transfers between devices, body(): current = join_cores(me, mine, lax.ppermute(other, 'core', swap))  4.72 us
    ppermute x1, starting transfers between devices, body(): blocks_b, pos_b = unpack(lax.ppermute(packed, 'core', swap))  4.23 us
  transfers between devices with their start and end apart: 8, of which 7 were waited for; matrix products, arithmetic and copies ran while one was open for 0% of the time, Pallas kernels for 11%

profile of v11, /device:TPU:1, one launch (start us, length us, event | category | flops | bytes accessed | tf_op | source)
XLA Modules:
  0.0 191.6 jit_solution(17044314871352297741)
XLA Ops:
  2.2 7.8 %all-to-all-start = ((f32[8,56,640]{2,1,0:T(8,128)}), f32[8,56,640]{2,1,0:T(8,128)S(1)}, u32[]{:S(2)}, u32[]{:S(2)}) async-start(f32[8,56,640]{2,1,0:T(8,128)} %pack.1), calls=%async_computation | async-start | bytes 2293760 | tf_op jit(solution)/shard_map/all_to_all | solution.py:398
  11.3 4.7 %collective-permute-start = (f32[2,56,128]{2,1,0:T(8,128)S(1)}, f32[2,56,128]{2,1,0:T(8,128)S(1)}, u32[]{:S(2)}, u32[]{:S(2)}) collective-permute-start(f32[2,56,128]{2,1,0:T(8,128)S(1)} %get-tuple-element.28), channel_id=1, source_target_pairs={{0,32},{32,0},{1,33},{33,1},{2,34},{34,2},{3,35},{35,3},{4,36},{36... | collective-permute-start | bytes 172040 | tf_op jit(solution)/shard_map/ppermute | solution.py:416
  16.0 20.5 %all-gather = f32[896,128]{1,0:T(8,128)S(1)} all-gather(f32[56,128]{1,0:T(8,128)S(1)} %get-tuple-element.29), channel_id=2, replica_groups=mesh['x'=4,'zl'=2,'core'=2,'zh'=4,'y'=8] {'x','zl','core'}, dimensions={0}, use_global_device_ids=true | all-gather | bytes 487424 | tf_op jit(solution)/shard_map/all_gather | solution.py:415
  39.5 4.2 %collective-permute-start.1 = (f32[8,56,640]{2,1,0:T(8,128)S(1)}, f32[8,56,640]{2,1,0:T(8,128)S(1)}, u32[]{:S(2)}, u32[]{:S(2)}) collective-permute-start(f32[8,56,640]{2,1,0:T(8,128)S(1)} %all-to-all-done.in_ref), channel_id=1, source_target_pairs={{0,32},{32,0},{1,33},{33,1},{2,34},{34,2},{3,35},{35,3},{4,36},{36... | collective-permute-start | bytes 3440648 | tf_op jit(solution)/shard_map/ppermute | solution.py:420
  47.2 3.2 %mirror.3 = f32[8,56,128]{2,1,0:T(8,128)} custom-call(s32[4]{0:T(128)S(1)} %pad_add_fusion.me_ref, s32[8,128]{1,0:T(8,128)S(1)} %get-tuple-element.31.pos_a_ref, s32[8,128]{1,0:T(8,128)S(1)} %get-tuple-element.32.pos_b_ref, f32[4,56,128]{2,1,0:T(8,128)S(1)} %join_cores.1.rows_ref, bf16[88,56,128]{2,1,0:T(8,128)(2,1)S(1)} %get-tuple-element.34.blocks_a_ref, ...), custom_call_target="tpu_custom_call" | custom-call | flops 200000000 | bytes 4000000 | tf_op jit(solution)/shard_map/mirror/pallas_call | solution.py:296
  50.4 5.8 %all-to-all-start.1 = ((f32[8,56,128]{2,1,0:T(8,128)}), f32[8,56,128]{2,1,0:T(8,128)S(1)}, u32[]{:S(2)}, u32[]{:S(2)}) async-start(f32[8,56,128]{2,1,0:T(8,128)} %mirror.3), calls=%async_computation.1 | async-start | bytes 458752 | tf_op jit(solution)/shard_map/all_to_all | solution.py:398
  56.2 3.5 %direct.3.rows_ref = f32[4,56,128]{2,1,0:T(8,128)S(1)} custom-call(s32[4]{0:T(128)S(1)} %pad_add_fusion.me_ref, s32[8,128]{1,0:T(8,128)S(1)} %get-tuple-element.31.pos_a_ref, s32[8,128]{1,0:T(8,128)S(1)} %get-tuple-element.32.pos_b_ref, f32[8,56,128]{2,1,0:T(8,128)S(1)} %pick_half.1.cols_ref, bf16[88,56,128]{2,1,0:T(8,128)(2,1)S(1)} %get-tuple-element.34.blocks_a_ref, ...), custom_call_target="tpu_custom_call" | custom-call | flops 200000000 | bytes 4000000 | tf_op jit(solution)/shard_map/direct/pallas_call | solution.py:296
  59.7 2.9 %all-to-all-done.1.cols_ref = f32[8,56,128]{2,1,0:T(8,128)S(1)} async-done(((f32[8,56,128]{2,1,0:T(8,128)}), f32[8,56,128]{2,1,0:T(8,128)S(1)}, u32[]{:S(2)}, u32[]{:S(2)}) %all-to-all-start.1) | async-done | bytes 229408 | tf_op jit(solution)/shard_map/all_to_all | solution.py:398
  63.1 21.3 %all_to_all.50 = f32[4,4,56,128]{3,2,1,0:T(8,128)S(1)} all-to-all(f32[4,4,56,128]{3,2,1,0:T(8,128)S(1)} %merge.2), channel_id=1, replica_groups=mesh['x'=4,'zl'=2,'core'=2,'zh'=4,'y'=8] {'zh'}, dimensions={0} | all-to-all | bytes 917504 | tf_op jit(solution)/shard_map/all_to_all | solution.py:398
  85.2 4.2 %all-to-all-start.3 = ((f32[8,56,128]{2,1,0:T(8,128)}), f32[8,56,128]{2,1,0:T(8,128)S(1)}, u32[]{:S(2)}, u32[]{:S(2)}) async-start(f32[8,56,128]{2,1,0:T(8,128)} %broadcast_in_dim.11), calls=%async_computation.3 | async-start | bytes 458752 | tf_op jit(solution)/shard_map/all_to_all | solution.py:398
  89.5 3.2 %mirror.4 = f32[8,56,128]{2,1,0:T(8,128)} custom-call(s32[4]{0:T(128)S(1)} %pad_add_fusion.me_ref, s32[8,128]{1,0:T(8,128)S(1)} %get-tuple-element.31.pos_a_ref, s32[8,128]{1,0:T(8,128)S(1)} %get-tuple-element.32.pos_b_ref, f32[4,56,128]{2,1,0:T(8,128)S(1)} %subtract_multiply_fusion.rows_ref.previous_ref, ...), custom_call_target="tpu_custom_call" | custom-call | flops 200000000 | bytes 4000000 | tf_op jit(solution)/shard_map/mirror/pallas_call | solution.py:296
  92.6 2.8 %all-to-all-done.3.cols_ref = f32[8,56,128]{2,1,0:T(8,128)S(1)} async-done(((f32[8,56,128]{2,1,0:T(8,128)}), f32[8,56,128]{2,1,0:T(8,128)S(1)}, u32[]{:S(2)}, u32[]{:S(2)}) %all-to-all-start.3) | async-done | bytes 229408 | tf_op jit(solution)/shard_map/all_to_all | solution.py:398
  95.4 3.4 %all-to-all-start.4 = ((f32[8,56,128]{2,1,0:T(8,128)}), f32[8,56,128]{2,1,0:T(8,128)S(1)}, u32[]{:S(2)}, u32[]{:S(2)}) async-start(f32[8,56,128]{2,1,0:T(8,128)} %mirror.4), calls=%async_computation.4 | async-start | bytes 458752 | tf_op jit(solution)/shard_map/all_to_all | solution.py:398
  98.8 3.5 %direct.4.rows_ref = f32[4,56,128]{2,1,0:T(8,128)S(1)} custom-call(s32[4]{0:T(128)S(1)} %pad_add_fusion.me_ref, s32[8,128]{1,0:T(8,128)S(1)} %get-tuple-element.31.pos_a_ref, s32[8,128]{1,0:T(8,128)S(1)} %get-tuple-element.32.pos_b_ref, f32[8,56,128]{2,1,0:T(8,128)S(1)} %all-to-all-done.3.cols_ref, bf16[88,56,128]{2,1,0:T(8,128)(2,1)S(1)} %get-tuple-element.34.blocks_a_ref, ...), custom_call_target="tpu_custom_call" | custom-call | flops 200000000 | bytes 4000000 | tf_op jit(solution)/shard_map/direct/pallas_call | solution.py:296
  102.3 2.4 %all-to-all-done.4.cols_ref = f32[8,56,128]{2,1,0:T(8,128)S(1)} async-done(((f32[8,56,128]{2,1,0:T(8,128)}), f32[8,56,128]{2,1,0:T(8,128)S(1)}, u32[]{:S(2)}, u32[]{:S(2)}) %all-to-all-start.4) | async-done | bytes 229408 | tf_op jit(solution)/shard_map/all_to_all | solution.py:398
  105.3 14.1 %all_to_all.51 = f32[4,4,56,128]{3,2,1,0:T(8,128)S(1)} all-to-all(f32[4,4,56,128]{3,2,1,0:T(8,128)S(1)} %merge.3), channel_id=1, replica_groups=mesh['x'=4,'zl'=2,'core'=2,'zh'=4,'y'=8] {'zh'}, dimensions={0} | all-to-all | bytes 917504 | tf_op jit(solution)/shard_map/all_to_all | solution.py:398
  120.2 4.5 %all-to-all-start.6 = ((f32[8,56,128]{2,1,0:T(8,128)}), f32[8,56,128]{2,1,0:T(8,128)S(1)}, u32[]{:S(2)}, u32[]{:S(2)}) async-start(f32[8,56,128]{2,1,0:T(8,128)} %broadcast_in_dim.25), calls=%async_computation.6 | async-start | bytes 458752 | tf_op jit(solution)/shard_map/all_to_all | solution.py:398
  124.7 3.2 %mirror.5 = f32[8,56,128]{2,1,0:T(8,128)} custom-call(s32[4]{0:T(128)S(1)} %pad_add_fusion.me_ref, s32[8,128]{1,0:T(8,128)S(1)} %get-tuple-element.31.pos_a_ref, s32[8,128]{1,0:T(8,128)S(1)} %get-tuple-element.32.pos_b_ref, f32[4,56,128]{2,1,0:T(8,128)S(1)} %multiply_subtract_fusion.rows_ref.current_ref, ...), custom_call_target="tpu_custom_call" | custom-call | flops 200000000 | bytes 4000000 | tf_op jit(solution)/shard_map/mirror/pallas_call | solution.py:296
  127.9 2.8 %all-to-all-done.6.cols_ref = f32[8,56,128]{2,1,0:T(8,128)S(1)} async-done(((f32[8,56,128]{2,1,0:T(8,128)}), f32[8,56,128]{2,1,0:T(8,128)S(1)}, u32[]{:S(2)}, u32[]{:S(2)}) %all-to-all-start.6) | async-done | bytes 229408 | tf_op jit(solution)/shard_map/all_to_all | solution.py:398
  130.7 3.4 %all-to-all-start.7 = ((f32[8,56,128]{2,1,0:T(8,128)}), f32[8,56,128]{2,1,0:T(8,128)S(1)}, u32[]{:S(2)}, u32[]{:S(2)}) async-start(f32[8,56,128]{2,1,0:T(8,128)} %mirror.5), calls=%async_computation.7 | async-start | bytes 458752 | tf_op jit(solution)/shard_map/all_to_all | solution.py:398
  134.1 3.5 %direct.5.rows_ref = f32[4,56,128]{2,1,0:T(8,128)S(1)} custom-call(s32[4]{0:T(128)S(1)} %pad_add_fusion.me_ref, s32[8,128]{1,0:T(8,128)S(1)} %get-tuple-element.31.pos_a_ref, s32[8,128]{1,0:T(8,128)S(1)} %get-tuple-element.32.pos_b_ref, f32[8,56,128]{2,1,0:T(8,128)S(1)} %all-to-all-done.6.cols_ref, bf16[88,56,128]{2,1,0:T(8,128)(2,1)S(1)} %get-tuple-element.34.blocks_a_ref, ...), custom_call_target="tpu_custom_call" | custom-call | flops 200000000 | bytes 4000000 | tf_op jit(solution)/shard_map/direct/pallas_call | solution.py:296
  137.6 2.4 %all-to-all-done.7 = f32[8,56,128]{2,1,0:T(8,128)S(1)} async-done(((f32[8,56,128]{2,1,0:T(8,128)}), f32[8,56,128]{2,1,0:T(8,128)S(1)}, u32[]{:S(2)}, u32[]{:S(2)}) %all-to-all-start.7) | async-done | bytes 229408 | tf_op jit(solution)/shard_map/all_to_all | solution.py:398
  141.0 19.4 %all_to_all.52 = f32[8,56,128]{2,1,0:T(8,128)S(1)} all-to-all(f32[8,56,128]{2,1,0:T(8,128)S(1)} %finish.1), channel_id=1, replica_groups=mesh['x'=4,'zl'=2,'core'=2,'zh'=4,'y'=8] {'core','zh'}, dimensions={0} | all-to-all | bytes 458752 | tf_op jit(solution)/shard_map/all_to_all | solution.py:398
  160.5 29.3 %all_to_all.53 = f32[32,56,128]{2,1,0:T(8,128)S(1)} all-to-all(f32[32,56,128]{2,1,0:T(8,128)S(1)} %broadcast_in_dim.26), channel_id=1, replica_groups=mesh['x'=4,'zl'=2,'core'=2,'zh'=4,'y'=8] {'y','zh'}, dimensions={0} | all-to-all | bytes 1835008 | tf_op jit(solution)/shard_map/all_to_all | solution.py:398
  (27 shorter events, 15.4 us)
Async XLA Ops:
  2.2 7.9 %copy-start = (f32[1792,128]{1,0:T(8,128)S(1)}, f32[1792,128]{1,0:T(8,128)}, u32[]{:S(2)}) copy-start(f32[1792,128]{1,0:T(8,128)} %param.4) | copy-start | bytes 2752516
  2.2 37.3 %all-to-all-start = ((f32[8,56,640]{2,1,0:T(8,128)}), f32[8,56,640]{2,1,0:T(8,128)S(1)}, u32[]{:S(2)}, u32[]{:S(2)}) async-start(f32[8,56,640]{2,1,0:T(8,128)} %pack.1), calls=%async_computation | async-start | bytes 2293760 | tf_op jit(solution)/shard_map/all_to_all | solution.py:398
  11.3 25.9 %collective-permute-start = (f32[2,56,128]{2,1,0:T(8,128)S(1)}, f32[2,56,128]{2,1,0:T(8,128)S(1)}, u32[]{:S(2)}, u32[]{:S(2)}) collective-permute-start(f32[2,56,128]{2,1,0:T(8,128)S(1)} %get-tuple-element.28), channel_id=1, source_target_pairs={{0,32},{32,0},{1,33},{33,1},{2,34},{34,2},{3,35},{35,3},{4,36},{36... | collective-permute-start | bytes 172040 | tf_op jit(solution)/shard_map/ppermute | solution.py:416
  39.5 6.6 %collective-permute-start.1 = (f32[8,56,640]{2,1,0:T(8,128)S(1)}, f32[8,56,640]{2,1,0:T(8,128)S(1)}, u32[]{:S(2)}, u32[]{:S(2)}) collective-permute-start(f32[8,56,640]{2,1,0:T(8,128)S(1)} %all-to-all-done.in_ref), channel_id=1, source_target_pairs={{0,32},{32,0},{1,33},{33,1},{2,34},{34,2},{3,35},{35,3},{4,36},{36... | collective-permute-start | bytes 3440648 | tf_op jit(solution)/shard_map/ppermute | solution.py:420
  50.4 12.2 %all-to-all-start.1 = ((f32[8,56,128]{2,1,0:T(8,128)}), f32[8,56,128]{2,1,0:T(8,128)S(1)}, u32[]{:S(2)}, u32[]{:S(2)}) async-start(f32[8,56,128]{2,1,0:T(8,128)} %mirror.3), calls=%async_computation.1 | async-start | bytes 458752 | tf_op jit(solution)/shard_map/all_to_all | solution.py:398
  85.2 10.2 %all-to-all-start.3 = ((f32[8,56,128]{2,1,0:T(8,128)}), f32[8,56,128]{2,1,0:T(8,128)S(1)}, u32[]{:S(2)}, u32[]{:S(2)}) async-start(f32[8,56,128]{2,1,0:T(8,128)} %broadcast_in_dim.11), calls=%async_computation.3 | async-start | bytes 458752 | tf_op jit(solution)/shard_map/all_to_all | solution.py:398
  95.4 9.3 %all-to-all-start.4 = ((f32[8,56,128]{2,1,0:T(8,128)}), f32[8,56,128]{2,1,0:T(8,128)S(1)}, u32[]{:S(2)}, u32[]{:S(2)}) async-start(f32[8,56,128]{2,1,0:T(8,128)} %mirror.4), calls=%async_computation.4 | async-start | bytes 458752 | tf_op jit(solution)/shard_map/all_to_all | solution.py:398
  120.2 10.4 %all-to-all-start.6 = ((f32[8,56,128]{2,1,0:T(8,128)}), f32[8,56,128]{2,1,0:T(8,128)S(1)}, u32[]{:S(2)}, u32[]{:S(2)}) async-start(f32[8,56,128]{2,1,0:T(8,128)} %broadcast_in_dim.25), calls=%async_computation.6 | async-start | bytes 458752 | tf_op jit(solution)/shard_map/all_to_all | solution.py:398
  130.7 9.3 %all-to-all-start.7 = ((f32[8,56,128]{2,1,0:T(8,128)}), f32[8,56,128]{2,1,0:T(8,128)S(1)}, u32[]{:S(2)}, u32[]{:S(2)}) async-start(f32[8,56,128]{2,1,0:T(8,128)} %mirror.5), calls=%async_computation.7 | async-start | bytes 458752 | tf_op jit(solution)/shard_map/all_to_all | solution.py:398

commit v12 on v11

--- a/solution.py
+++ b/solution.py
@@ -118,9 +118,8 @@
             hit = (target >= at) & (target < at + ORB) & (source == target - at + off)
             part = jnp.dot(term[:, window], jnp.where(hit, 1.0, 0.0).astype(bf16), preferred_element_type=f32)
             total = part if total is None else total + part
-        total = total.astype(bf16)
         for s in range(N_Y):
-            blocks_ref[s * SLOTS + t] = total[s * ORB : (s + 1) * ORB]
+            blocks_ref[s * SLOTS + t] = total[s * ORB : (s + 1) * ORB].astype(bf16)
     for s in range(N_Y):
         last = in_ref[s, 0:1, WIDE - LANES : WIDE]
         shown = lax.broadcasted_iota(jnp.int32, (1, LANES), 1) >= PLACE

time: 193 us -> 193 us (level)
  no operation moved by 1% of the time
where the time goes in v12:
time: 193 us; the launch traced here: 192 us
  blocking collectives  105 us (54%)
  starting transfers between devices  38.1 us (20%)
  Pallas kernels  30.7 us (16%)
  waiting for transfers between devices  16.2 us (8%)
    all_to_all x4, blocking collectives, exchange(): return lax.all_to_all(x, axes, split_axis=0, concat_axis=0, tiled=True)  84.1 us
    all_to_all x6, starting transfers between devices, exchange(): return lax.all_to_all(x, axes, split_axis=0, concat_axis=0, tiled=True)  29.2 us
    all_gather x1, blocking collectives, body(): lax.all_gather(own, ('x', 'zl', 'core'), axis=0, tiled=False)  20.5 us
    pallas_call x6, Pallas kernels, product(): pl.pallas_call(kernel, out_shape=jax.ShapeDtypeStruct((chunks, ORB, LANES...  19.9 us
    all_to_all x6, waiting for transfers between devices, exchange(): return lax.all_to_all(x, axes, split_axis=0, concat_axis=0, tiled=True)  14.9 us
    ppermute x1, starting transfers between devices, body(): current = join_cores(me, mine, lax.ppermute(other, 'core', swap))  4.72 us
    ppermute x1, starting transfers between devices, body(): blocks_b, pos_b = unpack(lax.ppermute(packed, 'core', swap))  4.23 us
  transfers between devices with their start and end apart: 8, of which 7 were waited for; matrix products, arithmetic and copies ran while one was open for 0% of the time, Pallas kernels for 11%

profile of v12, /device:TPU:1, one launch (start us, length us, event | category | flops | bytes accessed | tf_op | source)
XLA Modules:
  0.0 191.5 jit_solution(17044314871352297741)
XLA Ops:
  2.2 7.8 %all-to-all-start = ((f32[8,56,640]{2,1,0:T(8,128)}), f32[8,56,640]{2,1,0:T(8,128)S(1)}, u32[]{:S(2)}, u32[]{:S(2)}) async-start(f32[8,56,640]{2,1,0:T(8,128)} %pack.1), calls=%async_computation | async-start | bytes 2293760 | tf_op jit(solution)/shard_map/all_to_all | solution.py:397
  11.3 4.7 %collective-permute-start = (f32[2,56,128]{2,1,0:T(8,128)S(1)}, f32[2,56,128]{2,1,0:T(8,128)S(1)}, u32[]{:S(2)}, u32[]{:S(2)}) collective-permute-start(f32[2,56,128]{2,1,0:T(8,128)S(1)} %get-tuple-element.28), channel_id=1, source_target_pairs={{0,32},{32,0},{1,33},{33,1},{2,34},{34,2},{3,35},{35,3},{4,36},{36... | collective-permute-start | bytes 172040 | tf_op jit(solution)/shard_map/ppermute | solution.py:415
  16.0 20.5 %all-gather = f32[896,128]{1,0:T(8,128)S(1)} all-gather(f32[56,128]{1,0:T(8,128)S(1)} %get-tuple-element.29), channel_id=2, replica_groups=mesh['x'=4,'zl'=2,'core'=2,'zh'=4,'y'=8] {'x','zl','core'}, dimensions={0}, use_global_device_ids=true | all-gather | bytes 487424 | tf_op jit(solution)/shard_map/all_gather | solution.py:414
  39.5 4.2 %collective-permute-start.1 = (f32[8,56,640]{2,1,0:T(8,128)S(1)}, f32[8,56,640]{2,1,0:T(8,128)S(1)}, u32[]{:S(2)}, u32[]{:S(2)}) collective-permute-start(f32[8,56,640]{2,1,0:T(8,128)S(1)} %all-to-all-done.in_ref), channel_id=1, source_target_pairs={{0,32},{32,0},{1,33},{33,1},{2,34},{34,2},{3,35},{35,3},{4,36},{36... | collective-permute-start | bytes 3440648 | tf_op jit(solution)/shard_map/ppermute | solution.py:419
  47.2 3.2 %mirror.3 = f32[8,56,128]{2,1,0:T(8,128)} custom-call(s32[4]{0:T(128)S(1)} %pad_add_fusion.me_ref, s32[8,128]{1,0:T(8,128)S(1)} %get-tuple-element.31.pos_a_ref, s32[8,128]{1,0:T(8,128)S(1)} %get-tuple-element.32.pos_b_ref, f32[4,56,128]{2,1,0:T(8,128)S(1)} %join_cores.1.rows_ref, bf16[88,56,128]{2,1,0:T(8,128)(2,1)S(1)} %get-tuple-element.34.blocks_a_ref, ...), custom_call_target="tpu_custom_call" | custom-call | flops 200000000 | bytes 4000000 | tf_op jit(solution)/shard_map/mirror/pallas_call | solution.py:295
  50.3 5.9 %all-to-all-start.1 = ((f32[8,56,128]{2,1,0:T(8,128)}), f32[8,56,128]{2,1,0:T(8,128)S(1)}, u32[]{:S(2)}, u32[]{:S(2)}) async-start(f32[8,56,128]{2,1,0:T(8,128)} %mirror.3), calls=%async_computation.1 | async-start | bytes 458752 | tf_op jit(solution)/shard_map/all_to_all | solution.py:397
  56.2 3.5 %direct.3.rows_ref = f32[4,56,128]{2,1,0:T(8,128)S(1)} custom-call(s32[4]{0:T(128)S(1)} %pad_add_fusion.me_ref, s32[8,128]{1,0:T(8,128)S(1)} %get-tuple-element.31.pos_a_ref, s32[8,128]{1,0:T(8,128)S(1)} %get-tuple-element.32.pos_b_ref, f32[8,56,128]{2,1,0:T(8,128)S(1)} %pick_half.1.cols_ref, bf16[88,56,128]{2,1,0:T(8,128)(2,1)S(1)} %get-tuple-element.34.blocks_a_ref, ...), custom_call_target="tpu_custom_call" | custom-call | flops 200000000 | bytes 4000000 | tf_op jit(solution)/shard_map/direct/pallas_call | solution.py:295
  59.7 2.9 %all-to-all-done.1.cols_ref = f32[8,56,128]{2,1,0:T(8,128)S(1)} async-done(((f32[8,56,128]{2,1,0:T(8,128)}), f32[8,56,128]{2,1,0:T(8,128)S(1)}, u32[]{:S(2)}, u32[]{:S(2)}) %all-to-all-start.1) | async-done | bytes 229408 | tf_op jit(solution)/shard_map/all_to_all | solution.py:397
  63.2 21.3 %all_to_all.50 = f32[4,4,56,128]{3,2,1,0:T(8,128)S(1)} all-to-all(f32[4,4,56,128]{3,2,1,0:T(8,128)S(1)} %merge.2), channel_id=1, replica_groups=mesh['x'=4,'zl'=2,'core'=2,'zh'=4,'y'=8] {'zh'}, dimensions={0} | all-to-all | bytes 917504 | tf_op jit(solution)/shard_map/all_to_all | solution.py:397
  85.2 4.2 %all-to-all-start.3 = ((f32[8,56,128]{2,1,0:T(8,128)}), f32[8,56,128]{2,1,0:T(8,128)S(1)}, u32[]{:S(2)}, u32[]{:S(2)}) async-start(f32[8,56,128]{2,1,0:T(8,128)} %broadcast_in_dim.11), calls=%async_computation.3 | async-start | bytes 458752 | tf_op jit(solution)/shard_map/all_to_all | solution.py:397
  89.4 3.2 %mirror.4 = f32[8,56,128]{2,1,0:T(8,128)} custom-call(s32[4]{0:T(128)S(1)} %pad_add_fusion.me_ref, s32[8,128]{1,0:T(8,128)S(1)} %get-tuple-element.31.pos_a_ref, s32[8,128]{1,0:T(8,128)S(1)} %get-tuple-element.32.pos_b_ref, f32[4,56,128]{2,1,0:T(8,128)S(1)} %subtract_multiply_fusion.rows_ref.previous_ref, ...), custom_call_target="tpu_custom_call" | custom-call | flops 200000000 | bytes 4000000 | tf_op jit(solution)/shard_map/mirror/pallas_call | solution.py:295
  92.6 2.8 %all-to-all-done.3.cols_ref = f32[8,56,128]{2,1,0:T(8,128)S(1)} async-done(((f32[8,56,128]{2,1,0:T(8,128)}), f32[8,56,128]{2,1,0:T(8,128)S(1)}, u32[]{:S(2)}, u32[]{:S(2)}) %all-to-all-start.3) | async-done | bytes 229408 | tf_op jit(solution)/shard_map/all_to_all | solution.py:397
  95.4 3.4 %all-to-all-start.4 = ((f32[8,56,128]{2,1,0:T(8,128)}), f32[8,56,128]{2,1,0:T(8,128)S(1)}, u32[]{:S(2)}, u32[]{:S(2)}) async-start(f32[8,56,128]{2,1,0:T(8,128)} %mirror.4), calls=%async_computation.4 | async-start | bytes 458752 | tf_op jit(solution)/shard_map/all_to_all | solution.py:397
  98.8 3.5 %direct.4.rows_ref = f32[4,56,128]{2,1,0:T(8,128)S(1)} custom-call(s32[4]{0:T(128)S(1)} %pad_add_fusion.me_ref, s32[8,128]{1,0:T(8,128)S(1)} %get-tuple-element.31.pos_a_ref, s32[8,128]{1,0:T(8,128)S(1)} %get-tuple-element.32.pos_b_ref, f32[8,56,128]{2,1,0:T(8,128)S(1)} %all-to-all-done.3.cols_ref, bf16[88,56,128]{2,1,0:T(8,128)(2,1)S(1)} %get-tuple-element.34.blocks_a_ref, ...), custom_call_target="tpu_custom_call" | custom-call | flops 200000000 | bytes 4000000 | tf_op jit(solution)/shard_map/direct/pallas_call | solution.py:295
  102.3 2.4 %all-to-all-done.4.cols_ref = f32[8,56,128]{2,1,0:T(8,128)S(1)} async-done(((f32[8,56,128]{2,1,0:T(8,128)}), f32[8,56,128]{2,1,0:T(8,128)S(1)}, u32[]{:S(2)}, u32[]{:S(2)}) %all-to-all-start.4) | async-done | bytes 229408 | tf_op jit(solution)/shard_map/all_to_all | solution.py:397
  105.3 14.1 %all_to_all.51 = f32[4,4,56,128]{3,2,1,0:T(8,128)S(1)} all-to-all(f32[4,4,56,128]{3,2,1,0:T(8,128)S(1)} %merge.3), channel_id=1, replica_groups=mesh['x'=4,'zl'=2,'core'=2,'zh'=4,'y'=8] {'zh'}, dimensions={0} | all-to-all | bytes 917504 | tf_op jit(solution)/shard_map/all_to_all | solution.py:397
  120.2 4.5 %all-to-all-start.6 = ((f32[8,56,128]{2,1,0:T(8,128)}), f32[8,56,128]{2,1,0:T(8,128)S(1)}, u32[]{:S(2)}, u32[]{:S(2)}) async-start(f32[8,56,128]{2,1,0:T(8,128)} %broadcast_in_dim.25), calls=%async_computation.6 | async-start | bytes 458752 | tf_op jit(solution)/shard_map/all_to_all | solution.py:397
  124.7 3.2 %mirror.5 = f32[8,56,128]{2,1,0:T(8,128)} custom-call(s32[4]{0:T(128)S(1)} %pad_add_fusion.me_ref, s32[8,128]{1,0:T(8,128)S(1)} %get-tuple-element.31.pos_a_ref, s32[8,128]{1,0:T(8,128)S(1)} %get-tuple-element.32.pos_b_ref, f32[4,56,128]{2,1,0:T(8,128)S(1)} %multiply_subtract_fusion.rows_ref.current_ref, ...), custom_call_target="tpu_custom_call" | custom-call | flops 200000000 | bytes 4000000 | tf_op jit(solution)/shard_map/mirror/pallas_call | solution.py:295
  127.8 2.8 %all-to-all-done.6.cols_ref = f32[8,56,128]{2,1,0:T(8,128)S(1)} async-done(((f32[8,56,128]{2,1,0:T(8,128)}), f32[8,56,128]{2,1,0:T(8,128)S(1)}, u32[]{:S(2)}, u32[]{:S(2)}) %all-to-all-start.6) | async-done | bytes 229408 | tf_op jit(solution)/shard_map/all_to_all | solution.py:397
  130.6 3.4 %all-to-all-start.7 = ((f32[8,56,128]{2,1,0:T(8,128)}), f32[8,56,128]{2,1,0:T(8,128)S(1)}, u32[]{:S(2)}, u32[]{:S(2)}) async-start(f32[8,56,128]{2,1,0:T(8,128)} %mirror.5), calls=%async_computation.7 | async-start | bytes 458752 | tf_op jit(solution)/shard_map/all_to_all | solution.py:397
  134.1 3.5 %direct.5.rows_ref = f32[4,56,128]{2,1,0:T(8,128)S(1)} custom-call(s32[4]{0:T(128)S(1)} %pad_add_fusion.me_ref, s32[8,128]{1,0:T(8,128)S(1)} %get-tuple-element.31.pos_a_ref, s32[8,128]{1,0:T(8,128)S(1)} %get-tuple-element.32.pos_b_ref, f32[8,56,128]{2,1,0:T(8,128)S(1)} %all-to-all-done.6.cols_ref, bf16[88,56,128]{2,1,0:T(8,128)(2,1)S(1)} %get-tuple-element.34.blocks_a_ref, ...), custom_call_target="tpu_custom_call" | custom-call | flops 200000000 | bytes 4000000 | tf_op jit(solution)/shard_map/direct/pallas_call | solution.py:295
  137.5 2.4 %all-to-all-done.7 = f32[8,56,128]{2,1,0:T(8,128)S(1)} async-done(((f32[8,56,128]{2,1,0:T(8,128)}), f32[8,56,128]{2,1,0:T(8,128)S(1)}, u32[]{:S(2)}, u32[]{:S(2)}) %all-to-all-start.7) | async-done | bytes 229408 | tf_op jit(solution)/shard_map/all_to_all | solution.py:397
  141.0 19.4 %all_to_all.52 = f32[8,56,128]{2,1,0:T(8,128)S(1)} all-to-all(f32[8,56,128]{2,1,0:T(8,128)S(1)} %finish.1), channel_id=1, replica_groups=mesh['x'=4,'zl'=2,'core'=2,'zh'=4,'y'=8] {'core','zh'}, dimensions={0} | all-to-all | bytes 458752 | tf_op jit(solution)/shard_map/all_to_all | solution.py:397
  160.5 29.3 %all_to_all.53 = f32[32,56,128]{2,1,0:T(8,128)S(1)} all-to-all(f32[32,56,128]{2,1,0:T(8,128)S(1)} %broadcast_in_dim.26), channel_id=1, replica_groups=mesh['x'=4,'zl'=2,'core'=2,'zh'=4,'y'=8] {'y','zh'}, dimensions={0} | all-to-all | bytes 1835008 | tf_op jit(solution)/shard_map/all_to_all | solution.py:397
  (27 shorter events, 15.4 us)
Async XLA Ops:
  2.2 7.9 %copy-start = (f32[1792,128]{1,0:T(8,128)S(1)}, f32[1792,128]{1,0:T(8,128)}, u32[]{:S(2)}) copy-start(f32[1792,128]{1,0:T(8,128)} %param.4) | copy-start | bytes 2752516
  2.2 37.3 %all-to-all-start = ((f32[8,56,640]{2,1,0:T(8,128)}), f32[8,56,640]{2,1,0:T(8,128)S(1)}, u32[]{:S(2)}, u32[]{:S(2)}) async-start(f32[8,56,640]{2,1,0:T(8,128)} %pack.1), calls=%async_computation | async-start | bytes 2293760 | tf_op jit(solution)/shard_map/all_to_all | solution.py:397
  11.3 25.9 %collective-permute-start = (f32[2,56,128]{2,1,0:T(8,128)S(1)}, f32[2,56,128]{2,1,0:T(8,128)S(1)}, u32[]{:S(2)}, u32[]{:S(2)}) collective-permute-start(f32[2,56,128]{2,1,0:T(8,128)S(1)} %get-tuple-element.28), channel_id=1, source_target_pairs={{0,32},{32,0},{1,33},{33,1},{2,34},{34,2},{3,35},{35,3},{4,36},{36... | collective-permute-start | bytes 172040 | tf_op jit(solution)/shard_map/ppermute | solution.py:415
  39.5 6.6 %collective-permute-start.1 = (f32[8,56,640]{2,1,0:T(8,128)S(1)}, f32[8,56,640]{2,1,0:T(8,128)S(1)}, u32[]{:S(2)}, u32[]{:S(2)}) collective-permute-start(f32[8,56,640]{2,1,0:T(8,128)S(1)} %all-to-all-done.in_ref), channel_id=1, source_target_pairs={{0,32},{32,0},{1,33},{33,1},{2,34},{34,2},{3,35},{35,3},{4,36},{36... | collective-permute-start | bytes 3440648 | tf_op jit(solution)/shard_map/ppermute | solution.py:419
  50.3 12.2 %all-to-all-start.1 = ((f32[8,56,128]{2,1,0:T(8,128)}), f32[8,56,128]{2,1,0:T(8,128)S(1)}, u32[]{:S(2)}, u32[]{:S(2)}) async-start(f32[8,56,128]{2,1,0:T(8,128)} %mirror.3), calls=%async_computation.1 | async-start | bytes 458752 | tf_op jit(solution)/shard_map/all_to_all | solution.py:397
  85.2 10.2 %all-to-all-start.3 = ((f32[8,56,128]{2,1,0:T(8,128)}), f32[8,56,128]{2,1,0:T(8,128)S(1)}, u32[]{:S(2)}, u32[]{:S(2)}) async-start(f32[8,56,128]{2,1,0:T(8,128)} %broadcast_in_dim.11), calls=%async_computation.3 | async-start | bytes 458752 | tf_op jit(solution)/shard_map/all_to_all | solution.py:397
  95.4 9.3 %all-to-all-start.4 = ((f32[8,56,128]{2,1,0:T(8,128)}), f32[8,56,128]{2,1,0:T(8,128)S(1)}, u32[]{:S(2)}, u32[]{:S(2)}) async-start(f32[8,56,128]{2,1,0:T(8,128)} %mirror.4), calls=%async_computation.4 | async-start | bytes 458752 | tf_op jit(solution)/shard_map/all_to_all | solution.py:397
  120.2 10.4 %all-to-all-start.6 = ((f32[8,56,128]{2,1,0:T(8,128)}), f32[8,56,128]{2,1,0:T(8,128)S(1)}, u32[]{:S(2)}, u32[]{:S(2)}) async-start(f32[8,56,128]{2,1,0:T(8,128)} %broadcast_in_dim.25), calls=%async_computation.6 | async-start | bytes 458752 | tf_op jit(solution)/shard_map/all_to_all | solution.py:397
  130.6 9.3 %all-to-all-start.7 = ((f32[8,56,128]{2,1,0:T(8,128)}), f32[8,56,128]{2,1,0:T(8,128)S(1)}, u32[]{:S(2)}, u32[]{:S(2)}) async-start(f32[8,56,128]{2,1,0:T(8,128)} %mirror.5), calls=%async_computation.7 | async-start | bytes 458752 | tf_op jit(solution)/shard_map/all_to_all | solution.py:397

commit v13 on v12

--- a/solution.py
+++ b/solution.py
@@ -247,8 +247,8 @@
     core = me_ref[2]
     parts = ((pos_a_ref, blocks_a_ref, core), (pos_b_ref, blocks_b_ref, 1 - core))
 
-    def two_sources(pair, carry):
-        for s in (2 * pair, 2 * pair + 1):
+    def four_sources(four, carry):
+        for s in (4 * four + k for k in range(4)):
             for t in range(TILES):
                 for pos_ref, blocks_ref, core_s in parts:
                     row, col = row_col(pos_ref, core_s, s, t)
@@ -256,7 +256,7 @@
                     acc_ref[col] += both[:VS] + both[VS:]
         return carry
 
-    lax.fori_loop(0, N_Y // 2, two_sources, 0)
+    lax.fori_loop(0, N_Y // 4, four_sources, 0)
     for chunk in range(out_ref.shape[0]):
         x = acc_ref[chunk * GROUPS : (chunk + 1) * GROUPS].reshape(LANES, LANES)
         x = x + pltpu.roll(x, 64, 1)

time: 193 us -> 192 us (level)
  transfers between devices with their start and end apart: 8 -> 8, of which waited for: 7 -> 7; matrix products, arithmetic and copies ran while one was open for 0% -> 0% of each run, Pallas kernels for 11% -> 10%
where the time goes in v13:
time: 192 us; the launch traced here: 191 us
  blocking collectives  105 us (55%)
  starting transfers between devices  38.1 us (20%)
  Pallas kernels  30.2 us (16%)
  waiting for transfers between devices  16.6 us (9%)
    all_to_all x4, blocking collectives, exchange(): return lax.all_to_all(x, axes, split_axis=0, concat_axis=0, tiled=True)  84.2 us
    all_to_all x6, starting transfers between devices, exchange(): return lax.all_to_all(x, axes, split_axis=0, concat_axis=0, tiled=True)  29.1 us
    all_gather x1, blocking collectives, body(): lax.all_gather(own, ('x', 'zl', 'core'), axis=0, tiled=False)  20.5 us
    pallas_call x6, Pallas kernels, product(): pl.pallas_call(kernel, out_shape=jax.ShapeDtypeStruct((chunks, ORB, LANES...  19.3 us
    all_to_all x6, waiting for transfers between devices, exchange(): return lax.all_to_all(x, axes, split_axis=0, concat_axis=0, tiled=True)  15.2 us
    ppermute x1, starting transfers between devices, body(): current = join_cores(me, mine, lax.ppermute(other, 'core', swap))  4.72 us
    ppermute x1, starting transfers between devices, body(): blocks_b, pos_b = unpack(lax.ppermute(packed, 'core', swap))  4.23 us
  transfers between devices with their start and end apart: 8, of which 7 were waited for; matrix products, arithmetic and copies ran while one was open for 0% of the time, Pallas kernels for 10%

profile of v13, /device:TPU:1, one launch (start us, length us, event | category | flops | bytes accessed | tf_op | source)
XLA Modules:
  0.0 191.4 jit_solution(62508870948632558)
XLA Ops:
  2.2 7.8 %all-to-all-start = ((f32[8,56,640]{2,1,0:T(8,128)}), f32[8,56,640]{2,1,0:T(8,128)S(1)}, u32[]{:S(2)}, u32[]{:S(2)}) async-start(f32[8,56,640]{2,1,0:T(8,128)} %pack.1), calls=%async_computation | async-start | bytes 2293760 | tf_op jit(solution)/shard_map/all_to_all | solution.py:397
  11.3 4.7 %collective-permute-start = (f32[2,56,128]{2,1,0:T(8,128)S(1)}, f32[2,56,128]{2,1,0:T(8,128)S(1)}, u32[]{:S(2)}, u32[]{:S(2)}) collective-permute-start(f32[2,56,128]{2,1,0:T(8,128)S(1)} %get-tuple-element.28), channel_id=1, source_target_pairs={{0,32},{32,0},{1,33},{33,1},{2,34},{34,2},{3,35},{35,3},{4,36},{36... | collective-permute-start | bytes 172040 | tf_op jit(solution)/shard_map/ppermute | solution.py:415
  16.0 20.5 %all-gather = f32[896,128]{1,0:T(8,128)S(1)} all-gather(f32[56,128]{1,0:T(8,128)S(1)} %get-tuple-element.29), channel_id=2, replica_groups=mesh['x'=4,'zl'=2,'core'=2,'zh'=4,'y'=8] {'x','zl','core'}, dimensions={0}, use_global_device_ids=true | all-gather | bytes 487424 | tf_op jit(solution)/shard_map/all_gather | solution.py:414
  39.5 4.2 %collective-permute-start.1 = (f32[8,56,640]{2,1,0:T(8,128)S(1)}, f32[8,56,640]{2,1,0:T(8,128)S(1)}, u32[]{:S(2)}, u32[]{:S(2)}) collective-permute-start(f32[8,56,640]{2,1,0:T(8,128)S(1)} %all-to-all-done.in_ref), channel_id=1, source_target_pairs={{0,32},{32,0},{1,33},{33,1},{2,34},{34,2},{3,35},{35,3},{4,36},{36... | collective-permute-start | bytes 3440648 | tf_op jit(solution)/shard_map/ppermute | solution.py:419
  47.2 3.0 %mirror.3 = f32[8,56,128]{2,1,0:T(8,128)} custom-call(s32[4]{0:T(128)S(1)} %pad_add_fusion.me_ref, s32[8,128]{1,0:T(8,128)S(1)} %get-tuple-element.31.pos_a_ref, s32[8,128]{1,0:T(8,128)S(1)} %get-tuple-element.32.pos_b_ref, f32[4,56,128]{2,1,0:T(8,128)S(1)} %join_cores.1.rows_ref, bf16[88,56,128]{2,1,0:T(8,128)(2,1)S(1)} %get-tuple-element.34.blocks_a_ref, ...), custom_call_target="tpu_custom_call" | custom-call | flops 200000000 | bytes 4000000 | tf_op jit(solution)/shard_map/mirror/pallas_call | solution.py:295
  50.2 5.8 %all-to-all-start.1 = ((f32[8,56,128]{2,1,0:T(8,128)}), f32[8,56,128]{2,1,0:T(8,128)S(1)}, u32[]{:S(2)}, u32[]{:S(2)}) async-start(f32[8,56,128]{2,1,0:T(8,128)} %mirror.3), calls=%async_computation.1 | async-start | bytes 458752 | tf_op jit(solution)/shard_map/all_to_all | solution.py:397
  56.0 3.5 %direct.3.rows_ref = f32[4,56,128]{2,1,0:T(8,128)S(1)} custom-call(s32[4]{0:T(128)S(1)} %pad_add_fusion.me_ref, s32[8,128]{1,0:T(8,128)S(1)} %get-tuple-element.31.pos_a_ref, s32[8,128]{1,0:T(8,128)S(1)} %get-tuple-element.32.pos_b_ref, f32[8,56,128]{2,1,0:T(8,128)S(1)} %pick_half.1.cols_ref, bf16[88,56,128]{2,1,0:T(8,128)(2,1)S(1)} %get-tuple-element.34.blocks_a_ref, ...), custom_call_target="tpu_custom_call" | custom-call | flops 200000000 | bytes 4000000 | tf_op jit(solution)/shard_map/direct/pallas_call | solution.py:295
  59.5 2.9 %all-to-all-done.1.cols_ref = f32[8,56,128]{2,1,0:T(8,128)S(1)} async-done(((f32[8,56,128]{2,1,0:T(8,128)}), f32[8,56,128]{2,1,0:T(8,128)S(1)}, u32[]{:S(2)}, u32[]{:S(2)}) %all-to-all-start.1) | async-done | bytes 229408 | tf_op jit(solution)/shard_map/all_to_all | solution.py:397
  62.9 21.3 %all_to_all.50 = f32[4,4,56,128]{3,2,1,0:T(8,128)S(1)} all-to-all(f32[4,4,56,128]{3,2,1,0:T(8,128)S(1)} %merge.2), channel_id=1, replica_groups=mesh['x'=4,'zl'=2,'core'=2,'zh'=4,'y'=8] {'zh'}, dimensions={0} | all-to-all | bytes 917504 | tf_op jit(solution)/shard_map/all_to_all | solution.py:397
  85.1 4.2 %all-to-all-start.3 = ((f32[8,56,128]{2,1,0:T(8,128)}), f32[8,56,128]{2,1,0:T(8,128)S(1)}, u32[]{:S(2)}, u32[]{:S(2)}) async-start(f32[8,56,128]{2,1,0:T(8,128)} %broadcast_in_dim.11), calls=%async_computation.3 | async-start | bytes 458752 | tf_op jit(solution)/shard_map/all_to_all | solution.py:397
  89.3 3.0 %mirror.4 = f32[8,56,128]{2,1,0:T(8,128)} custom-call(s32[4]{0:T(128)S(1)} %pad_add_fusion.me_ref, s32[8,128]{1,0:T(8,128)S(1)} %get-tuple-element.31.pos_a_ref, s32[8,128]{1,0:T(8,128)S(1)} %get-tuple-element.32.pos_b_ref, f32[4,56,128]{2,1,0:T(8,128)S(1)} %subtract_multiply_fusion.rows_ref.previous_ref, ...), custom_call_target="tpu_custom_call" | custom-call | flops 200000000 | bytes 4000000 | tf_op jit(solution)/shard_map/mirror/pallas_call | solution.py:295
  92.2 3.0 %all-to-all-done.3.cols_ref = f32[8,56,128]{2,1,0:T(8,128)S(1)} async-done(((f32[8,56,128]{2,1,0:T(8,128)}), f32[8,56,128]{2,1,0:T(8,128)S(1)}, u32[]{:S(2)}, u32[]{:S(2)}) %all-to-all-start.3) | async-done | bytes 229408 | tf_op jit(solution)/shard_map/all_to_all | solution.py:397
  95.2 3.4 %all-to-all-start.4 = ((f32[8,56,128]{2,1,0:T(8,128)}), f32[8,56,128]{2,1,0:T(8,128)S(1)}, u32[]{:S(2)}, u32[]{:S(2)}) async-start(f32[8,56,128]{2,1,0:T(8,128)} %mirror.4), calls=%async_computation.4 | async-start | bytes 458752 | tf_op jit(solution)/shard_map/all_to_all | solution.py:397
  98.6 3.5 %direct.4.rows_ref = f32[4,56,128]{2,1,0:T(8,128)S(1)} custom-call(s32[4]{0:T(128)S(1)} %pad_add_fusion.me_ref, s32[8,128]{1,0:T(8,128)S(1)} %get-tuple-element.31.pos_a_ref, s32[8,128]{1,0:T(8,128)S(1)} %get-tuple-element.32.pos_b_ref, f32[8,56,128]{2,1,0:T(8,128)S(1)} %all-to-all-done.3.cols_ref, bf16[88,56,128]{2,1,0:T(8,128)(2,1)S(1)} %get-tuple-element.34.blocks_a_ref, ...), custom_call_target="tpu_custom_call" | custom-call | flops 200000000 | bytes 4000000 | tf_op jit(solution)/shard_map/direct/pallas_call | solution.py:295
  102.1 2.4 %all-to-all-done.4.cols_ref = f32[8,56,128]{2,1,0:T(8,128)S(1)} async-done(((f32[8,56,128]{2,1,0:T(8,128)}), f32[8,56,128]{2,1,0:T(8,128)S(1)}, u32[]{:S(2)}, u32[]{:S(2)}) %all-to-all-start.4) | async-done | bytes 229408 | tf_op jit(solution)/shard_map/all_to_all | solution.py:397
  105.1 14.2 %all_to_all.51 = f32[4,4,56,128]{3,2,1,0:T(8,128)S(1)} all-to-all(f32[4,4,56,128]{3,2,1,0:T(8,128)S(1)} %merge.3), channel_id=1, replica_groups=mesh['x'=4,'zl'=2,'core'=2,'zh'=4,'y'=8] {'zh'}, dimensions={0} | all-to-all | bytes 917504 | tf_op jit(solution)/shard_map/all_to_all | solution.py:397
  120.1 4.5 %all-to-all-start.6 = ((f32[8,56,128]{2,1,0:T(8,128)}), f32[8,56,128]{2,1,0:T(8,128)S(1)}, u32[]{:S(2)}, u32[]{:S(2)}) async-start(f32[8,56,128]{2,1,0:T(8,128)} %broadcast_in_dim.25), calls=%async_computation.6 | async-start | bytes 458752 | tf_op jit(solution)/shard_map/all_to_all | solution.py:397
  124.5 3.0 %mirror.5 = f32[8,56,128]{2,1,0:T(8,128)} custom-call(s32[4]{0:T(128)S(1)} %pad_add_fusion.me_ref, s32[8,128]{1,0:T(8,128)S(1)} %get-tuple-element.31.pos_a_ref, s32[8,128]{1,0:T(8,128)S(1)} %get-tuple-element.32.pos_b_ref, f32[4,56,128]{2,1,0:T(8,128)S(1)} %multiply_subtract_fusion.rows_ref.current_ref, ...), custom_call_target="tpu_custom_call" | custom-call | flops 200000000 | bytes 4000000 | tf_op jit(solution)/shard_map/mirror/pallas_call | solution.py:295
  127.5 3.0 %all-to-all-done.6.cols_ref = f32[8,56,128]{2,1,0:T(8,128)S(1)} async-done(((f32[8,56,128]{2,1,0:T(8,128)}), f32[8,56,128]{2,1,0:T(8,128)S(1)}, u32[]{:S(2)}, u32[]{:S(2)}) %all-to-all-start.6) | async-done | bytes 229408 | tf_op jit(solution)/shard_map/all_to_all | solution.py:397
  130.5 3.4 %all-to-all-start.7 = ((f32[8,56,128]{2,1,0:T(8,128)}), f32[8,56,128]{2,1,0:T(8,128)S(1)}, u32[]{:S(2)}, u32[]{:S(2)}) async-start(f32[8,56,128]{2,1,0:T(8,128)} %mirror.5), calls=%async_computation.7 | async-start | bytes 458752 | tf_op jit(solution)/shard_map/all_to_all | solution.py:397
  133.9 3.5 %direct.5.rows_ref = f32[4,56,128]{2,1,0:T(8,128)S(1)} custom-call(s32[4]{0:T(128)S(1)} %pad_add_fusion.me_ref, s32[8,128]{1,0:T(8,128)S(1)} %get-tuple-element.31.pos_a_ref, s32[8,128]{1,0:T(8,128)S(1)} %get-tuple-element.32.pos_b_ref, f32[8,56,128]{2,1,0:T(8,128)S(1)} %all-to-all-done.6.cols_ref, bf16[88,56,128]{2,1,0:T(8,128)(2,1)S(1)} %get-tuple-element.34.blocks_a_ref, ...), custom_call_target="tpu_custom_call" | custom-call | flops 200000000 | bytes 4000000 | tf_op jit(solution)/shard_map/direct/pallas_call | solution.py:295
  137.4 2.4 %all-to-all-done.7 = f32[8,56,128]{2,1,0:T(8,128)S(1)} async-done(((f32[8,56,128]{2,1,0:T(8,128)}), f32[8,56,128]{2,1,0:T(8,128)S(1)}, u32[]{:S(2)}, u32[]{:S(2)}) %all-to-all-start.7) | async-done | bytes 229408 | tf_op jit(solution)/shard_map/all_to_all | solution.py:397
  140.8 19.4 %all_to_all.52 = f32[8,56,128]{2,1,0:T(8,128)S(1)} all-to-all(f32[8,56,128]{2,1,0:T(8,128)S(1)} %finish.1), channel_id=1, replica_groups=mesh['x'=4,'zl'=2,'core'=2,'zh'=4,'y'=8] {'core','zh'}, dimensions={0} | all-to-all | bytes 458752 | tf_op jit(solution)/shard_map/all_to_all | solution.py:397
  160.3 29.3 %all_to_all.53 = f32[32,56,128]{2,1,0:T(8,128)S(1)} all-to-all(f32[32,56,128]{2,1,0:T(8,128)S(1)} %broadcast_in_dim.26), channel_id=1, replica_groups=mesh['x'=4,'zl'=2,'core'=2,'zh'=4,'y'=8] {'y','zh'}, dimensions={0} | all-to-all | bytes 1835008 | tf_op jit(solution)/shard_map/all_to_all | solution.py:397
  (27 shorter events, 15.4 us)
Async XLA Ops:
  2.2 7.9 %copy-start = (f32[1792,128]{1,0:T(8,128)S(1)}, f32[1792,128]{1,0:T(8,128)}, u32[]{:S(2)}) copy-start(f32[1792,128]{1,0:T(8,128)} %param.4) | copy-start | bytes 2752516
  2.2 37.3 %all-to-all-start = ((f32[8,56,640]{2,1,0:T(8,128)}), f32[8,56,640]{2,1,0:T(8,128)S(1)}, u32[]{:S(2)}, u32[]{:S(2)}) async-start(f32[8,56,640]{2,1,0:T(8,128)} %pack.1), calls=%async_computation | async-start | bytes 2293760 | tf_op jit(solution)/shard_map/all_to_all | solution.py:397
  11.3 25.9 %collective-permute-start = (f32[2,56,128]{2,1,0:T(8,128)S(1)}, f32[2,56,128]{2,1,0:T(8,128)S(1)}, u32[]{:S(2)}, u32[]{:S(2)}) collective-permute-start(f32[2,56,128]{2,1,0:T(8,128)S(1)} %get-tuple-element.28), channel_id=1, source_target_pairs={{0,32},{32,0},{1,33},{33,1},{2,34},{34,2},{3,35},{35,3},{4,36},{36... | collective-permute-start | bytes 172040 | tf_op jit(solution)/shard_map/ppermute | solution.py:415
  39.5 6.6 %collective-permute-start.1 = (f32[8,56,640]{2,1,0:T(8,128)S(1)}, f32[8,56,640]{2,1,0:T(8,128)S(1)}, u32[]{:S(2)}, u32[]{:S(2)}) collective-permute-start(f32[8,56,640]{2,1,0:T(8,128)S(1)} %all-to-all-done.in_ref), channel_id=1, source_target_pairs={{0,32},{32,0},{1,33},{33,1},{2,34},{34,2},{3,35},{35,3},{4,36},{36... | collective-permute-start | bytes 3440648 | tf_op jit(solution)/shard_map/ppermute | solution.py:419
  50.2 12.2 %all-to-all-start.1 = ((f32[8,56,128]{2,1,0:T(8,128)}), f32[8,56,128]{2,1,0:T(8,128)S(1)}, u32[]{:S(2)}, u32[]{:S(2)}) async-start(f32[8,56,128]{2,1,0:T(8,128)} %mirror.3), calls=%async_computation.1 | async-start | bytes 458752 | tf_op jit(solution)/shard_map/all_to_all | solution.py:397
  85.1 10.2 %all-to-all-start.3 = ((f32[8,56,128]{2,1,0:T(8,128)}), f32[8,56,128]{2,1,0:T(8,128)S(1)}, u32[]{:S(2)}, u32[]{:S(2)}) async-start(f32[8,56,128]{2,1,0:T(8,128)} %broadcast_in_dim.11), calls=%async_computation.3 | async-start | bytes 458752 | tf_op jit(solution)/shard_map/all_to_all | solution.py:397
  95.2 9.3 %all-to-all-start.4 = ((f32[8,56,128]{2,1,0:T(8,128)}), f32[8,56,128]{2,1,0:T(8,128)S(1)}, u32[]{:S(2)}, u32[]{:S(2)}) async-start(f32[8,56,128]{2,1,0:T(8,128)} %mirror.4), calls=%async_computation.4 | async-start | bytes 458752 | tf_op jit(solution)/shard_map/all_to_all | solution.py:397
  120.1 10.4 %all-to-all-start.6 = ((f32[8,56,128]{2,1,0:T(8,128)}), f32[8,56,128]{2,1,0:T(8,128)S(1)}, u32[]{:S(2)}, u32[]{:S(2)}) async-start(f32[8,56,128]{2,1,0:T(8,128)} %broadcast_in_dim.25), calls=%async_computation.6 | async-start | bytes 458752 | tf_op jit(solution)/shard_map/all_to_all | solution.py:397
  130.5 9.3 %all-to-all-start.7 = ((f32[8,56,128]{2,1,0:T(8,128)}), f32[8,56,128]{2,1,0:T(8,128)S(1)}, u32[]{:S(2)}, u32[]{:S(2)}) async-start(f32[8,56,128]{2,1,0:T(8,128)} %mirror.5), calls=%async_computation.7 | async-start | bytes 458752 | tf_op jit(solution)/shard_map/all_to_all | solution.py:397

commit v14 on v12

--- a/solution.py
+++ b/solution.py
@@ -411,10 +411,12 @@
     packed = exchange(packed, "y")
 
     mine, other, own = slice_vectors(me, vectors.reshape(-1, ORB, LANES))
-    cols = pick_half(me, lax.all_gather(own, ("x", "zl", "core"), axis=0, tiled=False))
-    current = join_cores(me, mine, lax.ppermute(other, "core", swap))
-
-    packed, current, cols = lax.optimization_barrier((packed, current, cols))
+    gathered = lax.all_gather(own, ("x", "zl", "core"), axis=0, tiled=False)
+    other = lax.ppermute(other, "core", swap)
+
+    packed, gathered, mine, other = lax.optimization_barrier((packed, gathered, mine, other))
+    cols = pick_half(me, gathered)
+    current = join_cores(me, mine, other)
     blocks_a, pos_a = unpack(packed)
     blocks_b, pos_b = unpack(lax.ppermute(packed, "core", swap))
     where, blocks = (me, pos_a, pos_b), (blocks_a, blocks_b)

time: 193 us -> 193 us (level)
  transfers between devices with their start and end apart: 8 -> 8, of which waited for: 7 -> 6; matrix products, arithmetic and copies ran while one was open for 0% -> 0% of each run, Pallas kernels for 11% -> 11%
where the time goes in v14:
time: 193 us; the launch traced here: 192 us
  blocking collectives  106 us (55%)
  starting transfers between devices  37.3 us (19%)
  Pallas kernels  30.7 us (16%)
  waiting for transfers between devices  16.3 us (8%)
    all_to_all x4, blocking collectives, exchange(): return lax.all_to_all(x, axes, split_axis=0, concat_axis=0, tiled=True)  85.2 us
    all_to_all x6, starting transfers between devices, exchange(): return lax.all_to_all(x, axes, split_axis=0, concat_axis=0, tiled=True)  28.4 us
    all_gather x1, blocking collectives, body(): gathered = lax.all_gather(own, ('x', 'zl', 'core'), axis=0, tiled=False)  20.5 us
    pallas_call x6, Pallas kernels, product(): pl.pallas_call(kernel, out_shape=jax.ShapeDtypeStruct((chunks, ORB, LANES...  19.8 us
    all_to_all x6, waiting for transfers between devices, exchange(): return lax.all_to_all(x, axes, split_axis=0, concat_axis=0, tiled=True)  16.3 us
    ppermute x1, starting transfers between devices, body(): other = lax.ppermute(other, 'core', swap)  4.72 us
    ppermute x1, starting transfers between devices, body(): blocks_b, pos_b = unpack(lax.ppermute(packed, 'core', swap))  4.23 us
  transfers between devices with their start and end apart: 8, of which 6 were waited for; matrix products, arithmetic and copies ran while one was open for 0% of the time, Pallas kernels for 11%

profile of v14, /device:TPU:1, one launch (start us, length us, event | category | flops | bytes accessed | tf_op | source)
XLA Modules:
  0.0 192.0 jit_solution(17827809029512665501)
XLA Ops:
  2.2 7.8 %all-to-all-start = ((f32[8,56,640]{2,1,0:T(8,128)}), f32[8,56,640]{2,1,0:T(8,128)S(1)}, u32[]{:S(2)}, u32[]{:S(2)}) async-start(f32[8,56,640]{2,1,0:T(8,128)} %pack.1), calls=%async_computation | async-start | bytes 2293760 | tf_op jit(solution)/shard_map/all_to_all | solution.py:397
  11.3 4.7 %collective-permute-start = (f32[2,56,128]{2,1,0:T(8,128)S(1)}, f32[2,56,128]{2,1,0:T(8,128)S(1)}, u32[]{:S(2)}, u32[]{:S(2)}) collective-permute-start(f32[2,56,128]{2,1,0:T(8,128)S(1)} %get-tuple-element.30), channel_id=1, source_target_pairs={{0,32},{32,0},{1,33},{33,1},{2,34},{34,2},{3,35},{35,3},{4,36},{36... | collective-permute-start | bytes 172040 | tf_op jit(solution)/shard_map/ppermute | solution.py:415
  16.0 20.5 %all-gather = f32[896,128]{1,0:T(8,128)S(1)} all-gather(f32[56,128]{1,0:T(8,128)S(1)} %get-tuple-element.28), channel_id=2, replica_groups=mesh['x'=4,'zl'=2,'core'=2,'zh'=4,'y'=8] {'x','zl','core'}, dimensions={0}, use_global_device_ids=true | all-gather | bytes 487424 | tf_op jit(solution)/shard_map/all_gather | solution.py:414
  36.5 3.0 %all-to-all-done.in_ref = f32[8,56,640]{2,1,0:T(8,128)S(1)} async-done(((f32[8,56,640]{2,1,0:T(8,128)}), f32[8,56,640]{2,1,0:T(8,128)S(1)}, u32[]{:S(2)}, u32[]{:S(2)}) %all-to-all-start) | async-done | bytes 1146912 | tf_op jit(solution)/shard_map/all_to_all | solution.py:397
  39.5 4.2 %collective-permute-start.1 = (f32[8,56,640]{2,1,0:T(8,128)S(1)}, f32[8,56,640]{2,1,0:T(8,128)S(1)}, u32[]{:S(2)}, u32[]{:S(2)}) collective-permute-start(f32[8,56,640]{2,1,0:T(8,128)S(1)} %all-to-all-done.in_ref), channel_id=1, source_target_pairs={{0,32},{32,0},{1,33},{33,1},{2,34},{34,2},{3,35},{35,3},{4,36},{36... | collective-permute-start | bytes 3440648 | tf_op jit(solution)/shard_map/ppermute | solution.py:421
  47.2 3.2 %mirror.3 = f32[8,56,128]{2,1,0:T(8,128)} custom-call(s32[4]{0:T(128)S(1)} %pad_add_fusion.me_ref, s32[8,128]{1,0:T(8,128)S(1)} %get-tuple-element.32.pos_a_ref, s32[8,128]{1,0:T(8,128)S(1)} %get-tuple-element.33.pos_b_ref, f32[4,56,128]{2,1,0:T(8,128)S(1)} %join_cores.1.rows_ref, bf16[88,56,128]{2,1,0:T(8,128)(2,1)S(1)} %get-tuple-element.36.blocks_a_ref, ...), custom_call_target="tpu_custom_call" | custom-call | flops 200000000 | bytes 4000000 | tf_op jit(solution)/shard_map/mirror/pallas_call | solution.py:295
  50.4 5.9 %all-to-all-start.1 = ((f32[8,56,128]{2,1,0:T(8,128)}), f32[8,56,128]{2,1,0:T(8,128)S(1)}, u32[]{:S(2)}, u32[]{:S(2)}) async-start(f32[8,56,128]{2,1,0:T(8,128)} %mirror.3), calls=%async_computation.1 | async-start | bytes 458752 | tf_op jit(solution)/shard_map/all_to_all | solution.py:397
  56.2 3.5 %direct.3.rows_ref = f32[4,56,128]{2,1,0:T(8,128)S(1)} custom-call(s32[4]{0:T(128)S(1)} %pad_add_fusion.me_ref, s32[8,128]{1,0:T(8,128)S(1)} %get-tuple-element.32.pos_a_ref, s32[8,128]{1,0:T(8,128)S(1)} %get-tuple-element.33.pos_b_ref, f32[8,56,128]{2,1,0:T(8,128)S(1)} %pick_half.1.cols_ref, bf16[88,56,128]{2,1,0:T(8,128)(2,1)S(1)} %get-tuple-element.36.blocks_a_ref, ...), custom_call_target="tpu_custom_call" | custom-call | flops 200000000 | bytes 4000000 | tf_op jit(solution)/shard_map/direct/pallas_call | solution.py:295
  59.7 2.9 %all-to-all-done.1.cols_ref = f32[8,56,128]{2,1,0:T(8,128)S(1)} async-done(((f32[8,56,128]{2,1,0:T(8,128)}), f32[8,56,128]{2,1,0:T(8,128)S(1)}, u32[]{:S(2)}, u32[]{:S(2)}) %all-to-all-start.1) | async-done | bytes 229408 | tf_op jit(solution)/shard_map/all_to_all | solution.py:397
  63.2 21.4 %all_to_all.50 = f32[4,4,56,128]{3,2,1,0:T(8,128)S(1)} all-to-all(f32[4,4,56,128]{3,2,1,0:T(8,128)S(1)} %merge.2), channel_id=1, replica_groups=mesh['x'=4,'zl'=2,'core'=2,'zh'=4,'y'=8] {'zh'}, dimensions={0} | all-to-all | bytes 917504 | tf_op jit(solution)/shard_map/all_to_all | solution.py:397
  85.4 4.2 %all-to-all-start.3 = ((f32[8,56,128]{2,1,0:T(8,128)}), f32[8,56,128]{2,1,0:T(8,128)S(1)}, u32[]{:S(2)}, u32[]{:S(2)}) async-start(f32[8,56,128]{2,1,0:T(8,128)} %broadcast_in_dim.11), calls=%async_computation.3 | async-start | bytes 458752 | tf_op jit(solution)/shard_map/all_to_all | solution.py:397
  89.6 3.1 %mirror.4 = f32[8,56,128]{2,1,0:T(8,128)} custom-call(s32[4]{0:T(128)S(1)} %pad_add_fusion.me_ref, s32[8,128]{1,0:T(8,128)S(1)} %get-tuple-element.32.pos_a_ref, s32[8,128]{1,0:T(8,128)S(1)} %get-tuple-element.33.pos_b_ref, f32[4,56,128]{2,1,0:T(8,128)S(1)} %subtract_multiply_fusion.rows_ref.previous_ref, ...), custom_call_target="tpu_custom_call" | custom-call | flops 200000000 | bytes 4000000 | tf_op jit(solution)/shard_map/mirror/pallas_call | solution.py:295
  92.7 2.8 %all-to-all-done.3.cols_ref = f32[8,56,128]{2,1,0:T(8,128)S(1)} async-done(((f32[8,56,128]{2,1,0:T(8,128)}), f32[8,56,128]{2,1,0:T(8,128)S(1)}, u32[]{:S(2)}, u32[]{:S(2)}) %all-to-all-start.3) | async-done | bytes 229408 | tf_op jit(solution)/shard_map/all_to_all | solution.py:397
  95.6 3.4 %all-to-all-start.4 = ((f32[8,56,128]{2,1,0:T(8,128)}), f32[8,56,128]{2,1,0:T(8,128)S(1)}, u32[]{:S(2)}, u32[]{:S(2)}) async-start(f32[8,56,128]{2,1,0:T(8,128)} %mirror.4), calls=%async_computation.4 | async-start | bytes 458752 | tf_op jit(solution)/shard_map/all_to_all | solution.py:397
  99.0 3.5 %direct.4.rows_ref = f32[4,56,128]{2,1,0:T(8,128)S(1)} custom-call(s32[4]{0:T(128)S(1)} %pad_add_fusion.me_ref, s32[8,128]{1,0:T(8,128)S(1)} %get-tuple-element.32.pos_a_ref, s32[8,128]{1,0:T(8,128)S(1)} %get-tuple-element.33.pos_b_ref, f32[8,56,128]{2,1,0:T(8,128)S(1)} %all-to-all-done.3.cols_ref, bf16[88,56,128]{2,1,0:T(8,128)(2,1)S(1)} %get-tuple-element.36.blocks_a_ref, ...), custom_call_target="tpu_custom_call" | custom-call | flops 200000000 | bytes 4000000 | tf_op jit(solution)/shard_map/direct/pallas_call | solution.py:295
  102.4 2.4 %all-to-all-done.4.cols_ref = f32[8,56,128]{2,1,0:T(8,128)S(1)} async-done(((f32[8,56,128]{2,1,0:T(8,128)}), f32[8,56,128]{2,1,0:T(8,128)S(1)}, u32[]{:S(2)}, u32[]{:S(2)}) %all-to-all-start.4) | async-done | bytes 229408 | tf_op jit(solution)/shard_map/all_to_all | solution.py:397
  105.5 14.6 %all_to_all.51 = f32[4,4,56,128]{3,2,1,0:T(8,128)S(1)} all-to-all(f32[4,4,56,128]{3,2,1,0:T(8,128)S(1)} %merge.3), channel_id=1, replica_groups=mesh['x'=4,'zl'=2,'core'=2,'zh'=4,'y'=8] {'zh'}, dimensions={0} | all-to-all | bytes 917504 | tf_op jit(solution)/shard_map/all_to_all | solution.py:397
  120.8 3.7 %all-to-all-start.6 = ((f32[8,56,128]{2,1,0:T(8,128)}), f32[8,56,128]{2,1,0:T(8,128)S(1)}, u32[]{:S(2)}, u32[]{:S(2)}) async-start(f32[8,56,128]{2,1,0:T(8,128)} %broadcast_in_dim.25), calls=%async_computation.6 | async-start | bytes 458752 | tf_op jit(solution)/shard_map/all_to_all | solution.py:397
  124.6 3.1 %mirror.5 = f32[8,56,128]{2,1,0:T(8,128)} custom-call(s32[4]{0:T(128)S(1)} %pad_add_fusion.me_ref, s32[8,128]{1,0:T(8,128)S(1)} %get-tuple-element.32.pos_a_ref, s32[8,128]{1,0:T(8,128)S(1)} %get-tuple-element.33.pos_b_ref, f32[4,56,128]{2,1,0:T(8,128)S(1)} %multiply_subtract_fusion.rows_ref.current_ref, ...), custom_call_target="tpu_custom_call" | custom-call | flops 200000000 | bytes 4000000 | tf_op jit(solution)/shard_map/mirror/pallas_call | solution.py:295
  127.7 2.8 %all-to-all-done.6.cols_ref = f32[8,56,128]{2,1,0:T(8,128)S(1)} async-done(((f32[8,56,128]{2,1,0:T(8,128)}), f32[8,56,128]{2,1,0:T(8,128)S(1)}, u32[]{:S(2)}, u32[]{:S(2)}) %all-to-all-start.6) | async-done | bytes 229408 | tf_op jit(solution)/shard_map/all_to_all | solution.py:397
  130.5 3.4 %all-to-all-start.7 = ((f32[8,56,128]{2,1,0:T(8,128)}), f32[8,56,128]{2,1,0:T(8,128)S(1)}, u32[]{:S(2)}, u32[]{:S(2)}) async-start(f32[8,56,128]{2,1,0:T(8,128)} %mirror.5), calls=%async_computation.7 | async-start | bytes 458752 | tf_op jit(solution)/shard_map/all_to_all | solution.py:397
  133.9 3.5 %direct.5.rows_ref = f32[4,56,128]{2,1,0:T(8,128)S(1)} custom-call(s32[4]{0:T(128)S(1)} %pad_add_fusion.me_ref, s32[8,128]{1,0:T(8,128)S(1)} %get-tuple-element.32.pos_a_ref, s32[8,128]{1,0:T(8,128)S(1)} %get-tuple-element.33.pos_b_ref, f32[8,56,128]{2,1,0:T(8,128)S(1)} %all-to-all-done.6.cols_ref, bf16[88,56,128]{2,1,0:T(8,128)(2,1)S(1)} %get-tuple-element.36.blocks_a_ref, ...), custom_call_target="tpu_custom_call" | custom-call | flops 200000000 | bytes 4000000 | tf_op jit(solution)/shard_map/direct/pallas_call | solution.py:295
  140.9 19.9 %all_to_all.52 = f32[8,56,128]{2,1,0:T(8,128)S(1)} all-to-all(f32[8,56,128]{2,1,0:T(8,128)S(1)} %finish.1), channel_id=1, replica_groups=mesh['x'=4,'zl'=2,'core'=2,'zh'=4,'y'=8] {'core','zh'}, dimensions={0} | all-to-all | bytes 458752 | tf_op jit(solution)/shard_map/all_to_all | solution.py:397
  160.9 29.3 %all_to_all.53 = f32[32,56,128]{2,1,0:T(8,128)S(1)} all-to-all(f32[32,56,128]{2,1,0:T(8,128)S(1)} %broadcast_in_dim.26), channel_id=1, replica_groups=mesh['x'=4,'zl'=2,'core'=2,'zh'=4,'y'=8] {'y','zh'}, dimensions={0} | all-to-all | bytes 1835008 | tf_op jit(solution)/shard_map/all_to_all | solution.py:397
  (27 shorter events, 14.9 us)
Async XLA Ops:
  2.2 7.9 %copy-start = (f32[1792,128]{1,0:T(8,128)S(1)}, f32[1792,128]{1,0:T(8,128)}, u32[]{:S(2)}) copy-start(f32[1792,128]{1,0:T(8,128)} %param.4) | copy-start | bytes 2752516
  2.2 37.3 %all-to-all-start = ((f32[8,56,640]{2,1,0:T(8,128)}), f32[8,56,640]{2,1,0:T(8,128)S(1)}, u32[]{:S(2)}, u32[]{:S(2)}) async-start(f32[8,56,640]{2,1,0:T(8,128)} %pack.1), calls=%async_computation | async-start | bytes 2293760 | tf_op jit(solution)/shard_map/all_to_all | solution.py:397
  11.3 25.2 %collective-permute-start = (f32[2,56,128]{2,1,0:T(8,128)S(1)}, f32[2,56,128]{2,1,0:T(8,128)S(1)}, u32[]{:S(2)}, u32[]{:S(2)}) collective-permute-start(f32[2,56,128]{2,1,0:T(8,128)S(1)} %get-tuple-element.30), channel_id=1, source_target_pairs={{0,32},{32,0},{1,33},{33,1},{2,34},{34,2},{3,35},{35,3},{4,36},{36... | collective-permute-start | bytes 172040 | tf_op jit(solution)/shard_map/ppermute | solution.py:415
  39.5 6.7 %collective-permute-start.1 = (f32[8,56,640]{2,1,0:T(8,128)S(1)}, f32[8,56,640]{2,1,0:T(8,128)S(1)}, u32[]{:S(2)}, u32[]{:S(2)}) collective-permute-start(f32[8,56,640]{2,1,0:T(8,128)S(1)} %all-to-all-done.in_ref), channel_id=1, source_target_pairs={{0,32},{32,0},{1,33},{33,1},{2,34},{34,2},{3,35},{35,3},{4,36},{36... | collective-permute-start | bytes 3440648 | tf_op jit(solution)/shard_map/ppermute | solution.py:421
  50.4 12.2 %all-to-all-start.1 = ((f32[8,56,128]{2,1,0:T(8,128)}), f32[8,56,128]{2,1,0:T(8,128)S(1)}, u32[]{:S(2)}, u32[]{:S(2)}) async-start(f32[8,56,128]{2,1,0:T(8,128)} %mirror.3), calls=%async_computation.1 | async-start | bytes 458752 | tf_op jit(solution)/shard_map/all_to_all | solution.py:397
  85.4 10.2 %all-to-all-start.3 = ((f32[8,56,128]{2,1,0:T(8,128)}), f32[8,56,128]{2,1,0:T(8,128)S(1)}, u32[]{:S(2)}, u32[]{:S(2)}) async-start(f32[8,56,128]{2,1,0:T(8,128)} %broadcast_in_dim.11), calls=%async_computation.3 | async-start | bytes 458752 | tf_op jit(solution)/shard_map/all_to_all | solution.py:397
  95.6 9.3 %all-to-all-start.4 = ((f32[8,56,128]{2,1,0:T(8,128)}), f32[8,56,128]{2,1,0:T(8,128)S(1)}, u32[]{:S(2)}, u32[]{:S(2)}) async-start(f32[8,56,128]{2,1,0:T(8,128)} %mirror.4), calls=%async_computation.4 | async-start | bytes 458752 | tf_op jit(solution)/shard_map/all_to_all | solution.py:397
  120.8 9.7 %all-to-all-start.6 = ((f32[8,56,128]{2,1,0:T(8,128)}), f32[8,56,128]{2,1,0:T(8,128)S(1)}, u32[]{:S(2)}, u32[]{:S(2)}) async-start(f32[8,56,128]{2,1,0:T(8,128)} %broadcast_in_dim.25), calls=%async_computation.6 | async-start | bytes 458752 | tf_op jit(solution)/shard_map/all_to_all | solution.py:397
  130.5 9.3 %all-to-all-start.7 = ((f32[8,56,128]{2,1,0:T(8,128)}), f32[8,56,128]{2,1,0:T(8,128)S(1)}, u32[]{:S(2)}, u32[]{:S(2)}) async-start(f32[8,56,128]{2,1,0:T(8,128)} %mirror.5), calls=%async_computation.7 | async-start | bytes 458752 | tf_op jit(solution)/shard_map/all_to_all | solution.py:397

commit v15 on v12

--- a/solution.py
+++ b/solution.py
@@ -243,6 +243,10 @@
 
 def mirror_kernel(me_ref, pos_a_ref, pos_b_ref, rows_ref, blocks_a_ref, blocks_b_ref, out_ref, v_ref, acc_ref):
     split_terms(rows_ref, v_ref)
+    mirror_split_kernel(me_ref, pos_a_ref, pos_b_ref, v_ref, blocks_a_ref, blocks_b_ref, out_ref, acc_ref)
+
+
+def mirror_split_kernel(me_ref, pos_a_ref, pos_b_ref, v_ref, blocks_a_ref, blocks_b_ref, out_ref, acc_ref):
     acc_ref[...] = jnp.zeros_like(acc_ref)
     core = me_ref[2]
     parts = ((pos_a_ref, blocks_a_ref, core), (pos_b_ref, blocks_b_ref, 1 - core))
@@ -290,6 +294,17 @@
         out_ref[chunk] = x.T[:ORB]
 
 
+def split(field):
+    return pl.pallas_call(
+        split_terms,
+        out_shape=jax.ShapeDtypeStruct((field.shape[0] * GROUPS, 2 * VS, LANES), bf16),
+        in_specs=vmem(1),
+        out_specs=vmem(1)[0],
+        compiler_params=params(),
+        name="split",
+    )(field)
+
+
 def product(kernel, name, scalars, field, blocks, chunks):
     smem = pl.BlockSpec(memory_space=pltpu.SMEM)
     return pl.pallas_call(
@@ -299,6 +314,7 @@
         out_specs=vmem(1)[0],
         scratch_shapes=[
             pltpu.VMEM((field.shape[0] * GROUPS, 2 * VS, LANES), bf16),
+        ] * (field.dtype == f32) + [
             pltpu.VMEM((chunks * GROUPS, VS, LANES), f32),
         ],
         compiler_params=params(),
@@ -414,14 +430,19 @@
     cols = pick_half(me, lax.all_gather(own, ("x", "zl", "core"), axis=0, tiled=False))
     current = join_cores(me, mine, lax.ppermute(other, "core", swap))
 
-    packed, current, cols = lax.optimization_barrier((packed, current, cols))
+    terms = split(current)
+
+    packed, current, cols, terms = lax.optimization_barrier((packed, current, cols, terms))
     blocks_a, pos_a = unpack(packed)
     blocks_b, pos_b = unpack(lax.ppermute(packed, "core", swap))
     where, blocks = (me, pos_a, pos_b), (blocks_a, blocks_b)
 
     previous = None
     for step in range(DEGREE):
-        out_cols = product(mirror_kernel, "mirror", where, current, blocks, N_R)
+        if step == 0:
+            out_cols = product(mirror_split_kernel, "mirror", where, terms, blocks, N_R)
+        else:
+            out_cols = product(mirror_kernel, "mirror", where, current, blocks, N_R)
         out_cols, cols = lax.optimization_barrier((out_cols, cols))
         got_cols = exchange(out_cols, ROW_AX)
         out_rows = product(direct_kernel, "direct", where, cols, blocks, N_ZH)

time: 193 us -> 192 us (level)
  no operation moved by 1% of the time
where the time goes in v15:
time: 192 us; the launch traced here: 191 us
  blocking collectives  105 us (55%)
  starting transfers between devices  38.1 us (20%)
  Pallas kernels  30.7 us (16%)
  waiting for transfers between devices  16.1 us (8%)
    all_to_all x4, blocking collectives, exchange(): return lax.all_to_all(x, axes, split_axis=0, concat_axis=0, tiled=True)  84.1 us
    all_to_all x6, starting transfers between devices, exchange(): return lax.all_to_all(x, axes, split_axis=0, concat_axis=0, tiled=True)  29.2 us
    all_gather x1, blocking collectives, body(): lax.all_gather(own, ('x', 'zl', 'core'), axis=0, tiled=False)  20.5 us
    pallas_call x6, Pallas kernels, product(): pl.pallas_call(kernel, out_shape=jax.ShapeDtypeStruct((chunks, ORB, LANES...  19.8 us
    all_to_all x6, waiting for transfers between devices, exchange(): return lax.all_to_all(x, axes, split_axis=0, concat_axis=0, tiled=True)  14.7 us
    ppermute x1, starting transfers between devices, body(): current = join_cores(me, mine, lax.ppermute(other, 'core', swap))  4.72 us
    ppermute x1, starting transfers between devices, body(): blocks_b, pos_b = unpack(lax.ppermute(packed, 'core', swap))  4.23 us
  transfers between devices with their start and end apart: 8, of which 7 were waited for; matrix products, arithmetic and copies ran while one was open for 0% of the time, Pallas kernels for 11%

profile of v15, /device:TPU:1, one launch (start us, length us, event | category | flops | bytes accessed | tf_op | source)
XLA Modules:
  0.0 191.4 jit_solution(8486583864284947752)
XLA Ops:
  2.2 7.8 %all-to-all-start = ((f32[8,56,640]{2,1,0:T(8,128)}), f32[8,56,640]{2,1,0:T(8,128)S(1)}, u32[]{:S(2)}, u32[]{:S(2)}) async-start(f32[8,56,640]{2,1,0:T(8,128)} %pack.1), calls=%async_computation | async-start | bytes 2293760 | tf_op jit(solution)/shard_map/all_to_all | solution.py:413
  11.3 4.7 %collective-permute-start = (f32[2,56,128]{2,1,0:T(8,128)S(1)}, f32[2,56,128]{2,1,0:T(8,128)S(1)}, u32[]{:S(2)}, u32[]{:S(2)}) collective-permute-start(f32[2,56,128]{2,1,0:T(8,128)S(1)} %get-tuple-element.29), channel_id=1, source_target_pairs={{0,32},{32,0},{1,33},{33,1},{2,34},{34,2},{3,35},{35,3},{4,36},{36... | collective-permute-start | bytes 172040 | tf_op jit(solution)/shard_map/ppermute | solution.py:431
  16.0 20.5 %all-gather = f32[896,128]{1,0:T(8,128)S(1)} all-gather(f32[56,128]{1,0:T(8,128)S(1)} %get-tuple-element.30), channel_id=2, replica_groups=mesh['x'=4,'zl'=2,'core'=2,'zh'=4,'y'=8] {'x','zl','core'}, dimensions={0}, use_global_device_ids=true | all-gather | bytes 487424 | tf_op jit(solution)/shard_map/all_gather | solution.py:430
  39.5 4.2 %collective-permute-start.1 = (f32[8,56,640]{2,1,0:T(8,128)S(1)}, f32[8,56,640]{2,1,0:T(8,128)S(1)}, u32[]{:S(2)}, u32[]{:S(2)}) collective-permute-start(f32[8,56,640]{2,1,0:T(8,128)S(1)} %all-to-all-done.in_ref), channel_id=1, source_target_pairs={{0,32},{32,0},{1,33},{33,1},{2,34},{34,2},{3,35},{35,3},{4,36},{36... | collective-permute-start | bytes 3440648 | tf_op jit(solution)/shard_map/ppermute | solution.py:437
  47.2 3.1 %mirror.3 = f32[8,56,128]{2,1,0:T(8,128)} custom-call(s32[4]{0:T(128)S(1)} %pad_add_fusion.me_ref, s32[8,128]{1,0:T(8,128)S(1)} %get-tuple-element.32.pos_a_ref, s32[8,128]{1,0:T(8,128)S(1)} %get-tuple-element.33.pos_b_ref, bf16[64,16,128]{2,1,0:T(8,128)(2,1)S(1)} %split.1.v_ref, bf16[88,56,128]{2,1,0:T(8,128)(2,1)S(1)} %get-tuple-element.35.blocks_a_ref, ...), custom_call_target="tpu_custom_call" | custom-call | flops 200000000 | bytes 4000000 | tf_op jit(solution)/shard_map/mirror/pallas_call | solution.py:310
  50.3 5.9 %all-to-all-start.1 = ((f32[8,56,128]{2,1,0:T(8,128)}), f32[8,56,128]{2,1,0:T(8,128)S(1)}, u32[]{:S(2)}, u32[]{:S(2)}) async-start(f32[8,56,128]{2,1,0:T(8,128)} %mirror.3), calls=%async_computation.1 | async-start | bytes 458752 | tf_op jit(solution)/shard_map/all_to_all | solution.py:413
  56.1 3.5 %direct.3.rows_ref = f32[4,56,128]{2,1,0:T(8,128)S(1)} custom-call(s32[4]{0:T(128)S(1)} %pad_add_fusion.me_ref, s32[8,128]{1,0:T(8,128)S(1)} %get-tuple-element.32.pos_a_ref, s32[8,128]{1,0:T(8,128)S(1)} %get-tuple-element.33.pos_b_ref, f32[8,56,128]{2,1,0:T(8,128)S(1)} %pick_half.1.cols_ref, bf16[88,56,128]{2,1,0:T(8,128)(2,1)S(1)} %get-tuple-element.35.blocks_a_ref, ...), custom_call_target="tpu_custom_call" | custom-call | flops 200000000 | bytes 4000000 | tf_op jit(solution)/shard_map/direct/pallas_call | solution.py:310
  59.6 2.9 %all-to-all-done.1.cols_ref = f32[8,56,128]{2,1,0:T(8,128)S(1)} async-done(((f32[8,56,128]{2,1,0:T(8,128)}), f32[8,56,128]{2,1,0:T(8,128)S(1)}, u32[]{:S(2)}, u32[]{:S(2)}) %all-to-all-start.1) | async-done | bytes 229408 | tf_op jit(solution)/shard_map/all_to_all | solution.py:413
  63.0 21.3 %all_to_all.50 = f32[4,4,56,128]{3,2,1,0:T(8,128)S(1)} all-to-all(f32[4,4,56,128]{3,2,1,0:T(8,128)S(1)} %merge.2), channel_id=1, replica_groups=mesh['x'=4,'zl'=2,'core'=2,'zh'=4,'y'=8] {'zh'}, dimensions={0} | all-to-all | bytes 917504 | tf_op jit(solution)/shard_map/all_to_all | solution.py:413
  85.1 4.2 %all-to-all-start.3 = ((f32[8,56,128]{2,1,0:T(8,128)}), f32[8,56,128]{2,1,0:T(8,128)S(1)}, u32[]{:S(2)}, u32[]{:S(2)}) async-start(f32[8,56,128]{2,1,0:T(8,128)} %broadcast_in_dim.11), calls=%async_computation.3 | async-start | bytes 458752 | tf_op jit(solution)/shard_map/all_to_all | solution.py:413
  89.4 3.2 %mirror.4 = f32[8,56,128]{2,1,0:T(8,128)} custom-call(s32[4]{0:T(128)S(1)} %pad_add_fusion.me_ref, s32[8,128]{1,0:T(8,128)S(1)} %get-tuple-element.32.pos_a_ref, s32[8,128]{1,0:T(8,128)S(1)} %get-tuple-element.33.pos_b_ref, f32[4,56,128]{2,1,0:T(8,128)S(1)} %subtract_multiply_fusion.rows_ref.previous_ref, ...), custom_call_target="tpu_custom_call" | custom-call | flops 200000000 | bytes 4000000 | tf_op jit(solution)/shard_map/mirror/pallas_call | solution.py:310
  92.5 2.8 %all-to-all-done.3.cols_ref = f32[8,56,128]{2,1,0:T(8,128)S(1)} async-done(((f32[8,56,128]{2,1,0:T(8,128)}), f32[8,56,128]{2,1,0:T(8,128)S(1)}, u32[]{:S(2)}, u32[]{:S(2)}) %all-to-all-start.3) | async-done | bytes 229408 | tf_op jit(solution)/shard_map/all_to_all | solution.py:413
  95.3 3.4 %all-to-all-start.4 = ((f32[8,56,128]{2,1,0:T(8,128)}), f32[8,56,128]{2,1,0:T(8,128)S(1)}, u32[]{:S(2)}, u32[]{:S(2)}) async-start(f32[8,56,128]{2,1,0:T(8,128)} %mirror.4), calls=%async_computation.4 | async-start | bytes 458752 | tf_op jit(solution)/shard_map/all_to_all | solution.py:413
  98.7 3.5 %direct.4.rows_ref = f32[4,56,128]{2,1,0:T(8,128)S(1)} custom-call(s32[4]{0:T(128)S(1)} %pad_add_fusion.me_ref, s32[8,128]{1,0:T(8,128)S(1)} %get-tuple-element.32.pos_a_ref, s32[8,128]{1,0:T(8,128)S(1)} %get-tuple-element.33.pos_b_ref, f32[8,56,128]{2,1,0:T(8,128)S(1)} %all-to-all-done.3.cols_ref, bf16[88,56,128]{2,1,0:T(8,128)(2,1)S(1)} %get-tuple-element.35.blocks_a_ref, ...), custom_call_target="tpu_custom_call" | custom-call | flops 200000000 | bytes 4000000 | tf_op jit(solution)/shard_map/direct/pallas_call | solution.py:310
  102.2 2.4 %all-to-all-done.4.cols_ref = f32[8,56,128]{2,1,0:T(8,128)S(1)} async-done(((f32[8,56,128]{2,1,0:T(8,128)}), f32[8,56,128]{2,1,0:T(8,128)S(1)}, u32[]{:S(2)}, u32[]{:S(2)}) %all-to-all-start.4) | async-done | bytes 229408 | tf_op jit(solution)/shard_map/all_to_all | solution.py:413
  105.2 14.1 %all_to_all.51 = f32[4,4,56,128]{3,2,1,0:T(8,128)S(1)} all-to-all(f32[4,4,56,128]{3,2,1,0:T(8,128)S(1)} %merge.3), channel_id=1, replica_groups=mesh['x'=4,'zl'=2,'core'=2,'zh'=4,'y'=8] {'zh'}, dimensions={0} | all-to-all | bytes 917504 | tf_op jit(solution)/shard_map/all_to_all | solution.py:413
  120.1 4.5 %all-to-all-start.6 = ((f32[8,56,128]{2,1,0:T(8,128)}), f32[8,56,128]{2,1,0:T(8,128)S(1)}, u32[]{:S(2)}, u32[]{:S(2)}) async-start(f32[8,56,128]{2,1,0:T(8,128)} %broadcast_in_dim.25), calls=%async_computation.6 | async-start | bytes 458752 | tf_op jit(solution)/shard_map/all_to_all | solution.py:413
  124.6 3.2 %mirror.5 = f32[8,56,128]{2,1,0:T(8,128)} custom-call(s32[4]{0:T(128)S(1)} %pad_add_fusion.me_ref, s32[8,128]{1,0:T(8,128)S(1)} %get-tuple-element.32.pos_a_ref, s32[8,128]{1,0:T(8,128)S(1)} %get-tuple-element.33.pos_b_ref, f32[4,56,128]{2,1,0:T(8,128)S(1)} %multiply_subtract_fusion.rows_ref.current_ref, ...), custom_call_target="tpu_custom_call" | custom-call | flops 200000000 | bytes 4000000 | tf_op jit(solution)/shard_map/mirror/pallas_call | solution.py:310
  127.8 2.8 %all-to-all-done.6.cols_ref = f32[8,56,128]{2,1,0:T(8,128)S(1)} async-done(((f32[8,56,128]{2,1,0:T(8,128)}), f32[8,56,128]{2,1,0:T(8,128)S(1)}, u32[]{:S(2)}, u32[]{:S(2)}) %all-to-all-start.6) | async-done | bytes 229408 | tf_op jit(solution)/shard_map/all_to_all | solution.py:413
  130.6 3.4 %all-to-all-start.7 = ((f32[8,56,128]{2,1,0:T(8,128)}), f32[8,56,128]{2,1,0:T(8,128)S(1)}, u32[]{:S(2)}, u32[]{:S(2)}) async-start(f32[8,56,128]{2,1,0:T(8,128)} %mirror.5), calls=%async_computation.7 | async-start | bytes 458752 | tf_op jit(solution)/shard_map/all_to_all | solution.py:413
  134.0 3.5 %direct.5.rows_ref = f32[4,56,128]{2,1,0:T(8,128)S(1)} custom-call(s32[4]{0:T(128)S(1)} %pad_add_fusion.me_ref, s32[8,128]{1,0:T(8,128)S(1)} %get-tuple-element.32.pos_a_ref, s32[8,128]{1,0:T(8,128)S(1)} %get-tuple-element.33.pos_b_ref, f32[8,56,128]{2,1,0:T(8,128)S(1)} %all-to-all-done.6.cols_ref, bf16[88,56,128]{2,1,0:T(8,128)(2,1)S(1)} %get-tuple-element.35.blocks_a_ref, ...), custom_call_target="tpu_custom_call" | custom-call | flops 200000000 | bytes 4000000 | tf_op jit(solution)/shard_map/direct/pallas_call | solution.py:310
  137.4 2.4 %all-to-all-done.7 = f32[8,56,128]{2,1,0:T(8,128)S(1)} async-done(((f32[8,56,128]{2,1,0:T(8,128)}), f32[8,56,128]{2,1,0:T(8,128)S(1)}, u32[]{:S(2)}, u32[]{:S(2)}) %all-to-all-start.7) | async-done | bytes 229408 | tf_op jit(solution)/shard_map/all_to_all | solution.py:413
  140.9 19.4 %all_to_all.52 = f32[8,56,128]{2,1,0:T(8,128)S(1)} all-to-all(f32[8,56,128]{2,1,0:T(8,128)S(1)} %finish.1), channel_id=1, replica_groups=mesh['x'=4,'zl'=2,'core'=2,'zh'=4,'y'=8] {'core','zh'}, dimensions={0} | all-to-all | bytes 458752 | tf_op jit(solution)/shard_map/all_to_all | solution.py:413
  160.4 29.3 %all_to_all.53 = f32[32,56,128]{2,1,0:T(8,128)S(1)} all-to-all(f32[32,56,128]{2,1,0:T(8,128)S(1)} %broadcast_in_dim.26), channel_id=1, replica_groups=mesh['x'=4,'zl'=2,'core'=2,'zh'=4,'y'=8] {'y','zh'}, dimensions={0} | all-to-all | bytes 1835008 | tf_op jit(solution)/shard_map/all_to_all | solution.py:413
  (28 shorter events, 15.4 us)
Async XLA Ops:
  2.2 7.9 %copy-start = (f32[1792,128]{1,0:T(8,128)S(1)}, f32[1792,128]{1,0:T(8,128)}, u32[]{:S(2)}) copy-start(f32[1792,128]{1,0:T(8,128)} %param.4) | copy-start | bytes 2752516
  2.2 37.3 %all-to-all-start = ((f32[8,56,640]{2,1,0:T(8,128)}), f32[8,56,640]{2,1,0:T(8,128)S(1)}, u32[]{:S(2)}, u32[]{:S(2)}) async-start(f32[8,56,640]{2,1,0:T(8,128)} %pack.1), calls=%async_computation | async-start | bytes 2293760 | tf_op jit(solution)/shard_map/all_to_all | solution.py:413
  11.3 25.9 %collective-permute-start = (f32[2,56,128]{2,1,0:T(8,128)S(1)}, f32[2,56,128]{2,1,0:T(8,128)S(1)}, u32[]{:S(2)}, u32[]{:S(2)}) collective-permute-start(f32[2,56,128]{2,1,0:T(8,128)S(1)} %get-tuple-element.29), channel_id=1, source_target_pairs={{0,32},{32,0},{1,33},{33,1},{2,34},{34,2},{3,35},{35,3},{4,36},{36... | collective-permute-start | bytes 172040 | tf_op jit(solution)/shard_map/ppermute | solution.py:431
  39.5 6.6 %collective-permute-start.1 = (f32[8,56,640]{2,1,0:T(8,128)S(1)}, f32[8,56,640]{2,1,0:T(8,128)S(1)}, u32[]{:S(2)}, u32[]{:S(2)}) collective-permute-start(f32[8,56,640]{2,1,0:T(8,128)S(1)} %all-to-all-done.in_ref), channel_id=1, source_target_pairs={{0,32},{32,0},{1,33},{33,1},{2,34},{34,2},{3,35},{35,3},{4,36},{36... | collective-permute-start | bytes 3440648 | tf_op jit(solution)/shard_map/ppermute | solution.py:437
  50.3 12.2 %all-to-all-start.1 = ((f32[8,56,128]{2,1,0:T(8,128)}), f32[8,56,128]{2,1,0:T(8,128)S(1)}, u32[]{:S(2)}, u32[]{:S(2)}) async-start(f32[8,56,128]{2,1,0:T(8,128)} %mirror.3), calls=%async_computation.1 | async-start | bytes 458752 | tf_op jit(solution)/shard_map/all_to_all | solution.py:413
  85.1 10.2 %all-to-all-start.3 = ((f32[8,56,128]{2,1,0:T(8,128)}), f32[8,56,128]{2,1,0:T(8,128)S(1)}, u32[]{:S(2)}, u32[]{:S(2)}) async-start(f32[8,56,128]{2,1,0:T(8,128)} %broadcast_in_dim.11), calls=%async_computation.3 | async-start | bytes 458752 | tf_op jit(solution)/shard_map/all_to_all | solution.py:413
  95.3 9.3 %all-to-all-start.4 = ((f32[8,56,128]{2,1,0:T(8,128)}), f32[8,56,128]{2,1,0:T(8,128)S(1)}, u32[]{:S(2)}, u32[]{:S(2)}) async-start(f32[8,56,128]{2,1,0:T(8,128)} %mirror.4), calls=%async_computation.4 | async-start | bytes 458752 | tf_op jit(solution)/shard_map/all_to_all | solution.py:413
  120.1 10.4 %all-to-all-start.6 = ((f32[8,56,128]{2,1,0:T(8,128)}), f32[8,56,128]{2,1,0:T(8,128)S(1)}, u32[]{:S(2)}, u32[]{:S(2)}) async-start(f32[8,56,128]{2,1,0:T(8,128)} %broadcast_in_dim.25), calls=%async_computation.6 | async-start | bytes 458752 | tf_op jit(solution)/shard_map/all_to_all | solution.py:413
  130.6 9.3 %all-to-all-start.7 = ((f32[8,56,128]{2,1,0:T(8,128)}), f32[8,56,128]{2,1,0:T(8,128)S(1)}, u32[]{:S(2)}, u32[]{:S(2)}) async-start(f32[8,56,128]{2,1,0:T(8,128)} %mirror.5), calls=%async_computation.7 | async-start | bytes 458752 | tf_op jit(solution)/shard_map/all_to_all | solution.py:413
